TPU v7x, 32 devices: a whole 2x2x4 slice. The times are simulated.
32 devices in a mesh: pipe: 2 (over core), dp: 4 (over y, x), seq: 4 (over z).
Axes of the slice: x: 2, y: 2, z: 4, core: 2. Of those that a mesh axis runs over, the one named last changes fastest.
Arguments:
- inputs: bfloat16 [8, 4096, 768], P('dp', 'seq'), may hold values from -6 to 6
- cotangent: bfloat16 [8, 4096, 768], P('dp', 'seq'), may hold values from -6 to 6
- in_weight: bfloat16 [2, 768, 3072], P('pipe'), may hold values from -0.21875 to 0.21875
- in_bias: float32 [2, 3072], P('pipe'), may hold values from -1.5 to 1.5
- out_weight: bfloat16 [2, 3072, 768], P('pipe'), may hold values from -0.109375 to 0.109375
- out_bias: float32 [2, 768], P('pipe'), may hold values from -1.5 to 1.5
- mix_gain: float32 [2, 768], P('pipe'), may hold values from 0.25 to 1.75
- mix_shift: float32 [2, 768], P('pipe'), may hold values from -1.5 to 1.5
- out_gain: float32 [2, 768], P('pipe'), may hold values from 0.25 to 1.75
- out_shift: float32 [2, 768], P('pipe'), may hold values from -1.5 to 1.5
Outputs:
- output: bfloat16 [8, 4096, 768], P('dp', 'seq', 'pipe')
- input_grad: bfloat16 [8, 4096, 768], P('dp', 'seq', 'pipe')
- in_weight_grad: float32 [2, 768, 3072], P('pipe')
- in_bias_grad: float32 [2, 3072], P('pipe')
- out_weight_grad: float32 [2, 3072, 768], P('pipe')
- out_bias_grad: float32 [2, 768], P('pipe')
- mix_gain_grad: float32 [2, 768], P('pipe')
- mix_shift_grad: float32 [2, 768], P('pipe')
- out_gain_grad: float32 [2, 768], P('pipe')
- out_shift_grad: float32 [2, 768], P('pipe')
All inputs are finite; a program needn't handle non-finite values.
Results may differ from a plain program's by a relative error of at most 0.014.
Values may be sent and summed in bfloat16 or wider, within the bound.
No kernel may reach another device: no remote copies, remote signals or barrier semaphores. Data moves between devices by JAX's collectives and lax.ppermute only.
A program may use at most 448 MiB of HBM per device.

v0:
```python
import math

import jax
import jax.numpy as jnp
from jax import lax
from jax.sharding import PartitionSpec as P


def from_behind(array, axis, by):
    peers = lax.axis_size(axis)
    pairs = [(i, i + by) for i in range(peers) if 0 <= i + by < peers]
    return lax.ppermute(array, axis, pairs)


def shifted(value, axis, steps):
    count = lax.axis_size(axis)
    pairs = [(source, (source + steps) % count) for source in range(count)]
    return lax.ppermute(value, axis, pairs)


def phase_table(row_start, row_count, col_count, length):
    row_ids = row_start + lax.broadcasted_iota(jnp.int32, (row_count, col_count), 0)
    col_ids = lax.broadcasted_iota(jnp.int32, (row_count, col_count), 1)
    angles = (row_ids * col_ids % length).astype(jnp.float32) * (2.0 * math.pi / length)
    return (jnp.cos(angles).astype(jnp.bfloat16), jnp.sin(angles).astype(jnp.bfloat16))


def table_rows(row_start, row_count, length):
    row_block = math.gcd(row_count, 512)
    offsets = jnp.arange(row_count // row_block, dtype=jnp.int32) * row_block

    def one_block(offset):
        return phase_table(row_start + offset, row_block, length, length)

    cos_blocks, sin_blocks = lax.map(one_block, offsets)
    return (cos_blocks.reshape(row_count, length), sin_blocks.reshape(row_count, length))


def normalize(hidden, gain, shift):
    centered = hidden - jnp.mean(hidden, axis=-1, keepdims=True)
    spread = jnp.mean(centered * centered, axis=-1, keepdims=True)
    return centered * lax.rsqrt(spread + 1e-05) * gain + shift


def product(left, right):
    return jnp.dot(left, right, preferred_element_type=jnp.float32)


def mixing(layer_in, hidden_table, tables):
    tok_rows, features = layer_in.shape
    length = tok_rows * lax.axis_size("seq")
    cos_rows, sin_rows = tables
    spectra = product(layer_in, hidden_table) * (1.0 / math.sqrt(features))
    spectra = spectra.astype(jnp.bfloat16).reshape(tok_rows, 2, features)
    factor = 1.0 / math.sqrt(length)
    columns = lax.all_to_all(spectra, "seq", split_axis=2, concat_axis=0, tiled=True)
    mixture = product(cos_rows, columns[:, 0, :]) + product(sin_rows, columns[:, 1, :])
    mixture = (mixture * factor).astype(jnp.bfloat16)
    return lax.all_to_all(mixture, "seq", split_axis=0, concat_axis=1, tiled=True)


def spectral_back(grad_mix, tables):
    tok_rows, features = grad_mix.shape
    length = tok_rows * lax.axis_size("seq")
    factor = 1.0 / math.sqrt(length)
    cos_rows, sin_rows = tables
    columns = lax.all_to_all(grad_mix, "seq", split_axis=1, concat_axis=0, tiled=True)
    paired = jnp.stack([product(cos_rows, columns), product(sin_rows, columns)], axis=1)
    paired = (paired * factor).astype(jnp.bfloat16)
    return lax.all_to_all(paired, "seq", split_axis=0, concat_axis=2, tiled=True)


def local_forward(layer_in, mixture, params):
    hidden = layer_in.astype(jnp.float32) + mixture.astype(jnp.float32)
    normed = normalize(hidden, params[4], params[5])
    pre_act = product(normed.astype(jnp.bfloat16), params[0]) + params[1]
    activation = jax.nn.gelu(pre_act, approximate=False).astype(jnp.bfloat16)
    branch = product(activation, params[2]) + params[3]
    return normalize(normed + branch, params[6], params[7]).astype(jnp.bfloat16)


def local_backward(layer_in, mixture, grad_out, params, hidden_table, tables):
    features = layer_in.shape[1]
    contract_rows = (((0,), (0,)), ((), ()))
    contract_cols = (((1,), (1,)), ((), ()))
    hidden = layer_in.astype(jnp.float32) + mixture.astype(jnp.float32)
    normed, first_pull = jax.vjp(normalize, hidden, params[4], params[5])
    normed_low = normed.astype(jnp.bfloat16)
    pre_act = product(normed_low, params[0]) + params[1]
    activation_f, gelu_pull = jax.vjp(lambda value: jax.nn.gelu(value, approximate=False), pre_act)
    activation = activation_f.astype(jnp.bfloat16)
    branch = product(activation, params[2]) + params[3]
    second_pull = jax.vjp(
        lambda upper, lower, gain, shift: normalize(upper + lower, gain, shift),
        normed,
        branch,
        params[6],
        params[7],
    )[1]
    grad_normed_a, grad_branch, grad_out_gain, grad_out_shift = second_pull(
        grad_out.astype(jnp.float32)
    )
    branch_low = grad_branch.astype(jnp.bfloat16)
    grad_out_bias = jnp.sum(branch_low.astype(jnp.float32), axis=0)
    grad_out_weight = lax.dot_general(
        activation, branch_low, contract_rows, preferred_element_type=jnp.float32
    )
    grad_act = lax.dot_general(
        branch_low, params[2], contract_cols, preferred_element_type=jnp.float32
    )
    pre_low = gelu_pull(grad_act)[0].astype(jnp.bfloat16)
    grad_in_bias = jnp.sum(pre_low.astype(jnp.float32), axis=0)
    grad_in_weight = lax.dot_general(
        normed_low, pre_low, contract_rows, preferred_element_type=jnp.float32
    )
    grad_normed = grad_normed_a + lax.dot_general(
        pre_low, params[0], contract_cols, preferred_element_type=jnp.float32
    )
    grad_hidden, grad_mix_gain, grad_mix_shift = first_pull(grad_normed)
    grad_spec = spectral_back(grad_hidden.astype(jnp.bfloat16), tables)
    grad_spec = grad_spec.reshape(grad_spec.shape[0], 2 * features)
    grad_in = grad_hidden + lax.dot_general(
        grad_spec, hidden_table, contract_cols, preferred_element_type=jnp.float32
    ) * (1.0 / math.sqrt(features))
    weight_terms = (
        grad_in_weight,
        grad_in_bias,
        grad_out_weight,
        grad_out_bias,
        grad_mix_gain,
        grad_mix_shift,
        grad_out_gain,
        grad_out_shift,
    )
    return (grad_in.astype(jnp.bfloat16), weight_terms)


def on_device(
    inputs,
    cotangent,
    in_weight,
    in_bias,
    out_weight,
    out_bias,
    mix_gain,
    mix_shift,
    out_gain,
    out_shift,
):
    micro_count, tok_rows, features = inputs.shape
    length = tok_rows * lax.axis_size("seq")
    section_index = lax.axis_index("pipe")
    is_first = section_index == 0
    params = (
        in_weight[0],
        in_bias[0],
        out_weight[0],
        out_bias[0],
        mix_gain[0],
        mix_shift[0],
        out_gain[0],
        out_shift[0],
    )
    hidden_cos, hidden_sin = phase_table(0, features, features, features)
    hidden_table = jnp.concatenate([hidden_cos, -hidden_sin], axis=1)
    tables = table_rows(0, length, length)
    blank = jnp.zeros((tok_rows, features), jnp.bfloat16)
    received = blank
    stored = []
    outputs = []
    for tick_index in range(micro_count + 1):
        incoming = inputs[tick_index] if tick_index < micro_count else blank
        layer_in = jnp.where(is_first, incoming, received)
        mixture = mixing(layer_in, hidden_table, tables)
        layer_out = local_forward(layer_in, mixture, params)
        stored.append((layer_in, mixture))
        outputs.append(layer_out)
        if tick_index < micro_count:
            received = from_behind(layer_out, "pipe", 1)
    received = blank
    totals = tuple((jnp.zeros_like(weight, jnp.float32) for weight in params))
    input_grads = [blank] * micro_count
    for back_step in range(micro_count + 1):
        layer_in, mixture = stored[micro_count - back_step]
        if back_step > 0:
            mixture = mixing(layer_in, hidden_table, tables)
        slot_index = micro_count - 1 - back_step
        incoming = cotangent[slot_index] if slot_index >= 0 else blank
        grad_out = jnp.where(is_first, received, incoming)
        grad_in, weight_terms = local_backward(
            layer_in, mixture, grad_out, params, hidden_table, tables
        )
        totals = tuple((total + term for total, term in zip(totals, weight_terms)))
        if back_step > 0:
            input_grads[micro_count - back_step] = grad_in
        if back_step < micro_count:
            received = from_behind(grad_in, "pipe", -1)
    summed = lax.psum(totals, ("dp", "seq"))
    half_width = features // 2
    final = jnp.stack(outputs[1 : micro_count + 1], axis=0)
    grads_all = jnp.stack(input_grads, axis=0)
    sent_out, sent_grad = shifted(
        (final[:, :, :half_width], grads_all[:, :, half_width:]), "pipe", 1
    )
    output_half = jnp.where(is_first, sent_out, final[:, :, half_width:])
    grad_half = jnp.where(is_first, grads_all[:, :, :half_width], sent_grad)
    return (
        output_half,
        grad_half,
        summed[0][None],
        summed[1][None],
        summed[2][None],
        summed[3][None],
        summed[4][None],
        summed[5][None],
        summed[6][None],
        summed[7][None],
    )


def solution(mesh):
    return jax.shard_map(
        on_device,
        mesh=mesh,
        in_specs=(
            P("dp", "seq", None),
            P("dp", "seq", None),
            P("pipe", None, None),
            P("pipe", None),
            P("pipe", None, None),
            P("pipe", None),
            P("pipe", None),
            P("pipe", None),
            P("pipe", None),
            P("pipe", None),
        ),
        out_specs=(
            P("dp", "seq", "pipe"),
            P("dp", "seq", "pipe"),
            P("pipe", None, None),
            P("pipe", None),
            P("pipe", None, None),
            P("pipe", None),
            P("pipe", None),
            P("pipe", None),
            P("pipe", None),
            P("pipe", None),
        ),
        check_vma=False,
    )
```

profile of v0, /device:TPU:0, one launch (start us, length us, event | category | flops | bytes accessed | tf_op | source)
XLA Modules:
  0.0 2127.8 jit_solution(2626890093634932832)
XLA Ops:
  44.1 11.2 copy.87
  61.9 303.9 %while.14 = (s32[]{:T(128)}, bf16[8,512,4096]{2,1,0:T(8,128)(2,1)}, bf16[8,512,4096]{2,1,0:T(8,128)(2,1)}, s32[8]{0:T(128)S(1)}, s32[]{:T(128)}) while((s32[]{:T(128)}, bf16[8,512,4096]{2,1,0:T(8,128)(2,1)}, bf16[8,512,4096]{2,1,0:T(8,128)(2,1)}, s32[8]{0:T(128)S(1)}, s32[]{:T(128)}) %tuple.79), condition=%wide.region_1.2_spmd, body=%wide.region_0.1_spmd.sunk | while | flops 33554944 | bytes 8392793 | solution.py:35
  63.1 36.8 %fusion.189 = (bf16[8,512,4096]{2,1,0:T(8,128)(2,1)}, bf16[8,512,4096]{2,1,0:T(8,128)(2,1)}) fusion(bf16[8,512,4096]{2,1,0:T(8,128)(2,1)} %get-tuple-element.233, s32[]{:T(128)S(6)} %copy.148, s32[512]{0:T(512)S(1)} %iota_add_fusion.2, bf16[8,512,4096]{2,1,0:T(8,128)(2,1)} %get-tuple-element.232), kind=kLoop, calls=%fused_computation.12.clone.1 | loop fusion | flops 33554432 | bytes 8390660 | tf_op jit(solution)/shard_map/while/body/jit(dynamic_update_index_in_dim)/dynamic_update_slice | solution.py:35
  101.1 36.7 %fusion.189 = (bf16[8,512,4096]{2,1,0:T(8,128)(2,1)}, bf16[8,512,4096]{2,1,0:T(8,128)(2,1)}) fusion(bf16[8,512,4096]{2,1,0:T(8,128)(2,1)} %get-tuple-element.233, s32[]{:T(128)S(6)} %copy.148, s32[512]{0:T(512)S(1)} %iota_add_fusion.2, bf16[8,512,4096]{2,1,0:T(8,128)(2,1)} %get-tuple-element.232), kind=kLoop, calls=%fused_computation.12.clone.1 | loop fusion | flops 33554432 | bytes 8390660 | tf_op jit(solution)/shard_map/while/body/jit(dynamic_update_index_in_dim)/dynamic_update_slice | solution.py:35
  139.1 36.7 %fusion.189 = (bf16[8,512,4096]{2,1,0:T(8,128)(2,1)}, bf16[8,512,4096]{2,1,0:T(8,128)(2,1)}) fusion(bf16[8,512,4096]{2,1,0:T(8,128)(2,1)} %get-tuple-element.233, s32[]{:T(128)S(6)} %copy.148, s32[512]{0:T(512)S(1)} %iota_add_fusion.2, bf16[8,512,4096]{2,1,0:T(8,128)(2,1)} %get-tuple-element.232), kind=kLoop, calls=%fused_computation.12.clone.1 | loop fusion | flops 33554432 | bytes 8390660 | tf_op jit(solution)/shard_map/while/body/jit(dynamic_update_index_in_dim)/dynamic_update_slice | solution.py:35
  177.0 36.7 %fusion.189 = (bf16[8,512,4096]{2,1,0:T(8,128)(2,1)}, bf16[8,512,4096]{2,1,0:T(8,128)(2,1)}) fusion(bf16[8,512,4096]{2,1,0:T(8,128)(2,1)} %get-tuple-element.233, s32[]{:T(128)S(6)} %copy.148, s32[512]{0:T(512)S(1)} %iota_add_fusion.2, bf16[8,512,4096]{2,1,0:T(8,128)(2,1)} %get-tuple-element.232), kind=kLoop, calls=%fused_computation.12.clone.1 | loop fusion | flops 33554432 | bytes 8390660 | tf_op jit(solution)/shard_map/while/body/jit(dynamic_update_index_in_dim)/dynamic_update_slice | solution.py:35
  215.0 36.8 %fusion.189 = (bf16[8,512,4096]{2,1,0:T(8,128)(2,1)}, bf16[8,512,4096]{2,1,0:T(8,128)(2,1)}) fusion(bf16[8,512,4096]{2,1,0:T(8,128)(2,1)} %get-tuple-element.233, s32[]{:T(128)S(6)} %copy.148, s32[512]{0:T(512)S(1)} %iota_add_fusion.2, bf16[8,512,4096]{2,1,0:T(8,128)(2,1)} %get-tuple-element.232), kind=kLoop, calls=%fused_computation.12.clone.1 | loop fusion | flops 33554432 | bytes 8390660 | tf_op jit(solution)/shard_map/while/body/jit(dynamic_update_index_in_dim)/dynamic_update_slice | solution.py:35
  253.0 36.7 %fusion.189 = (bf16[8,512,4096]{2,1,0:T(8,128)(2,1)}, bf16[8,512,4096]{2,1,0:T(8,128)(2,1)}) fusion(bf16[8,512,4096]{2,1,0:T(8,128)(2,1)} %get-tuple-element.233, s32[]{:T(128)S(6)} %copy.148, s32[512]{0:T(512)S(1)} %iota_add_fusion.2, bf16[8,512,4096]{2,1,0:T(8,128)(2,1)} %get-tuple-element.232), kind=kLoop, calls=%fused_computation.12.clone.1 | loop fusion | flops 33554432 | bytes 8390660 | tf_op jit(solution)/shard_map/while/body/jit(dynamic_update_index_in_dim)/dynamic_update_slice | solution.py:35
  291.0 36.7 %fusion.189 = (bf16[8,512,4096]{2,1,0:T(8,128)(2,1)}, bf16[8,512,4096]{2,1,0:T(8,128)(2,1)}) fusion(bf16[8,512,4096]{2,1,0:T(8,128)(2,1)} %get-tuple-element.233, s32[]{:T(128)S(6)} %copy.148, s32[512]{0:T(512)S(1)} %iota_add_fusion.2, bf16[8,512,4096]{2,1,0:T(8,128)(2,1)} %get-tuple-element.232), kind=kLoop, calls=%fused_computation.12.clone.1 | loop fusion | flops 33554432 | bytes 8390660 | tf_op jit(solution)/shard_map/while/body/jit(dynamic_update_index_in_dim)/dynamic_update_slice | solution.py:35
  329.0 36.7 %fusion.189 = (bf16[8,512,4096]{2,1,0:T(8,128)(2,1)}, bf16[8,512,4096]{2,1,0:T(8,128)(2,1)}) fusion(bf16[8,512,4096]{2,1,0:T(8,128)(2,1)} %get-tuple-element.233, s32[]{:T(128)S(6)} %copy.148, s32[512]{0:T(512)S(1)} %iota_add_fusion.2, bf16[8,512,4096]{2,1,0:T(8,128)(2,1)} %get-tuple-element.232), kind=kLoop, calls=%fused_computation.12.clone.1 | loop fusion | flops 33554432 | bytes 8390660 | tf_op jit(solution)/shard_map/while/body/jit(dynamic_update_index_in_dim)/dynamic_update_slice | solution.py:35
  368.9 18.8 fusion.104
  387.7 18.4 fusion.32
  414.2 35.2 %all-to-all-done.1 = bf16[4,1024,192]{1,2,0:T(8,128)(2,1)S(1)} async-done(((bf16[4,1024,192]{1,2,0:T(8,128)(2,1)}), bf16[4,1024,192]{1,2,0:T(8,128)(2,1)S(1)}, u32[]{:S(2)}, u32[]{:S(2)}) %all-to-all-start.1) | async-done | bytes 1572896 | tf_op jit(solution)/shard_map/all_to_all | solution.py:59
  453.5 36.8 %multiply_convert_fusion.2 = (bf16[1024,3072]{1,0:T(8,128)(2,1)}, f32[1024,3072]{1,0:T(8,128)}, f32[1024,3072]{1,0:T(8,128)}) fusion(f32[3072]{0:T(1024)S(1)} %bitcast.325, bf16[1024,768]{0,1:T(8,128)(2,1)S(1)} %fusion.97, bf16[1,768,3072]{2,1,0:T(8,128)(2,1)S(1)} %bitcast.324), kind=kOutput, calls=%fused_computation.52 | convolution fusion | flops 5039456256 | bytes 37761024 | tf_op jit(solution)/shard_map/dot_general | solution.py:46
  525.0 75.9 %all_to_all.215 = bf16[1024,2,768]{0,1,2:T(2,128)(2,1)S(1)} all-to-all(bf16[1024,2,768]{0,1,2:T(2,128)(2,1)} %copy.91), channel_id=1, replica_groups=mesh['pipe'=2,'dp'=4,'seq'=4] {'seq'}, dimensions={2} | all-to-all | bytes 6291456 | tf_op jit(solution)/shard_map/all_to_all | solution.py:56
  602.1 17.1 fusion.103
  619.2 17.5 fusion.33
  636.9 40.0 %all_to_all.216 = bf16[4,1024,192]{1,2,0:T(8,128)(2,1)S(1)} all-to-all(bf16[4,1024,192]{1,2,0:T(8,128)(2,1)S(1)} %bitcast.277), channel_id=1, replica_groups=mesh['pipe'=2,'dp'=4,'seq'=4] {'seq'}, dimensions={0} | all-to-all | bytes 3145728 | tf_op jit(solution)/shard_map/all_to_all | solution.py:59
  678.4 38.7 %multiply_convert_fusion.1 = (bf16[1024,3072]{1,0:T(8,128)(2,1)S(1)}, f32[1024,3072]{1,0:T(8,128)}, f32[1024,3072]{1,0:T(8,128)}) fusion(f32[3072]{0:T(1024)S(1)} %bitcast.326, bf16[1,768,3072]{2,1,0:T(8,128)(2,1)} %param.14, f32[1024,768]{0,1:T(8,128)S(1)} %get-tuple-element.163, f32[1024]{0:T(1024)S(1)} %fusion.116, ...), kind=kOutput, calls=%fused_computation.39 | convolution fusion | flops 5043388416 | bytes 39348224 | tf_op jit(solution)/shard_map/dot_general | solution.py:46
  749.5 75.3 %all_to_all.217 = bf16[1024,2,768]{0,1,2:T(2,128)(2,1)S(1)} all-to-all(bf16[1024,2,768]{0,1,2:T(2,128)(2,1)} %copy.95), channel_id=1, replica_groups=mesh['pipe'=2,'dp'=4,'seq'=4] {'seq'}, dimensions={2} | all-to-all | bytes 6291456 | tf_op jit(solution)/shard_map/all_to_all | solution.py:56
  826.1 17.1 fusion.102
  843.2 17.5 fusion.34
  871.0 31.2 %all-to-all-done.5 = bf16[4,1024,192]{1,2,0:T(8,128)(2,1)S(1)} async-done(((bf16[4,1024,192]{1,2,0:T(8,128)(2,1)}), bf16[4,1024,192]{1,2,0:T(8,128)(2,1)S(1)}, u32[]{:S(2)}, u32[]{:S(2)}) %all-to-all-start.5) | async-done | bytes 1572896 | tf_op jit(solution)/shard_map/all_to_all | solution.py:59
  903.3 39.2 %multiply_convert_fusion = (bf16[1024,3072]{1,0:T(8,128)(2,1)S(1)}, f32[1024,3072]{1,0:T(8,128)}, f32[1024,3072]{1,0:T(8,128)}) fusion(f32[3072]{0:T(1024)S(1)} %bitcast.327, bf16[1,768,3072]{2,1,0:T(8,128)(2,1)} %param.14, f32[1024,768]{0,1:T(8,128)S(1)} %get-tuple-element.159, f32[1024]{0:T(1024)S(1)} %fusion.118, f32[1024]{0:T(1024)S(1)} %broadcast_multiply_fusion.1, ...), kind=kOutput, calls=%fused_computation.26 | convolution fusion | flops 5043388416 | bytes 39348224 | tf_op jit(solution)/shard_map/dot_general | solution.py:46
  954.9 18.1 convert_reduce_fusion.2
  973.0 11.5 multiply_reduce_fusion.2
  985.8 40.2 %all_to_all.218 = bf16[1024,4,192]{0,2,1:T(8,128)(2,1)S(1)} all-to-all(bf16[1024,4,192]{0,2,1:T(8,128)(2,1)S(1)} %bitcast.281), channel_id=1, replica_groups=mesh['pipe'=2,'dp'=4,'seq'=4] {'seq'}, dimensions={1} | all-to-all | bytes 3145728 | tf_op jit(solution)/shard_map/all_to_all | solution.py:67
  1026.2 17.1 convolution_bitcast_fusion.4
  1043.3 17.1 convolution_bitcast_fusion.5
  1068.2 98.4 %all_to_all.219 = bf16[4096,2,192]{2,1,0:T(2,128)(2,1)} all-to-all(bf16[4096,2,192]{2,1,0:T(2,128)(2,1)} %copy.101), channel_id=1, replica_groups=mesh['pipe'=2,'dp'=4,'seq'=4] {'seq'}, dimensions={0} | all-to-all | bytes 6291456 | tf_op jit(solution)/shard_map/all_to_all | solution.py:70
  1166.6 10.9 copy.121
  1198.5 19.2 convert_reduce_fusion.1
  1217.6 11.2 multiply_reduce_fusion.1
  1230.2 40.3 %all_to_all.220 = bf16[1024,4,192]{0,2,1:T(8,128)(2,1)S(1)} all-to-all(bf16[1024,4,192]{0,2,1:T(8,128)(2,1)S(1)} %bitcast.282), channel_id=1, replica_groups=mesh['pipe'=2,'dp'=4,'seq'=4] {'seq'}, dimensions={1} | all-to-all | bytes 3145728 | tf_op jit(solution)/shard_map/all_to_all | solution.py:67
  1270.6 17.1 convolution_bitcast_fusion.2
  1287.7 17.1 convolution_bitcast_fusion.3
  1347.1 63.7 %all-to-all-done.9 = bf16[4096,2,192]{2,1,0:T(2,128)(2,1)} async-done(((bf16[4096,2,192]{2,1,0:T(2,128)(2,1)}), bf16[4096,2,192]{2,1,0:T(2,128)(2,1)}, u32[]{:S(2)}, u32[]{:S(2)}) %all-to-all-start.9) | async-done | bytes 3145760 | tf_op jit(solution)/shard_map/all_to_all | solution.py:70
  1440.4 16.9 convert_reduce_fusion
  1457.3 16.8 add_bitcast_fusion
  1474.2 11.8 add_bitcast_fusion.1
  1486.0 11.1 multiply_reduce_fusion
  1498.3 79.4 %all_to_all.221 = bf16[1024,4,192]{0,2,1:T(8,128)(2,1)S(1)} all-to-all(bf16[1024,4,192]{0,2,1:T(8,128)(2,1)S(1)} %bitcast.283), channel_id=1, replica_groups=mesh['pipe'=2,'dp'=4,'seq'=4] {'seq'}, dimensions={1} | all-to-all | bytes 3145728 | tf_op jit(solution)/shard_map/all_to_all | solution.py:67
  1577.9 17.2 convolution_bitcast_fusion
  1595.0 17.6 convolution_bitcast_fusion.1
  1628.7 163.0 %all-to-all-done.11 = bf16[4096,2,192]{2,1,0:T(2,128)(2,1)} async-done(((bf16[4096,2,192]{2,1,0:T(2,128)(2,1)}), bf16[4096,2,192]{2,1,0:T(2,128)(2,1)}, u32[]{:S(2)}, u32[]{:S(2)}) %all-to-all-start.11) | async-done | bytes 3145760 | tf_op jit(solution)/shard_map/all_to_all | solution.py:70
  1791.8 11.0 copy.123
  1815.7 75.2 %all-reduce = (f32[1,3072]{1,0:T(1,128)}, f32[1,768]{1,0:T(1,128)}, f32[1,768]{1,0:T(1,128)}, f32[1,768]{1,0:T(1,128)}, f32[1,768]{1,0:T(1,128)}, /*index=5*/f32[1,768]{1,0:T(1,128)}) all-reduce(f32[1,3072]{1,0:T(1,128)S(1)} %bitcast.304, f32[1,768]{1,0:T(1,128)S(1)} %broadcast_in_dim.109, ...), channel_id=1, replica_groups=mesh['pipe'=2,'dp'=4,'seq'=4] {'dp','seq'}, use_global_device_ids=true, to_apply=%region_30.31 | all-reduce | flops 6912 | bytes 55296 | tf_op jit(solution)/shard_map/psum | solution.py:198
  1893.9 214.3 %all-reduce.4.cloned.1.call-done = (f32[1,768,3072]{2,1,0:T(8,128)}, f32[1,3072,768]{2,1,0:T(8,128)}) async-done(((f32[1,768,3072]{2,1,0:T(8,128)}, f32[1,3072,768]{2,1,0:T(8,128)}), (f32[1,768,3072]{2,1,0:T(8,128)}, f32[1,3072,768]{2,1,0:T(8,128)})) %all-reduce.4.cloned.1.call-update) | async-done | bytes 18874384 | tf_op jit(solution)/shard_map/psum | solution.py:198
  (390 shorter events, 312.1 us)
Async XLA Ops:
  55.3 310.4 %all-to-all-start = ((bf16[1024,2,768]{0,1,2:T(2,128)(2,1)}), bf16[1024,2,768]{0,1,2:T(2,128)(2,1)}, u32[]{:S(2)}, u32[]{:S(2)}) async-start(bf16[1024,2,768]{0,1,2:T(2,128)(2,1)} %copy.87), calls=%async_computation | async-start | bytes 6291456 | tf_op jit(solution)/shard_map/all_to_all | solution.py:56
  407.4 42.0 %all-to-all-start.1 = ((bf16[4,1024,192]{1,2,0:T(8,128)(2,1)}), bf16[4,1024,192]{1,2,0:T(8,128)(2,1)S(1)}, u32[]{:S(2)}, u32[]{:S(2)}) async-start(bf16[4,1024,192]{1,2,0:T(8,128)(2,1)} %bitcast.276), calls=%async_computation.1 | async-start | bytes 3145728 | tf_op jit(solution)/shard_map/all_to_all | solution.py:59
  414.1 528.4 %copy-start.77 = (f32[768]{0:T(1024)}, f32[768]{0:T(1024)S(1)}, u32[]{:S(2)}) copy-start(f32[768]{0:T(1024)S(1)} %reduce.2) | copy-start | bytes 9220
  450.1 40.3 %copy-start.10 = (f32[1024,768]{0,1:T(8,128)}, f32[1024,768]{0,1:T(8,128)S(1)}, u32[]{:S(2)}) copy-start(f32[1024,768]{0,1:T(8,128)S(1)} %get-tuple-element.167) | copy-start | bytes 9437188
  450.1 40.2 %copy-start.59 = (f32[1024]{0:T(1024)}, f32[1024]{0:T(1024)S(1)}, u32[]{:S(2)}) copy-start(f32[1024]{0:T(1024)S(1)} %broadcast_multiply_fusion.5) | copy-start | bytes 12292
  451.1 39.2 %copy-start.63 = (f32[1024]{0:T(1024)}, f32[1024]{0:T(1024)S(1)}, u32[]{:S(2)}) copy-start(f32[1024]{0:T(1024)S(1)} %fusion.114) | copy-start | bytes 12292
  451.5 38.8 %slice-start = ((s8[4718592]{0:T(1024)(128)(4,1)}), s8[4194304]{0:T(1024)(128)(4,1)S(1)}, s32[]{:S(2)}) async-start(s8[4718592]{0:T(1024)(128)(4,1)} %bitcast.317), calls=%async_computation.13 | async-start | bytes 8388608
  453.5 36.8 %slice-start.1 = ((s8[4718592]{0:T(1024)(128)(4,1)}), s8[524288]{0:T(1024)(128)(4,1)S(1)}, s32[]{:S(2)}) async-start(s8[4718592]{0:T(1024)(128)(4,1)} %bitcast.317), calls=%async_computation.14 | async-start | bytes 1048576
  500.5 4.6 collective-permute-start
  636.7 40.1 %copy-start.30 = (bf16[1,1024,768]{1,2,0:T(8,128)(2,1)S(1)}, bf16[1,1024,768]{1,2,0:T(8,128)(2,1)}, u32[]{:S(2)}) copy-start(bf16[1,1024,768]{1,2,0:T(8,128)(2,1)} %copy-done.29) | copy-start | bytes 4718596
  676.9 40.3 %slice-start.2 = ((s8[4718592]{0:T(1024)(128)(4,1)}), s8[4194304]{0:T(1024)(128)(4,1)S(1)}, s32[]{:S(2)}) async-start(s8[4718592]{0:T(1024)(128)(4,1)} %bitcast.319), calls=%async_computation.15 | async-start | bytes 8388608
  677.9 39.1 %copy-start.7 = (f32[1024,768]{0,1:T(8,128)}, f32[1024,768]{0,1:T(8,128)S(1)}, u32[]{:S(2)}) copy-start(f32[1024,768]{0,1:T(8,128)S(1)} %get-tuple-element.163) | copy-start | bytes 9437188
  677.9 39.1 %copy-start.65 = (f32[1024]{0:T(1024)}, f32[1024]{0:T(1024)S(1)}, u32[]{:S(2)}) copy-start(f32[1024]{0:T(1024)S(1)} %broadcast_multiply_fusion.3) | copy-start | bytes 12292
  678.3 38.7 %copy-start.71 = (f32[1024]{0:T(1024)}, f32[1024]{0:T(1024)S(1)}, u32[]{:S(2)}) copy-start(f32[1024]{0:T(1024)S(1)} %multiply_reduce_fusion.9) | copy-start | bytes 12292
  678.4 38.7 %copy-start.75 = (f32[1024]{0:T(1024)}, f32[1024]{0:T(1024)S(1)}, u32[]{:S(2)}) copy-start(f32[1024]{0:T(1024)S(1)} %fusion.116) | copy-start | bytes 12292
  678.4 38.7 %slice-start.3 = ((s8[4718592]{0:T(1024)(128)(4,1)}), s8[524288]{0:T(1024)(128)(4,1)S(1)}, s32[]{:S(2)}) async-start(s8[4718592]{0:T(1024)(128)(4,1)} %bitcast.319), calls=%async_computation.16 | async-start | bytes 1048576
  724.8 5.5 collective-permute-start.1
  861.9 40.2 %all-to-all-start.5 = ((bf16[4,1024,192]{1,2,0:T(8,128)(2,1)}), bf16[4,1024,192]{1,2,0:T(8,128)(2,1)S(1)}, u32[]{:S(2)}, u32[]{:S(2)}) async-start(bf16[4,1024,192]{1,2,0:T(8,128)(2,1)} %bitcast.262), calls=%async_computation.5 | async-start | bytes 3145728 | tf_op jit(solution)/shard_map/all_to_all | solution.py:59
  871.0 102.0 %copy-start.5 = (bf16[1,1024,768]{1,2,0:T(8,128)(2,1)}, bf16[1,1024,768]{1,2,0:T(8,128)(2,1)S(1)}, u32[]{:S(2)}) copy-start(bf16[1,1024,768]{1,2,0:T(8,128)(2,1)S(1)} %copy.126) | copy-start | bytes 4718596
  902.2 40.4 %slice-start.4 = ((s8[4718592]{0:T(1024)(128)(4,1)}), s8[4194304]{0:T(1024)(128)(4,1)S(1)}, s32[]{:S(2)}) async-start(s8[4718592]{0:T(1024)(128)(4,1)} %bitcast.321), calls=%async_computation.17 | async-start | bytes 8388608
  902.9 39.6 %copy-start.13 = (f32[1024,768]{0,1:T(8,128)}, f32[1024,768]{0,1:T(8,128)S(1)}, u32[]{:S(2)}) copy-start(f32[1024,768]{0,1:T(8,128)S(1)} %get-tuple-element.159) | copy-start | bytes 9437188
  903.3 39.2 %slice-start.5 = ((s8[4718592]{0:T(1024)(128)(4,1)}), s8[524288]{0:T(1024)(128)(4,1)S(1)}, s32[]{:S(2)}) async-start(s8[4718592]{0:T(1024)(128)(4,1)} %bitcast.321), calls=%async_computation.18 | async-start | bytes 1048576
  954.9 18.1 copy-start.35
  973.0 11.6 copy-start.14
  985.4 40.6 %copy-start.26 = (f32[1024,768]{0,1:T(8,128)}, f32[1024,768]{0,1:T(8,128)S(1)}, u32[]{:S(2)}) copy-start(f32[1024,768]{0,1:T(8,128)S(1)} %get-tuple-element.155) | copy-start | bytes 9437188
  1183.8 5.9 collective-permute-start.3
  1198.5 19.2 copy-start.8
  1198.5 19.2 copy-start.66
  1198.5 19.2 copy-start.76
  1217.6 11.2 copy-start.72
  1229.7 40.8 %copy-start.24 = (f32[1024,768]{0,1:T(8,128)}, f32[1024,768]{0,1:T(8,128)S(1)}, u32[]{:S(2)}) copy-start(f32[1024,768]{0,1:T(8,128)S(1)} %get-tuple-element.152) | copy-start | bytes 9437188
  1312.8 98.0 %all-to-all-start.9 = ((bf16[4096,2,192]{2,1,0:T(2,128)(2,1)}), bf16[4096,2,192]{2,1,0:T(2,128)(2,1)}, u32[]{:S(2)}, u32[]{:S(2)}) async-start(bf16[4096,2,192]{2,1,0:T(2,128)(2,1)} %copy.107), calls=%async_computation.9 | async-start | bytes 8388608 | tf_op jit(solution)/shard_map/all_to_all | solution.py:70
  1317.9 790.3 %all-reduce.4.cloned.1.call-start = ((), (), s32[]{:S(2)}) async-start(), calls=%async_computation.12 | async-start | bytes 37748736 | tf_op jit(solution)/shard_map/psum | solution.py:198
  1317.9 10.9 copy-start.36
  1318.0 21.2 slice-start.8
  1328.9 10.3 copy-start.9
  1328.9 10.3 slice-start.9
  1427.0 9.6 collective-permute-start.4
  1457.3 16.9 copy-start.11
  1457.3 16.9 copy-start.60
  1457.3 16.9 copy-start.64
  1457.3 16.9 copy-start.96
  1486.0 11.1 copy-start.68
  1486.0 11.1 copy-start.12
  1497.9 79.8 %copy-start.22 = (f32[1024,768]{0,1:T(8,128)}, f32[1024,768]{0,1:T(8,128)S(1)}, u32[]{:S(2)}) copy-start(f32[1024,768]{0,1:T(8,128)S(1)} %get-tuple-element.150) | copy-start | bytes 9437188
  1620.5 171.3 %all-to-all-start.11 = ((bf16[4096,2,192]{2,1,0:T(2,128)(2,1)}), bf16[4096,2,192]{2,1,0:T(2,128)(2,1)}, u32[]{:S(2)}, u32[]{:S(2)}) async-start(bf16[4096,2,192]{2,1,0:T(2,128)(2,1)} %copy.112), calls=%async_computation.11 | async-start | bytes 8388608 | tf_op jit(solution)/shard_map/all_to_all | solution.py:70
  1628.6 182.4 %collective-permute-start.2 = (bf16[2,1024,384]{1,2,0:T(8,128)(2,1)}, bf16[2,1024,384]{1,2,0:T(8,128)(2,1)}, u32[]{:S(2)}, u32[]{:S(2)}) collective-permute-start(bf16[2,1024,384]{1,2,0:T(8,128)(2,1)} %fusion.100), channel_id=1, source_target_pairs={{0,16},{16,0},{1,17},{17,1},{2,18},{18,2},{3,19},{19,3},{4,20},{20... | collective-permute-start | bytes 4718600 | tf_op jit(solution)/shard_map/ppermute | solution.py:18
  1809.3 81.7 %collective-permute-start.5 = (bf16[2,1024,384]{1,2,0:T(8,128)(2,1)}, bf16[2,1024,384]{1,2,0:T(8,128)(2,1)}, u32[]{:S(2)}, u32[]{:S(2)}) collective-permute-start(bf16[2,1024,384]{1,2,0:T(8,128)(2,1)} %pad_maximum_fusion.1), channel_id=1, source_target_pairs={{0,16},{16,0},{1,17},{17,1},{2,18},{18,2},{3,19},{19,3},{4,20},{20... | collective-permute-start | bytes 4718600 | tf_op jit(solution)/shard_map/ppermute | solution.py:18
  (75 other events, 286.4 us)
Sparse Core Ops, SparseCore 0:
  1486.1 622.0 all-reduce.3
where the time goes:
time: 2130 us
  blocking collectives  525 us (25%)
  matrix products  522 us (25%)
  waiting for transfers between devices  513 us (24%)
  other arithmetic  359 us (17%)
  local copies, waits for them, and re-layouts  159 us (7%)
  starting transfers between devices  34.4 us (2%)
    dot_general x21, matrix products, product(): return jnp.dot(left, right, preferred_element_type=jnp.float32)  359 us
    dynamic_update_slice x8, other arithmetic, table_rows(): cos_blocks, sin_blocks = lax.map(one_block, offsets)  294 us
    all_to_all x2, waiting for transfers between devices, spectral_back(): lax.all_to_all(paired, 'seq', split_axis=0, concat_axis=2, tiled=True)  227 us
    psum x1, waiting for transfers between devices, on_device(): summed = lax.psum(totals, ('dp', 'seq'))  214 us
    all_to_all x3, blocking collectives, spectral_back(): lax.all_to_all(grad_mix, 'seq', split_axis=1, concat_axis=0, tiled=True)  160 us
    all_to_all x2, blocking collectives, mixing(): lax.all_to_all(spectra, 'seq', split_axis=2, concat_axis=0, tiled=True)  151 us
    all_to_all x1, blocking collectives, spectral_back(): lax.all_to_all(paired, 'seq', split_axis=0, concat_axis=2, tiled=True)  98.4 us
    psum x1, blocking collectives, on_device(): summed = lax.psum(totals, ('dp', 'seq'))  75.2 us
  transfers between devices with their start and end apart: 12, of which 8 were waited for; matrix products, arithmetic and copies ran while one was open for 20% of the time, Pallas kernels for 0%

commit v1 on v0

v1 whole, which is shorter than its diff:
```python
import math

import jax
import jax.numpy as jnp
from jax import lax
from jax.experimental import pallas as pl
from jax.experimental.pallas import tpu as pltpu
from jax.sharding import PartitionSpec as P

BF = jnp.bfloat16
F32 = jnp.float32
PAD = 16
ROWS = 256
CHUNK = 768


def product(left, right):
    return jnp.dot(left, right, preferred_element_type=F32)


def contract(left, right, left_dim, right_dim):
    dims = (((left_dim,), (right_dim,)), ((), ()))
    return lax.dot_general(left, right, dims, preferred_element_type=F32)


def swap_cores(value):
    return lax.ppermute(value, "pipe", [(0, 1), (1, 0)])


def turn(phase, length):
    angles = (phase % length).astype(F32) * (2.0 * math.pi / length)
    return jnp.cos(angles), jnp.sin(angles)


def column_sets(width):
    quarter, half = width // 4, width // 2
    return (
        (list(range(quarter)) + [half], list(range(1, quarter))),
        (list(range(quarter, half)), list(range(quarter, half))),
    )


def feature_tables(width, core):
    sets = column_sets(width)
    order = []
    for cos_ids, sin_ids in sets:
        order.append(([k for k in cos_ids] + [k for k in sin_ids], [0] * len(cos_ids) + [1] * len(sin_ids)))
    ids_a = jnp.array(order[0][0] + order[1][0], jnp.int32)
    ids_b = jnp.array(order[1][0] + order[0][0], jnp.int32)
    odd_a = jnp.array(order[0][1] + order[1][1], jnp.int32)
    odd_b = jnp.array(order[1][1] + order[0][1], jnp.int32)
    first = core == 0
    ids = jnp.where(first, ids_a, ids_b)
    odd = jnp.where(first, odd_a, odd_b)
    sign = jnp.where(first, 1.0, -1.0)
    rows = jnp.arange(width, dtype=jnp.int32)
    cos, sin = turn(rows[:, None] * ids[None, :], width)
    spread = jnp.where(odd[None, :] == 1, -sign * sin, cos).astype(BF)
    direct = rows[None, :] == ids[:, None]
    mirror = rows[None, :] == ((width - ids) % width)[:, None]
    even_rows = (direct | mirror).astype(F32)
    odd_rows = sign * (direct.astype(F32) - mirror.astype(F32))
    unfold = jnp.where(odd[:, None] == 1, odd_rows, even_rows).astype(BF)
    return spread, unfold


def token_tables(block, rows, blocks, length):
    tall = rows + PAD
    inner = jnp.arange(tall, dtype=jnp.int32)
    slots = jnp.arange(blocks, dtype=jnp.int32)
    columns = ((block + blocks - slots) % blocks * rows)[:, None, None] + inner
    coarse = block * rows + PAD * jnp.arange(tall // PAD, dtype=jnp.int32)
    fine = jnp.arange(PAD, dtype=jnp.int32)
    cos_c, sin_c = turn(coarse[:, None] * columns, length)
    cos_f, sin_f = turn(fine[:, None] * columns, length)
    cos_c, sin_c, cos_f, sin_f = cos_c[:, :, None], sin_c[:, :, None], cos_f[:, None], sin_f[:, None]
    cos = (cos_c * cos_f - sin_c * sin_f).astype(BF)
    sin = (sin_c * cos_f + cos_c * sin_f).astype(BF)
    return cos.reshape(blocks, tall, tall), sin.reshape(blocks, tall, tall)


def row_block(height, width):
    return pl.BlockSpec((height, width), lambda i: (i, 0))


def whole(*shape):
    return pl.BlockSpec(shape, lambda *_: (0,) * len(shape), pipeline_mode=pl.Buffered(1))


def scalar_block():
    return pl.BlockSpec(memory_space=pltpu.SMEM)


def layer_block(layer, *shape):
    return pl.BlockSpec((1, *shape), lambda i: (layer,) + (0,) * len(shape), pipeline_mode=pl.Buffered(1))


def call(body, grid, in_specs, out_specs, out_shape, flops, moved, name, vmem):
    return pl.pallas_call(
        body,
        grid=grid,
        in_specs=in_specs,
        out_specs=out_specs,
        out_shape=out_shape,
        compiler_params=pltpu.CompilerParams(vmem_limit_bytes=vmem << 20),
        cost_estimate=pl.CostEstimate(flops=flops, bytes_accessed=moved, transcendentals=0),
        name=name,
    )


def like(*shape, dtype=BF):
    return jax.ShapeDtypeStruct(shape, dtype)


def divisor(count, most):
    return max(d for d in range(1, most + 1) if count % d == 0)


def fold_spectra(core, own, recv):
    rows, half = own.shape

    def body(core_ref, own_ref, recv_ref, out_ref):
        first = core_ref[0] == 0
        out_ref[:rows] = (own_ref[...].astype(F32) + recv_ref[...].astype(F32)).astype(BF)
        mine, theirs = own_ref[:PAD], recv_ref[:PAD]
        at = lax.broadcasted_iota(jnp.int32, (PAD, half), 0)
        low = jnp.where(first, mine, theirs)
        high = jnp.where(first, theirs, mine)
        out_ref[:PAD] = jnp.where(at == 0, low, out_ref[:PAD])
        out_ref[rows:] = jnp.where(at == 0, high, jnp.zeros_like(high))

    spec = pl.BlockSpec((rows, half), lambda i: (0, 0))
    return call(
        body,
        (1,),
        [scalar_block(), spec, spec],
        pl.BlockSpec((rows + PAD, half), lambda i: (0, 0)),
        like(rows + PAD, half),
        rows * half,
        6 * rows * half,
        "fold_spectra",
        8,
    )(core, own, recv)


def transform_part(cos, sin, slot, part):
    tall, half = part.shape
    wide = -(-(half // 2 + 1) // 128) * 128
    tile = divisor(tall // PAD, 17) * PAD

    def body(cos_ref, sin_ref, part_ref, out_ref):
        out_ref[:, :wide] = product(cos_ref[0], part_ref[:, :wide])
        out_ref[:, wide:] = product(sin_ref[0], part_ref[:, half - wide :])

    table = pl.BlockSpec((1, tile, tall), lambda i: (slot, i, 0))
    return call(
        body,
        (tall // tile,),
        [table, table, whole(tall, half)],
        row_block(tile, 2 * wide),
        like(tall, 2 * wide, dtype=F32),
        4 * tall * tall * wide,
        4 * tall * (tall + 2 * wide),
        "transform_part",
        12,
    )(cos, sin, part)


def transform_rest(core, cos, sin, begun, parts, factor):
    tall, half = parts[0].shape
    wide = begun.shape[1] // 2
    tile = divisor(tall // PAD, 17) * PAD
    lead = half - wide

    def body(*refs):
        core_ref, begun_ref = refs[:2]
        tables = refs[2 : 2 + 2 * len(parts)]
        part_refs = refs[2 + 2 * len(parts) : -1]
        out_ref = refs[-1]
        even, odd = begun_ref[:, :wide], begun_ref[:, wide:]
        for at, part_ref in enumerate(part_refs):
            even = even + product(tables[2 * at][0], part_ref[:, :wide])
            odd = odd + product(tables[2 * at + 1][0], part_ref[:, lead:])
        lanes = lax.broadcasted_iota(jnp.int32, (tile, wide - lead), 1) + lead
        cos_count = half // 2 + 1 - core_ref[0]
        middle = jnp.where(lanes < cos_count, even[:, lead:], odd[:, : wide - lead])
        out_ref[:, :lead] = (even[:, :lead] * factor).astype(BF)
        out_ref[:, lead:wide] = (middle * factor).astype(BF)
        out_ref[:, wide:] = (odd[:, wide - lead :] * factor).astype(BF)

    tables, specs = [], []
    for at in range(len(parts)):
        spec = pl.BlockSpec((1, tile, tall), lambda i, at=at: (at + 1, i, 0))
        tables += [cos, sin]
        specs += [spec, spec]
    return call(
        body,
        (tall // tile,),
        [scalar_block(), row_block(tile, 2 * wide)] + specs + [whole(tall, half)] * len(parts),
        row_block(tile, half),
        like(tall, half),
        4 * tall * tall * wide * len(parts),
        4 * tall * (tall * len(parts) + 2 * wide),
        "transform_rest",
        14,
    )(core, begun, *tables, *parts)


def transform(core, own, recv, cos, sin, group_shifts, factor, beside=None):
    folded = fold_spectra(core, own, recv)
    parts = [lax.ppermute(folded, "seq", pairs) for pairs in group_shifts]
    begun = transform_part(cos, sin, 0, folded)
    mixed = transform_rest(core, cos, sin, begun, parts, factor)
    return mixed, swap_cores(mixed)


def standardize(hidden):
    centered = hidden - jnp.mean(hidden, axis=-1, keepdims=True)
    spread = jnp.mean(centered * centered, axis=-1, keepdims=True)
    scale = lax.rsqrt(spread + 1e-05)
    return centered * scale, scale


def standardize_back(grad, unit, scale):
    mean_grad = jnp.mean(grad, axis=-1, keepdims=True)
    mean_both = jnp.mean(grad * unit, axis=-1, keepdims=True)
    return (grad - mean_grad - unit * mean_both) * scale


def mixture_tile(core_ref, mine_ref, mine_top, theirs_ref, theirs_top, unfold_ref):
    tile, half = mine_ref.shape
    at = lax.broadcasted_iota(jnp.int32, (tile, half), 0)
    odd_row = (at == 0) & (core_ref[0] == 1) & (pl.program_id(0) == 0)
    mine = jnp.where(odd_row, mine_top[:1], mine_ref[...])
    theirs = jnp.where(odd_row, theirs_top[:1], theirs_ref[...])
    return product(mine, unfold_ref[:half]) + product(theirs, unfold_ref[half:])


def mixture_specs(rows, half, tile):
    block = row_block(tile, half)
    top = pl.BlockSpec((PAD, half), lambda i: (rows // PAD, 0))
    return [block, top, block, top, whole(2 * half, 2 * half)]


def spectra_call(core, x, spread):
    rows, width = x.shape
    half = width // 2
    tile = min(ROWS, rows)
    factor = 1.0 / math.sqrt(width)

    def body(x_ref, spread_ref, own_ref, other_ref):
        spectra = product(x_ref[...], spread_ref[...]) * factor
        own_ref[...] = spectra[:, :half].astype(BF)
        other_ref[...] = spectra[:, half:].astype(BF)

    return call(
        body,
        (rows // tile,),
        [row_block(tile, width), whole(width, width)],
        [row_block(tile, half)] * 2,
        [like(rows, half)] * 2,
        2 * rows * width * width,
        4 * rows * width,
        "spectra",
        12,
    )(x, spread)


def forward(core, layer, x, mixed, unfold, w1, w2, b1, vec, spread):
    rows, width = x.shape
    hidden = w1.shape[2]
    half = width // 2
    tile = min(ROWS, rows)
    chunk = min(CHUNK, hidden)
    factor = 1.0 / math.sqrt(width)

    def body(core_ref, x_ref, m0, t0, m1, t1, unfold_ref, w1_ref, w2_ref, b1_ref, vec_ref, spread_ref, *outs):
        out_ref, own_ref, other_ref, low_ref, act_ref, slope_ref, unit1_ref, scale1_ref, unit2_ref, scale2_ref = outs
        mixture = mixture_tile(core_ref, m0, t0, m1, t1, unfold_ref).astype(BF).astype(F32)
        unit, scale = standardize(x_ref[...].astype(F32) + mixture)
        b2, mg, ms, og, os = (vec_ref[0, i : i + 1] for i in range(5))
        normed = unit * mg + ms
        unit1_ref[...] = unit.astype(BF)
        scale1_ref[...] = jnp.broadcast_to(scale, scale1_ref.shape)
        low = normed.astype(BF)
        low_ref[...] = low
        total = normed + b2
        for start in range(0, hidden, chunk):
            span = slice(start, start + chunk)
            pre = product(low, w1_ref[0, :, span]) + b1_ref[0, :, span]
            cdf = 0.5 + 0.5 * lax.erf(pre * (1.0 / math.sqrt(2.0)))
            act = (pre * cdf).astype(BF)
            act_ref[:, span] = act
            slope_ref[:, span] = (cdf + pre * (jnp.exp(-0.5 * pre * pre) * (1.0 / math.sqrt(2.0 * math.pi)))).astype(BF)
            total = total + product(act, w2_ref[0, span, :])
        unit, scale = standardize(total)
        unit2_ref[...] = unit.astype(BF)
        scale2_ref[...] = jnp.broadcast_to(scale, scale2_ref.shape)
        out = (unit * og + os).astype(BF)
        out_ref[...] = out
        spectra = product(out, spread_ref[...]) * factor
        own_ref[...] = spectra[:, :half].astype(BF)
        other_ref[...] = spectra[:, half:].astype(BF)

    mine, theirs = mixed
    return call(
        body,
        (rows // tile,),
        [scalar_block(), row_block(tile, width)]
        + mixture_specs(rows, half, tile)
        + [
            layer_block(layer, width, hidden),
            layer_block(layer, hidden, width),
            layer_block(layer, 1, hidden),
            layer_block(layer, 5, width),
            whole(width, width),
        ],
        [
            row_block(tile, width),
            row_block(tile, half),
            row_block(tile, half),
            row_block(tile, width),
            row_block(tile, hidden),
            row_block(tile, hidden),
            row_block(tile, width),
            row_block(tile, 128),
            row_block(tile, width),
            row_block(tile, 128),
        ],
        [
            like(rows, width),
            like(rows, half),
            like(rows, half),
            like(rows, width),
            like(rows, hidden),
            like(rows, hidden),
            like(rows, width),
            like(rows, 128, dtype=F32),
            like(rows, width),
            like(rows, 128, dtype=F32),
        ],
        4 * rows * width * (hidden + width),
        4 * width * hidden + 4 * rows * hidden + 14 * rows * width,
        "layer_forward",
        34,
    )(core, x, mine, mine, theirs, theirs, unfold, w1, w2, b1, vec, spread)


def backward(core, layer, grad, mixed, unfold, kept, w1, w2, vec, spread):
    low, act, slope, unit1, scale1, unit2, scale2 = kept
    rows, width = grad.shape
    hidden = w1.shape[2]
    half = width // 2
    tile = min(ROWS, rows)
    chunk = min(CHUNK, hidden)
    factor = 1.0 / math.sqrt(width)
    count = 0 if mixed is None else 6

    def body(*refs):
        grad_ref = refs[0]
        slope_ref, unit1_ref, scale1_ref, unit2_ref, scale2_ref, w1_ref, w2_ref, vec_ref, spread_ref = refs[1 + count : 10 + count]
        gh_ref, gb_ref, gp_ref, own_ref, other_ref, wide_ref, sums_ref = refs[10 + count :]

        @pl.when(pl.program_id(0) == 0)
        def _():
            wide_ref[...] = jnp.zeros_like(wide_ref)
            sums_ref[...] = jnp.zeros_like(sums_ref)

        grad = grad_ref[...].astype(F32)
        if count:
            grad = (grad + mixture_tile(*refs[1 : 1 + count])).astype(BF).astype(F32)
        mg, og = vec_ref[0, 1:2], vec_ref[0, 3:4]
        unit2 = unit2_ref[...].astype(F32)
        g_branch = standardize_back(grad * og, unit2, scale2_ref[:, :1])
        gb = g_branch.astype(BF)
        gb_ref[...] = gb
        total = g_branch
        for start in range(0, hidden, chunk):
            span = slice(start, start + chunk)
            g_act = contract(gb, w2_ref[0, span, :], 1, 1)
            gp = (g_act * slope_ref[:, span].astype(F32)).astype(BF)
            gp_ref[:, span] = gp
            wide_ref[:, span] += jnp.sum(gp.astype(F32), axis=0, keepdims=True)
            total = total + contract(gp, w1_ref[0, :, span], 1, 1)
        unit1 = unit1_ref[...].astype(F32)
        g_h = standardize_back(total * mg, unit1, scale1_ref[:, :1])
        gh_ref[...] = g_h
        for at, terms in enumerate((gb.astype(F32), total * unit1, total, grad * unit2, grad)):
            sums_ref[at : at + 1] += jnp.sum(terms, axis=0, keepdims=True)
        spectra = product(g_h.astype(BF), spread_ref[...]) * factor
        own_ref[...] = spectra[:, :half].astype(BF)
        other_ref[...] = spectra[:, half:].astype(BF)

    if count:
        mine, theirs = mixed
        extra = [core, mine, mine, theirs, theirs, unfold]
        extra_specs = [scalar_block()] + mixture_specs(rows, half, tile)
    else:
        extra, extra_specs = [], []
    return call(
        body,
        (rows // tile,),
        [row_block(tile, width)]
        + extra_specs
        + [
            row_block(tile, hidden),
            row_block(tile, width),
            row_block(tile, 128),
            row_block(tile, width),
            row_block(tile, 128),
            layer_block(layer, width, hidden),
            layer_block(layer, hidden, width),
            layer_block(layer, 5, width),
            whole(width, width),
        ],
        [
            row_block(tile, width),
            row_block(tile, width),
            row_block(tile, hidden),
            row_block(tile, half),
            row_block(tile, half),
            whole(1, hidden),
            whole(8, width),
        ],
        [
            like(rows, width, dtype=F32),
            like(rows, width),
            like(rows, hidden),
            like(rows, half),
            like(rows, half),
            like(1, hidden, dtype=F32),
            like(8, width, dtype=F32),
        ],
        4 * rows * width * (hidden + width),
        4 * width * hidden + 4 * rows * hidden + 14 * rows * width,
        "layer_backward",
        34,
    )(grad, *extra, slope, unit1, scale1, unit2, scale2, w1, w2, vec, spread)


def weight_grad(scalars, low, gp, act, gb, start, count, recv=None):
    rows, width = low.shape

    def body(scalar_ref, low_ref, gp_ref, act_ref, gb_ref, *refs):
        def write(value):
            if recv is None:
                refs[0][0] = value.astype(BF)
            else:
                value = (value + refs[0][0].astype(F32)).astype(BF)
                refs[1][0] = value[: width // 2]
                refs[2][0] = value[width // 2 :]

        @pl.when(scalar_ref[0] == 0)
        def _():
            write(contract(low_ref[...], gp_ref[...], 0, 0))

        @pl.when(scalar_ref[0] != 0)
        def _():
            write(contract(act_ref[...], gb_ref[...], 0, 0))

    full = pl.BlockSpec((rows, width), lambda j, s: (0, 0))
    block = pl.BlockSpec((1, width, width), lambda j, s: (j, 0, 0))
    half = pl.BlockSpec((1, width // 2, width), lambda j, s: (j, 0, 0))
    return pl.pallas_call(
        body,
        grid_spec=pltpu.PrefetchScalarGridSpec(
            num_scalar_prefetch=1,
            grid=(count,),
            in_specs=[
                full,
                pl.BlockSpec((rows, width), lambda j, s: (0, jnp.where(s[0] == 0, (j + start) ^ s[1], 0))),
                pl.BlockSpec((rows, width), lambda j, s: (0, jnp.where(s[0] == 0, 0, (j + start) ^ s[1]))),
                full,
            ]
            + ([] if recv is None else [block]),
            out_specs=block if recv is None else [half, half],
        ),
        out_shape=like(count, width, width) if recv is None else [like(count, width // 2, width)] * 2,
        compiler_params=pltpu.CompilerParams(vmem_limit_bytes=26 << 20),
        cost_estimate=pl.CostEstimate(
            flops=2 * rows * width * width * count, bytes_accessed=2 * rows * width * (count + 2) + 2 * width * width * count, transcendentals=0
        ),
        name="weight_grad",
    )(scalars, low, gp, act, gb, *([] if recv is None else [recv]))


def write_weights(scalars, first_mine, first_far, second_far, second_mine):
    count, halves, slots, piece, width = first_mine.shape
    tall = slots * piece

    def body(s, a_ref, b_ref, c_ref, d_ref, in_ref, out_ref):
        def write(source, target):
            for slot in range(slots):
                at = pl.multiple_of((s[2] + slots - slot) % slots * piece, piece)
                target[0, pl.ds(at, piece), :] = source[0, 0, slot].astype(F32)

        @pl.when(s[0] == 0)
        def _():
            write(a_ref, in_ref)
            write(b_ref, out_ref)

        @pl.when(s[0] != 0)
        def _():
            write(c_ref, in_ref)
            write(d_ref, out_ref)

    def source(core):
        return pl.BlockSpec(
            (1, 1, slots, piece, width),
            lambda q, h, s: (jnp.where(s[0] == core, q, 0), jnp.where(s[0] == core, h, 0), 0, 0, 0),
        )

    return pl.pallas_call(
        body,
        grid_spec=pltpu.PrefetchScalarGridSpec(
            num_scalar_prefetch=1,
            grid=(count, halves),
            in_specs=[source(0), source(0), source(1), source(1)],
            out_specs=[
                pl.BlockSpec((1, tall, width), lambda q, h, s: (0, h, q ^ s[1])),
                pl.BlockSpec((1, tall, width), lambda q, h, s: (0, (q ^ s[1]) * halves + h, 0)),
            ],
        ),
        out_shape=[like(1, tall * halves, width * count, dtype=F32), like(1, tall * halves * count, width, dtype=F32)],
        compiler_params=pltpu.CompilerParams(vmem_limit_bytes=20 << 20),
        cost_estimate=pl.CostEstimate(flops=0, bytes_accessed=12 * width * width * count, transcendentals=0),
        name="write_weights",
    )(scalars, first_mine, first_far, second_far, second_mine)


def finish(core, g_h, mixed, unfold):
    rows, width = g_h.shape
    half = width // 2
    tile = min(ROWS, rows)

    def body(g_ref, *refs):
        refs[-1][...] = (g_ref[...] + mixture_tile(*refs[:-1])).astype(BF)

    mine, theirs = mixed
    return call(
        body,
        (rows // tile,),
        [row_block(tile, width), scalar_block()] + mixture_specs(rows, half, tile),
        row_block(tile, width),
        like(rows, width),
        2 * rows * width * width,
        8 * rows * width,
        "finish",
        14,
    )(g_h, core, mine, mine, theirs, theirs, unfold)


def bit_pairs(count, bit):
    return [(i, i ^ (1 << bit)) for i in range(count)]


def added(left, right):
    return (left.astype(F32) + right.astype(F32)).astype(BF)


class Line:
    def __init__(self):
        self.last = None

    def __call__(self, step, *args):
        if self.last is not None:
            args, _ = lax.optimization_barrier((args, self.last))
        out = step(*args)
        self.last = min(jax.tree.leaves(out), key=lambda leaf: leaf.size)
        return out

    def after(self, value):
        return lax.optimization_barrier((value, self.last))[0]


class ChipSum:
    def __init__(self):
        self.peers = lax.axis_size("seq")
        self.z = lax.axis_index("seq")

    def across(self, bit, value):
        return lax.ppermute(value, "dp", bit_pairs(4, bit))

    def along(self, value, by):
        return lax.ppermute(value, "seq", [(i, (i + by) % self.peers) for i in range(self.peers)])

    def start_upper(self, upper):
        self.upper = upper
        self.got = [self.across(0, upper[0][1]), self.across(1, upper[1])]

    def start_lower(self, lower):
        self.lower = lower
        self.got.append(self.across(0, lower[0][1]))

    def first_sums(self):
        args = (self.upper[0], self.lower[0], self.lower[1], *self.got)
        return (lambda u, a, b, g3, g23, g1: (added(u[0], g3), added(a[0], g1), added(b[1], g23[1]), added(b[0], g23[0]))), args

    def start_second(self, sums):
        self.kept = (sums[1], sums[3])
        self.got = (self.across(1, sums[0]), self.across(0, sums[2]))

    def second_sums(self):
        def step(a, b, g0, g1, z):
            both = jnp.stack([added(a, g0), added(b, g1)])
            both = both.reshape(2, self.peers, -1, both.shape[-1])
            return [lax.dynamic_index_in_dim(both, (z + d) % self.peers, 1, keepdims=False) for d in range(self.peers)]

        return step, (*self.kept, *self.got, self.z)

    def start_scatter(self, pieces):
        self.kept = pieces[0]
        self.got = [self.along(piece, d) for d, piece in enumerate(pieces) if d]

    def scattered(self):
        def step(kept, *got):
            return sum((g.astype(F32) for g in got), kept.astype(F32)).astype(BF)

        return step, (self.kept, *self.got)

    def start_gather(self, piece):
        self.kept = piece
        self.got = [self.along(piece, d) for d in range(1, self.peers)]

    def gathered(self):
        def step(*pieces):
            return [jnp.stack([piece[at] for piece in pieces]) for at in range(2)]

        return step, (self.kept, *self.got)

    def start_back(self, halves):
        self.own = halves
        self.near = (self.across(1, halves[0]), self.across(0, halves[1]))

    def start_last(self):
        self.far = [
            (self.across(0, self.own[0]), self.across(0, self.near[0])),
            (self.across(1, self.own[1]), self.across(1, self.near[1])),
        ]

    def pieces(self):
        def step(a, b, a2, b1, a1, a3, b2, b3):
            return jnp.stack([jnp.stack([a, b]), jnp.stack([a1, b1]), jnp.stack([a2, b2]), jnp.stack([a3, b3])])

        return step, (*self.own, *self.near, *self.far[0], *self.far[1])


def small_hops():
    hops = []
    for axis in ("pipe", "seq", "dp"):
        count = lax.axis_size(axis)
        hops += [(axis, bit_pairs(count, bit)) for bit in range(count.bit_length() - 1)]
    return hops


def on_device(
    inputs,
    cotangent,
    in_weight,
    in_bias,
    out_weight,
    out_bias,
    mix_gain,
    mix_shift,
    out_gain,
    out_shift,
):
    rows, width = inputs.shape[1:]
    hidden = in_weight.shape[2]
    peers = lax.axis_size("seq")
    blocks = peers // 2
    half = width // 2
    core = lax.axis_index("pipe")
    z = lax.axis_index("seq")
    first = core == 0
    low = z < blocks
    local = low == first
    block = jnp.minimum(z, peers - 1 - z)
    which = core.astype(jnp.int32).reshape(1)

    def place(member, is_low):
        return member if is_low else peers - 1 - member

    group_shifts = [
        [(place(b, side), place((b + d) % blocks, side)) for side in (True, False) for b in range(blocks)]
        for d in range(1, blocks)
    ]
    in_pairs = []
    out_pairs = ([], [])
    for i in range(peers):
        facing = peers - 1 - i
        source = peers + i if i < blocks else i
        in_pairs.append((source, facing if i < blocks else peers + facing))
        out_pairs[0].append((source, facing))
        out_pairs[1].append((source, peers + facing))

    row_ids = lax.broadcasted_iota(jnp.int32, (rows, rows), 0)
    col_ids = lax.broadcasted_iota(jnp.int32, (rows, rows), 1)
    order = (col_ids == jnp.where(first, row_ids, (rows - row_ids) % rows)).astype(BF)

    def send_in(items):
        sent = jnp.where(low, items[1], items[0])
        kept = jnp.where(low, items[0], items[1])
        return kept, lax.ppermute(sent, ("pipe", "seq"), in_pairs)

    def arranged(kept, moved):
        return product(order, jnp.where(local, kept, moved)).astype(BF)

    def give_start(value):
        mine = jnp.where(first, value[:, :half], value[:, half:])
        theirs = jnp.where(first, value[:, half:], value[:, :half])
        return (
            mine,
            swap_cores(theirs),
            lax.ppermute(value[:, :half], ("pipe", "seq"), out_pairs[0]),
            lax.ppermute(value[:, half:], ("pipe", "seq"), out_pairs[1]),
        )

    def give_end(moved):
        mine, beside, far0, far1 = moved
        near_part = jnp.where(local, mine, beside)
        far_part = jnp.where(first, far0, far1)
        return jnp.stack([jnp.where(low, near_part, far_part), jnp.where(low, far_part, near_part)])

    x = arranged(*send_in(inputs))
    vectors = jnp.concatenate([in_bias[0], out_bias[0], mix_gain[0], mix_shift[0], out_gain[0], out_shift[0]])
    other_vectors = swap_cores(vectors)
    vectors = jnp.where(first, jnp.stack([vectors, other_vectors]), jnp.stack([other_vectors, vectors]))
    b1 = vectors[:, :hidden].reshape(2, 1, hidden)
    vec = vectors[:, hidden:].reshape(2, 5, width)
    w1 = lax.all_gather(in_weight, "pipe", axis=0, tiled=True)
    w2 = lax.all_gather(out_weight, "pipe", axis=0, tiled=True)
    spread, unfold = feature_tables(width, core)
    cos, sin = token_tables(block, rows, blocks, rows * peers)
    factor = 1.0 / math.sqrt(rows * peers)

    line = Line()

    def fold(own, other):
        folded = line(lambda a, b: fold_spectra(which, a, b), own, swap_cores(other))
        return folded, [lax.ppermute(folded, "seq", pairs) for pairs in group_shifts]

    def part(folded):
        return line(lambda f: transform_part(cos, sin, 0, f), folded)

    def rest(begun, parts):
        mixed = line(lambda a, *b: transform_rest(which, cos, sin, a, list(b), factor), begun, *parts)
        return mixed, swap_cores(mixed)

    kept = []
    own, other = line(lambda v: spectra_call(which, v, spread), x)
    for layer in range(2):
        folded, parts = fold(own, other)
        begun = part(folded)
        if layer == 1:
            grad = line(lambda v, w: arranged(v, w), *cot)
        mixed = rest(begun, parts)
        if layer == 0:
            cot = send_in(line.after(cotangent))
        x, own, other, *saved = line(
            lambda v, m, l=layer: forward(which, l, v, m, unfold, w1, w2, b1, vec, spread), x, mixed
        )
        kept.append(saved)

    def back(layer, grad, mixed):
        return line(
            lambda g, m, k: backward(which, layer, g, m, unfold, k, w1, w2, vec, spread), grad, mixed, kept[layer]
        )

    index = lax.axis_index("dp")
    zero = jnp.zeros((), jnp.int32)
    quick = lax.axis_size("dp") == 4 and hidden == 4 * width and (width // 2) % peers == 0
    begin = index if quick else zero
    to_mine = jnp.stack([core, begin]).astype(jnp.int32)
    to_theirs = jnp.stack([1 - core, begin]).astype(jnp.int32)

    def theirs(layer, start, count, gp, gb):
        return swap_cores(
            line(lambda t, a, c, p, b: weight_grad(t, a, p, c, b, start, count), to_theirs, *kept[layer][:2], gp, gb)
        )

    def mine(layer, start, count, gp, gb, recv):
        return line(
            lambda t, a, c, p, b, r: weight_grad(t, a, p, c, b, start, count, r), to_mine, *kept[layer][:2], gp, gb, recv
        )

    def run(work):
        return line(work[0], *work[1])

    def flat_small(wide, narrow):
        return jnp.concatenate([wide.reshape(-1), narrow[:5].reshape(-1)])

    sums = [ChipSum(), ChipSum()]
    early = sums[1]
    late = sums[0]
    grad, gb1, gp1, own, other, wide1, narrow1 = back(1, grad, None)
    folded, parts = fold(own, other)
    half_count = hidden // width // 2
    upper = theirs(1, half_count, half_count, gp1, gb1)
    lower = theirs(1, 0, half_count, gp1, gb1)
    begun = part(folded)
    early.start_upper(mine(1, half_count, half_count, gp1, gb1, upper))
    early.start_lower(mine(1, 0, half_count, gp1, gb1, lower))
    out_ready = line(lambda v: product(order, v).astype(BF), x)
    mixed = rest(begun, parts)
    out_moved = give_start(line.after(out_ready))
    grad, gb0, gp0, own, other, wide0, narrow0 = back(0, grad, mixed)
    folded, parts = fold(own, other)
    early.start_second(run(early.first_sums()))
    upper = theirs(0, half_count, half_count, gp0, gb0)
    lower = theirs(0, 0, half_count, gp0, gb0)
    late.start_upper(mine(0, half_count, half_count, gp0, gb0, upper))
    late.start_lower(mine(0, 0, half_count, gp0, gb0, lower))
    begun = part(folded)
    out = line(give_end, out_moved)
    early.start_scatter(run(early.second_sums()))
    mixed = rest(begun, parts)
    in_ready = line(lambda g, m: product(order, finish(which, g, m, unfold)).astype(BF), grad, mixed)
    early.start_gather(run(early.scattered()))
    small = line(lambda *v: jnp.stack([flat_small(*v[:2]), flat_small(*v[2:])]), wide0, narrow0, wide1, narrow1)
    hops = small_hops()
    late.start_second(run(late.first_sums()))
    early.start_back(run(early.gathered()))
    in_moved = give_start(line.after(in_ready))
    for axis, pairs in hops[:2]:
        small = line(lambda a, b: a + b, small, lax.ppermute(small, axis, pairs))
    late.start_scatter(run(late.second_sums()))
    early.start_last()
    for axis, pairs in hops[2:]:
        small = line(lambda a, b: a + b, small, lax.ppermute(small, axis, pairs))
    late.start_gather(run(late.scattered()))
    in_grad = line(give_end, in_moved)
    early_sum = run(early.pieces())
    to_second = lax.ppermute(early_sum, "pipe", [(0, 1)])
    late.start_back(run(late.gathered()))
    late.start_last()
    late_sum = run(late.pieces())
    to_first = lax.ppermute(late_sum, "pipe", [(1, 0)])
    scalars = jnp.stack([core, index, z]).astype(jnp.int32)
    g_w1, g_w2 = line(write_weights, scalars, late_sum, to_first, to_second, early_sum)
    small = jnp.where(first, small[0], small[1])
    g_b1 = small[:hidden]
    g_b2, g_mg, g_ms, g_og, g_os = (small[hidden + i * width : hidden + (i + 1) * width] for i in range(5))
    return (
        out,
        in_grad,
        g_w1,
        g_b1[None],
        g_w2,
        g_b2[None],
        g_mg[None],
        g_ms[None],
        g_og[None],
        g_os[None],
    )


def solution(mesh):
    return jax.shard_map(
        on_device,
        mesh=mesh,
        in_specs=(
            P("dp", "seq", None),
            P("dp", "seq", None),
            P("pipe", None, None),
            P("pipe", None),
            P("pipe", None, None),
            P("pipe", None),
            P("pipe", None),
            P("pipe", None),
            P("pipe", None),
            P("pipe", None),
        ),
        out_specs=(
            P("dp", "seq", "pipe"),
            P("dp", "seq", "pipe"),
            P("pipe", None, None),
            P("pipe", None),
            P("pipe", None, None),
            P("pipe", None),
            P("pipe", None),
            P("pipe", None),
            P("pipe", None),
            P("pipe", None),
        ),
        check_vma=False,
    )
```

time: 2130 us -> 625 us (0.29)
  the two profiles are of different devices: /device:TPU:0 before, /device:TPU:25 now
where the time goes in v1:
time: 625 us; the launch traced here: 616 us
  waiting for transfers between devices  209 us (33%)
  Pallas kernels  164 us (26%)
  starting transfers between devices  114 us (18%)
  local copies, waits for them, and re-layouts  52.8 us (8%)
  other arithmetic  47.3 us (8%)
  between operations  16 us (3%)
  matrix products  11.6 us (2%)
    ppermute x22, waiting for transfers between devices, across(): return lax.ppermute(value, 'dp', bit_pairs(4, bit))  81.1 us
    ppermute x12, waiting for transfers between devices, along(): lax.ppermute(value, 'seq', [(i, (i + by) % self.peers) for i in range(sel...  78.5 us
    pallas_call x2, Pallas kernels, forward(): call(body, (rows // tile,), [scalar_block(), row_block(tile, width)] + mi...  48.7 us
    unnamed x183, local copies, waits for them, and re-layouts  46.7 us
    pallas_call x2, Pallas kernels, backward(): call(body, (rows // tile,), [row_block(tile, width)] + extra_specs + [row...  43.6 us
    pallas_call x8, Pallas kernels, weight_grad(): pl.pallas_call(body, grid_spec=pltpu.PrefetchScalarGridSpec(num_scalar_pr...  35.2 us
    ppermute x4, waiting for transfers between devices, fold(): lax.ppermute(folded, 'seq', pairs)  32.6 us
    ppermute x15, starting transfers between devices, swap_cores(): return lax.ppermute(value, 'pipe', [(0, 1), (1, 0)])  30.2 us
  transfers between devices with their start and end apart: 68, of which 25 were waited for; matrix products, arithmetic and copies ran while one was open for 10% of the time, Pallas kernels for 15%

profile of v1, /device:TPU:25, one launch (start us, length us, event | category | flops | bytes accessed | tf_op | source)
XLA Modules:
  0.0 615.8 jit_solution(14799183719691807823)
XLA Ops:
  14.2 11.8 %select_convert_fusion = (bf16[768,768]{1,0:T(8,128)(2,1)}, bf16[768,768]{1,0:T(8,128)(2,1)S(1)}) fusion(s32[768]{0:T(1024)S(1)} %get-tuple-element.499, s32[768]{0:T(1024)S(1)} %get-tuple-element.500, f32[]{:T(128)S(6)} %select_n.279, pred[768]{0:T(1024)(128)(4,1)S(1)} %select_compare_fusion.1, f32[]{:T(128)S(6)} %neg.3), kind=kLoop, calls=%fused_computation.8 | loop fusion | flops 12976128 | bytes 2366216 | tf_op jit(solution)/shard_map/convert_element_type | solution.py:63
  30.2 11.2 %collective-permute-start.1 = (bf16[1024,384]{1,0:T(8,128)(2,1)S(1)}, bf16[1024,384]{1,0:T(8,128)(2,1)S(1)}, u32[]{:S(2)}, u32[]{:S(2)}) collective-permute-start(bf16[1024,384]{1,0:T(8,128)(2,1)S(1)} %get-tuple-element.229), channel_id=1, source_target_pairs={{0,16},{16,0},{1,17},{17,1},{2,18},{18,2},{3,19},{19,3},{4,20},{20... | collective-permute-start | bytes 2359304 | tf_op jit(solution)/shard_map/ppermute | solution.py:27
  45.0 15.7 %collective-permute-start.2 = (bf16[1040,384]{1,0:T(8,128)(2,1)S(1)}, bf16[1040,384]{1,0:T(8,128)(2,1)S(1)}, u32[]{:S(2)}, u32[]{:S(2)}) collective-permute-start(bf16[1040,384]{1,0:T(8,128)(2,1)S(1)} %fold_spectra.4.part_ref), channel_id=1, source_target_pairs={{0,1},{1,0},{3,2},{2,3},{4,5},{5,4},{7,6},{6,7},{8,9},{9,8},{11,10... | collective-permute-start | bytes 2396168 | tf_op jit(solution)/shard_map/ppermute | solution.py:741
  60.7 3.3 add_convert_fusion
  66.3 12.5 %collective-permute-done.2.refs_4_ = bf16[1040,384]{1,0:T(8,128)(2,1)S(1)} collective-permute-done((bf16[1040,384]{1,0:T(8,128)(2,1)S(1)}, bf16[1040,384]{1,0:T(8,128)(2,1)S(1)}, u32[]{:S(2)}, u32[]{:S(2)}) %collective-permute-start.2) | collective-permute-done | bytes 798752 | tf_op jit(solution)/shard_map/ppermute | solution.py:741
  82.0 3.8 select_bitcast_fusion
  94.6 24.1 %layer_forward.2 = (bf16[1024,768]{1,0:T(8,128)(2,1)S(1)}, bf16[1024,384]{1,0:T(8,128)(2,1)S(1)}, bf16[1024,384]{1,0:T(8,128)(2,1)S(1)}, bf16[1024,768]{1,0:T(8,...) custom-call(s32[1]{0:T(128)} %bitcast.core_ref.refs_0_.refs_1_, ...), custom_call_target="tpu_custom_call" | custom-call | flops 12079595520 | bytes 33030144 | tf_op jit(solution)/shard_map/layer_forward/pallas_call | solution.py:306
  128.1 13.1 %collective-permute-done.6.refs_4_ = bf16[1040,384]{1,0:T(8,128)(2,1)S(1)} collective-permute-done((bf16[1040,384]{1,0:T(8,128)(2,1)S(1)}, bf16[1040,384]{1,0:T(8,128)(2,1)S(1)}, u32[]{:S(2)}, u32[]{:S(2)}) %collective-permute-start.6) | collective-permute-done | bytes 798752 | tf_op jit(solution)/shard_map/ppermute | solution.py:741
  146.8 24.6 %layer_forward.3 = (bf16[1024,768]{1,0:T(8,128)(2,1)S(1)}, bf16[1024,384]{1,0:T(8,128)(2,1)}, bf16[1024,384]{1,0:T(8,128)(2,1)}, bf16[1024,768]{1,0:T(8,128)(2,1...) custom-call(s32[1]{0:T(128)} %bitcast.core_ref.refs_0_.refs_1_, ...), custom_call_target="tpu_custom_call" | custom-call | flops 12079595520 | bytes 33030144 | tf_op jit(solution)/shard_map/layer_forward/pallas_call | solution.py:306
  175.1 20.4 %layer_backward.2 = (f32[1024,768]{1,0:T(8,128)S(1)}, bf16[1024,768]{1,0:T(8,128)(2,1)S(1)}, bf16[1024,3072]{1,0:T(8,128)(2,1)S(1)}, bf16[1024,384]{1,0:T(8,128)...) custom-call(bf16[1024,768]{1,0:T(8,128)(2,1)S(1)} %convolution_convert_fusion.2.refs_0_, ...), custom_call_target="tpu_custom_call" | custom-call | flops 12079595520 | bytes 33030144 | tf_op jit(solution)/shard_map/layer_backward/pallas_call | solution.py:400
  208.9 2.8 copy-done.10
  211.7 4.8 weight_grad.8
  216.9 4.9 weight_grad.9
  228.3 3.8 weight_grad.10
  233.1 4.0 weight_grad.11
  237.2 3.4 convolution_convert_fusion.1
  248.7 23.2 %layer_backward.3 = (f32[1024,768]{1,0:T(8,128)S(1)}, bf16[1024,768]{1,0:T(8,128)(2,1)S(1)}, bf16[1024,3072]{1,0:T(8,128)(2,1)}, bf16[1024,384]{1,0:T(8,128)(2,1...) custom-call(f32[1024,768]{1,0:T(8,128)S(1)} %copy-done.50, ...), custom_call_target="tpu_custom_call" | custom-call | flops 12079595520 | bytes 33030144 | tf_op jit(solution)/shard_map/layer_backward/pallas_call | solution.py:400
  277.2 11.9 %collective-permute-done.20 = bf16[384,768]{1,0:T(8,128)(2,1)S(1)} collective-permute-done((bf16[384,768]{1,0:T(8,128)(2,1)}, bf16[384,768]{1,0:T(8,128)(2,1)S(1)}, u32[]{:S(2)}, u32[]{:S(2)}) %collective-permute-start.20) | collective-permute-done | bytes 589856 | tf_op jit(solution)/shard_map/ppermute | solution.py:582
  289.1 12.6 %collective-permute-done.18 = bf16[384,768]{1,0:T(8,128)(2,1)S(1)} collective-permute-done((bf16[384,768]{1,0:T(8,128)(2,1)S(1)}, bf16[384,768]{1,0:T(8,128)(2,1)S(1)}, u32[]{:S(2)}, u32[]{:S(2)}) %collective-permute-start.18) | collective-permute-done | bytes 589856 | tf_op jit(solution)/shard_map/ppermute | solution.py:582
  302.7 2.8 copy-done.5
  305.5 2.8 copy-done.6
  308.3 4.8 weight_grad.12
  314.1 5.0 weight_grad.13
  332.0 3.9 weight_grad.14
  338.1 3.8 weight_grad.15
  342.0 4.0 transform_part.7.refs_1_
  352.4 6.5 %collective-permute-done.23.refs_4_ = bf16[1040,384]{1,0:T(8,128)(2,1)} collective-permute-done((bf16[1040,384]{1,0:T(8,128)(2,1)}, bf16[1040,384]{1,0:T(8,128)(2,1)}, u32[]{:S(2)}, u32[]{:S(2)}) %collective-permute-start.23) | collective-permute-done | bytes 798752 | tf_op jit(solution)/shard_map/ppermute | solution.py:741
  363.6 3.6 transform_rest.7.refs_1_.refs_2_
  367.2 7.9 %collective-permute-start.26 = (bf16[1040,384]{1,0:T(8,128)(2,1)S(1)}, bf16[1040,384]{1,0:T(8,128)(2,1)S(1)}, u32[]{:S(2)}, u32[]{:S(2)}) collective-permute-start(bf16[1040,384]{1,0:T(8,128)(2,1)S(1)} %transform_rest.7.refs_1_.refs_2_), channel_id=1, source_target_pairs={{0,16},{16,0},{1,17},{17,1},{2,18},{18,2},{3,19},{19,3},{4,20},{20... | collective-permute-start | bytes 2396168 | tf_op jit(solution)/shard_map/ppermute | solution.py:27
  375.1 3.0 collective-permute-start.27
  384.7 3.4 convolution_convert_fusion
  388.6 14.9 %collective-permute-done.28 = bf16[2,96,768]{2,1,0:T(8,128)(2,1)S(1)} collective-permute-done((bf16[2,96,768]{2,1,0:T(8,128)(2,1)S(1)}, bf16[2,96,768]{2,1,0:T(8,128)(2,1)S(1)}, u32[]{:S(2)}, u32[]{:S(2)}) %collective-permute-start.28) | collective-permute-done | bytes 294944 | tf_op jit(solution)/shard_map/ppermute | solution.py:585
  403.7 3.0 collective-permute-start.31
  409.9 3.9 collective-permute-done.34
  415.6 16.6 %collective-permute-done.31 = bf16[2,96,768]{2,1,0:T(8,128)(2,1)} collective-permute-done((bf16[2,96,768]{2,1,0:T(8,128)(2,1)S(1)}, bf16[2,96,768]{2,1,0:T(8,128)(2,1)}, u32[]{:S(2)}, u32[]{:S(2)}) %collective-permute-start.31) | collective-permute-done | bytes 294944 | tf_op jit(solution)/shard_map/ppermute | solution.py:585
  440.7 8.9 %collective-permute-done.40 = bf16[384,768]{1,0:T(8,128)(2,1)} collective-permute-done((bf16[384,768]{1,0:T(8,128)(2,1)S(1)}, bf16[384,768]{1,0:T(8,128)(2,1)}, u32[]{:S(2)}, u32[]{:S(2)}) %collective-permute-start.40) | collective-permute-done | bytes 589856 | tf_op jit(solution)/shard_map/ppermute | solution.py:582
  456.4 3.3 collective-permute-start.36
  461.9 24.7 %collective-permute-done.44 = bf16[2,96,768]{2,1,0:T(8,128)(2,1)S(1)} collective-permute-done((bf16[2,96,768]{2,1,0:T(8,128)(2,1)S(1)}, bf16[2,96,768]{2,1,0:T(8,128)(2,1)S(1)}, u32[]{:S(2)}, u32[]{:S(2)}) %collective-permute-start.44) | collective-permute-done | bytes 294944 | tf_op jit(solution)/shard_map/ppermute | solution.py:585
  489.4 7.8 %collective-permute-done.52 = bf16[4,96,768]{2,1,0:T(8,128)(2,1)S(1)} collective-permute-done((bf16[4,96,768]{2,1,0:T(8,128)(2,1)S(1)}, bf16[4,96,768]{2,1,0:T(8,128)(2,1)S(1)}, u32[]{:S(2)}, u32[]{:S(2)}) %collective-permute-start.52) | collective-permute-done | bytes 589856 | tf_op jit(solution)/shard_map/ppermute | solution.py:582
  502.3 4.0 collective-permute-start.49
  509.9 13.0 %collective-permute-start.50 = (bf16[2,96,768]{2,1,0:T(8,128)(2,1)S(1)}, bf16[2,96,768]{2,1,0:T(8,128)(2,1)S(1)}, u32[]{:S(2)}, u32[]{:S(2)}) collective-permute-start(bf16[2,96,768]{2,1,0:T(8,128)(2,1)S(1)} %add_convert_fusion.9), channel_id=1, source_target_pairs={{0,2},{1,3},{2,0},{3,1},{4,6},{5,7},{6,4},{7,5},{8,10},{9,11},{10,... | collective-permute-start | bytes 884744 | tf_op jit(solution)/shard_map/ppermute | solution.py:585
  525.5 22.3 %collective-permute-done.50 = bf16[2,96,768]{2,1,0:T(8,128)(2,1)S(1)} collective-permute-done((bf16[2,96,768]{2,1,0:T(8,128)(2,1)S(1)}, bf16[2,96,768]{2,1,0:T(8,128)(2,1)S(1)}, u32[]{:S(2)}, u32[]{:S(2)}) %collective-permute-start.50) | collective-permute-done | bytes 294944 | tf_op jit(solution)/shard_map/ppermute | solution.py:585
  551.6 10.8 %collective-permute-done.59 = bf16[4,96,768]{2,1,0:T(8,128)(2,1)S(1)} collective-permute-done((bf16[4,96,768]{2,1,0:T(8,128)(2,1)S(1)}, bf16[4,96,768]{2,1,0:T(8,128)(2,1)S(1)}, u32[]{:S(2)}, u32[]{:S(2)}) %collective-permute-start.59) | collective-permute-done | bytes 589856 | tf_op jit(solution)/shard_map/ppermute | solution.py:582
  565.8 10.3 %collective-permute-done.62 = bf16[4,96,768]{2,1,0:T(8,128)(2,1)S(1)} collective-permute-done((bf16[4,96,768]{2,1,0:T(8,128)(2,1)S(1)}, bf16[4,96,768]{2,1,0:T(8,128)(2,1)S(1)}, u32[]{:S(2)}, u32[]{:S(2)}) %collective-permute-start.62) | collective-permute-done | bytes 589856 | tf_op jit(solution)/shard_map/ppermute | solution.py:582
  576.1 12.6 %collective-permute-done.63 = bf16[4,96,768]{2,1,0:T(8,128)(2,1)S(1)} collective-permute-done((bf16[4,96,768]{2,1,0:T(8,128)(2,1)S(1)}, bf16[4,96,768]{2,1,0:T(8,128)(2,1)S(1)}, u32[]{:S(2)}, u32[]{:S(2)}) %collective-permute-start.63) | collective-permute-done | bytes 589856 | tf_op jit(solution)/shard_map/ppermute | solution.py:582
  589.8 3.9 collective-permute-start.64
  595.0 5.9 collective-permute-done.64.b_ref
  600.9 7.6 %write_weights.1 = (f32[1,768,3072]{2,1,0:T(8,128)}, f32[1,3072,768]{2,1,0:T(8,128)}) custom-call(s32[3]{0:T(128)S(1)} %pad_add_fusion.2.s, bf16[4,2,4,96,768]{4,3,2,1,0:T(8,128)(2,1)S(1)} %pad_maximum_fusion.1.a_ref, bf16[4,2,4,96,768]{4,3,2,1,0:T(8,128)(2,1)S(1)} %collective-permute-done.64.b_ref, ...), custom_call_target="tpu_custom_call" | custom-call | bytes 28311552 | tf_op jit(solution)/shard_map/write_weights/pallas_call | solution.py:513
  (398 shorter events, 162.9 us)
Async XLA Ops:
  7.2 81.5 %all-gather.3.cloned.1.call-start = ((), (), s32[]{:S(2)}) async-start(), calls=%async_computation | async-start | bytes 14155776 | tf_op jit(solution)/shard_map/all_gather | solution.py:731
  7.9 80.7 %all-gather.5.cloned.1.call-start = ((), (), s32[]{:S(2)}) async-start(), calls=%async_computation.1 | async-start | bytes 14155776 | tf_op jit(solution)/shard_map/all_gather | solution.py:732
  11.2 14.9 %collective-permute-start = (bf16[1024,768]{1,0:T(8,128)(2,1)}, bf16[1024,768]{1,0:T(8,128)(2,1)}, u32[]{:S(2)}, u32[]{:S(2)}) collective-permute-start(bf16[1024,768]{1,0:T(8,128)(2,1)} %select_bitcast_fusion.2), channel_id=1, source_target_pairs={{16,3},{17,2},{2,17},{3,16},{20,7},{21,6},{6,21},{7,20},{24,11},{2... | collective-permute-start | bytes 4718600 | tf_op jit(solution)/shard_map/ppermute | solution.py:704
  13.3 50.7 %collective-permute-start.4 = (f32[6912]{0:T(1024)S(1)}, f32[6912]{0:T(1024)S(1)}, u32[]{:S(2)}, u32[]{:S(2)}) collective-permute-start(f32[6912]{0:T(1024)S(1)} %constant_dynamic-update-slice_fusion), channel_id=1, source_target_pairs={{0,16},{16,0},{1,17},{17,1},{2,18},{18,2},{3,19},{19,3},{4,20},{20... | collective-permute-start | bytes 82952 | tf_op jit(solution)/shard_map/ppermute | solution.py:27
  30.2 14.5 %collective-permute-start.1 = (bf16[1024,384]{1,0:T(8,128)(2,1)S(1)}, bf16[1024,384]{1,0:T(8,128)(2,1)S(1)}, u32[]{:S(2)}, u32[]{:S(2)}) collective-permute-start(bf16[1024,384]{1,0:T(8,128)(2,1)S(1)} %get-tuple-element.229), channel_id=1, source_target_pairs={{0,16},{16,0},{1,17},{17,1},{2,18},{18,2},{3,19},{19,3},{4,20},{20... | collective-permute-start | bytes 2359304 | tf_op jit(solution)/shard_map/ppermute | solution.py:27
  45.0 33.8 %collective-permute-start.2 = (bf16[1040,384]{1,0:T(8,128)(2,1)S(1)}, bf16[1040,384]{1,0:T(8,128)(2,1)S(1)}, u32[]{:S(2)}, u32[]{:S(2)}) collective-permute-start(bf16[1040,384]{1,0:T(8,128)(2,1)S(1)} %fold_spectra.4.part_ref), channel_id=1, source_target_pairs={{0,1},{1,0},{3,2},{2,3},{4,5},{5,4},{7,6},{6,7},{8,9},{9,8},{11,10... | collective-permute-start | bytes 2396168 | tf_op jit(solution)/shard_map/ppermute | solution.py:741
  85.8 39.6 %collective-permute-start.7 = (bf16[1024,768]{1,0:T(8,128)(2,1)}, bf16[1024,768]{1,0:T(8,128)(2,1)}, u32[]{:S(2)}, u32[]{:S(2)}) collective-permute-start(bf16[1024,768]{1,0:T(8,128)(2,1)} %get-tuple-element.450), channel_id=1, source_target_pairs={{16,3},{17,2},{2,17},{3,16},{20,7},{21,6},{6,21},{7,20},{24,11},{2... | collective-permute-start | bytes 4718600 | tf_op jit(solution)/shard_map/ppermute | solution.py:704
  122.2 19.1 %collective-permute-start.6 = (bf16[1040,384]{1,0:T(8,128)(2,1)S(1)}, bf16[1040,384]{1,0:T(8,128)(2,1)S(1)}, u32[]{:S(2)}, u32[]{:S(2)}) collective-permute-start(bf16[1040,384]{1,0:T(8,128)(2,1)S(1)} %fold_spectra.5.part_ref), channel_id=1, source_target_pairs={{0,1},{1,0},{3,2},{2,3},{4,5},{5,4},{7,6},{6,7},{8,9},{9,8},{11,10... | collective-permute-start | bytes 2396168 | tf_op jit(solution)/shard_map/ppermute | solution.py:741
  222.1 19.0 %collective-permute-start.12 = (bf16[1040,384]{1,0:T(8,128)(2,1)S(1)}, bf16[1040,384]{1,0:T(8,128)(2,1)S(1)}, u32[]{:S(2)}, u32[]{:S(2)}) collective-permute-start(bf16[1040,384]{1,0:T(8,128)(2,1)S(1)} %fold_spectra.6.part_ref), channel_id=1, source_target_pairs={{0,1},{1,0},{3,2},{2,3},{4,5},{5,4},{7,6},{6,7},{8,9},{9,8},{11,10... | collective-permute-start | bytes 2396168 | tf_op jit(solution)/shard_map/ppermute | solution.py:741
  244.7 57.0 %collective-permute-start.19 = (bf16[2,384,768]{2,1,0:T(8,128)(2,1)S(1)}, bf16[2,384,768]{2,1,0:T(8,128)(2,1)}, u32[]{:S(2)}, u32[]{:S(2)}) collective-permute-start(bf16[2,384,768]{2,1,0:T(8,128)(2,1)S(1)} %copy-done.44), channel_id=1, source_target_pairs={{0,8},{4,12},{8,0},{12,4},{1,9},{5,13},{9,1},{13,5},{2,10},{6,14},... | collective-permute-start | bytes 3538952 | tf_op jit(solution)/shard_map/ppermute | solution.py:582
  274.0 15.1 %collective-permute-start.20 = (bf16[384,768]{1,0:T(8,128)(2,1)}, bf16[384,768]{1,0:T(8,128)(2,1)S(1)}, u32[]{:S(2)}, u32[]{:S(2)}) collective-permute-start(bf16[384,768]{1,0:T(8,128)(2,1)} %slice_bitcast_fusion.2), channel_id=1, source_target_pairs={{0,4},{4,0},{8,12},{12,8},{1,5},{5,1},{9,13},{13,9},{2,6},{6,2},{1... | collective-permute-start | bytes 1769480 | tf_op jit(solution)/shard_map/ppermute | solution.py:582
  275.3 26.4 %collective-permute-start.18 = (bf16[384,768]{1,0:T(8,128)(2,1)S(1)}, bf16[384,768]{1,0:T(8,128)(2,1)S(1)}, u32[]{:S(2)}, u32[]{:S(2)}) collective-permute-start(bf16[384,768]{1,0:T(8,128)(2,1)S(1)} %slice_bitcast_fusion.3), channel_id=1, source_target_pairs={{0,4},{4,0},{8,12},{12,8},{1,5},{5,1},{9,13},{13,9},{2,6},{6,2},{1... | collective-permute-start | bytes 1769480 | tf_op jit(solution)/shard_map/ppermute | solution.py:582
  313.1 14.7 %collective-permute-start.22 = (bf16[2,768,768]{2,1,0:T(8,128)(2,1)}, bf16[2,768,768]{2,1,0:T(8,128)(2,1)S(1)}, u32[]{:S(2)}, u32[]{:S(2)}) collective-permute-start(bf16[2,768,768]{2,1,0:T(8,128)(2,1)} %weight_grad.12), channel_id=1, source_target_pairs={{0,16},{16,0},{1,17},{17,1},{2,18},{18,2},{3,19},{19,3},{4,20},{20... | collective-permute-start | bytes 7077896 | tf_op jit(solution)/shard_map/ppermute | solution.py:27
  319.2 17.7 %collective-permute-start.21 = (bf16[2,768,768]{2,1,0:T(8,128)(2,1)}, bf16[2,768,768]{2,1,0:T(8,128)(2,1)S(1)}, u32[]{:S(2)}, u32[]{:S(2)}) collective-permute-start(bf16[2,768,768]{2,1,0:T(8,128)(2,1)} %weight_grad.13), channel_id=1, source_target_pairs={{0,16},{16,0},{1,17},{17,1},{2,18},{18,2},{3,19},{19,3},{4,20},{20... | collective-permute-start | bytes 7077896 | tf_op jit(solution)/shard_map/ppermute | solution.py:27
  320.7 25.3 %collective-permute-start.13 = (bf16[1024,384]{1,0:T(8,128)(2,1)}, bf16[1024,384]{1,0:T(8,128)(2,1)}, u32[]{:S(2)}, u32[]{:S(2)}) collective-permute-start(bf16[1024,384]{1,0:T(8,128)(2,1)} %get-tuple-element.464), channel_id=1, source_target_pairs={{0,16},{16,0},{1,17},{17,1},{2,18},{18,2},{3,19},{19,3},{4,20},{20... | collective-permute-start | bytes 2359304 | tf_op jit(solution)/shard_map/ppermute | solution.py:27
  321.2 25.6 %collective-permute-start.14 = (bf16[1024,384]{1,0:T(8,128)(2,1)}, bf16[1024,384]{1,0:T(8,128)(2,1)}, u32[]{:S(2)}, u32[]{:S(2)}) collective-permute-start(bf16[1024,384]{1,0:T(8,128)(2,1)} %get-tuple-element.465), channel_id=1, source_target_pairs={{16,3},{17,2},{2,1},{3,0},{20,7},{21,6},{6,5},{7,4},{24,11},{25,10... | collective-permute-start | bytes 2359304 | tf_op jit(solution)/shard_map/ppermute | solution.py:715
  322.8 24.1 %collective-permute-start.15 = (bf16[1024,384]{1,0:T(8,128)(2,1)}, bf16[1024,384]{1,0:T(8,128)(2,1)}, u32[]{:S(2)}, u32[]{:S(2)}) collective-permute-start(bf16[1024,384]{1,0:T(8,128)(2,1)} %get-tuple-element.462), channel_id=1, source_target_pairs={{16,19},{17,18},{2,17},{3,16},{20,23},{21,22},{6,21},{7,20},{24,27... | collective-permute-start | bytes 2359304 | tf_op jit(solution)/shard_map/ppermute | solution.py:716
  329.2 20.3 %collective-permute-start.24 = (bf16[384,768]{1,0:T(8,128)(2,1)S(1)}, bf16[384,768]{1,0:T(8,128)(2,1)}, u32[]{:S(2)}, u32[]{:S(2)}) collective-permute-start(bf16[384,768]{1,0:T(8,128)(2,1)S(1)} %copy-done.68), channel_id=1, source_target_pairs={{0,8},{4,12},{8,0},{12,4},{1,9},{5,13},{9,1},{13,5},{2,10},{6,14},... | collective-permute-start | bytes 1769480 | tf_op jit(solution)/shard_map/ppermute | solution.py:582
  367.2 13.8 %collective-permute-start.26 = (bf16[1040,384]{1,0:T(8,128)(2,1)S(1)}, bf16[1040,384]{1,0:T(8,128)(2,1)S(1)}, u32[]{:S(2)}, u32[]{:S(2)}) collective-permute-start(bf16[1040,384]{1,0:T(8,128)(2,1)S(1)} %transform_rest.7.refs_1_.refs_2_), channel_id=1, source_target_pairs={{0,16},{16,0},{1,17},{17,1},{2,18},{18,2},{3,19},{19,3},{4,20},{20... | collective-permute-start | bytes 2396168 | tf_op jit(solution)/shard_map/ppermute | solution.py:27
  378.1 25.3 %collective-permute-start.28 = (bf16[2,96,768]{2,1,0:T(8,128)(2,1)S(1)}, bf16[2,96,768]{2,1,0:T(8,128)(2,1)S(1)}, u32[]{:S(2)}, u32[]{:S(2)}) collective-permute-start(bf16[2,96,768]{2,1,0:T(8,128)(2,1)S(1)} %get-tuple-element.473), channel_id=1, source_target_pairs={{0,2},{1,3},{2,0},{3,1},{4,6},{5,7},{6,4},{7,5},{8,10},{9,11},{10,... | collective-permute-start | bytes 884744 | tf_op jit(solution)/shard_map/ppermute | solution.py:585
  378.1 25.3 %collective-permute-start.29 = (bf16[2,96,768]{2,1,0:T(8,128)(2,1)S(1)}, bf16[2,96,768]{2,1,0:T(8,128)(2,1)S(1)}, u32[]{:S(2)}, u32[]{:S(2)}) collective-permute-start(bf16[2,96,768]{2,1,0:T(8,128)(2,1)S(1)} %get-tuple-element.470), channel_id=1, source_target_pairs={{0,3},{1,0},{2,1},{3,2},{4,7},{5,4},{6,5},{7,6},{8,11},{9,8},{10,9... | collective-permute-start | bytes 884744 | tf_op jit(solution)/shard_map/ppermute | solution.py:585
  379.8 26.9 %collective-permute-start.35 = (bf16[384,768]{1,0:T(8,128)(2,1)}, bf16[384,768]{1,0:T(8,128)(2,1)}, u32[]{:S(2)}, u32[]{:S(2)}) collective-permute-start(bf16[384,768]{1,0:T(8,128)(2,1)} %slice_bitcast_fusion), channel_id=1, source_target_pairs={{0,4},{4,0},{8,12},{12,8},{1,5},{5,1},{9,13},{13,9},{2,6},{6,2},{1... | collective-permute-start | bytes 1769480 | tf_op jit(solution)/shard_map/ppermute | solution.py:582
  381.0 27.3 %collective-permute-start.33 = (bf16[384,768]{1,0:T(8,128)(2,1)}, bf16[384,768]{1,0:T(8,128)(2,1)}, u32[]{:S(2)}, u32[]{:S(2)}) collective-permute-start(bf16[384,768]{1,0:T(8,128)(2,1)} %slice_bitcast_fusion.1), channel_id=1, source_target_pairs={{0,4},{4,0},{8,12},{12,8},{1,5},{5,1},{9,13},{13,9},{2,6},{6,2},{1... | collective-permute-start | bytes 1769480 | tf_op jit(solution)/shard_map/ppermute | solution.py:582
  388.1 25.7 %collective-permute-start.34 = (bf16[2,384,768]{2,1,0:T(8,128)(2,1)S(1)}, bf16[2,384,768]{2,1,0:T(8,128)(2,1)}, u32[]{:S(2)}, u32[]{:S(2)}) collective-permute-start(bf16[2,384,768]{2,1,0:T(8,128)(2,1)S(1)} %copy-done.42), channel_id=1, source_target_pairs={{0,8},{4,12},{8,0},{12,4},{1,9},{5,13},{9,1},{13,5},{2,10},{6,14},... | collective-permute-start | bytes 3538952 | tf_op jit(solution)/shard_map/ppermute | solution.py:582
  403.7 28.6 %collective-permute-start.31 = (bf16[2,96,768]{2,1,0:T(8,128)(2,1)S(1)}, bf16[2,96,768]{2,1,0:T(8,128)(2,1)}, u32[]{:S(2)}, u32[]{:S(2)}) collective-permute-start(bf16[2,96,768]{2,1,0:T(8,128)(2,1)S(1)} %add_convert_fusion.10), channel_id=1, source_target_pairs={{0,2},{1,3},{2,0},{3,1},{4,6},{5,7},{6,4},{7,5},{8,10},{9,11},{10,... | collective-permute-start | bytes 884744 | tf_op jit(solution)/shard_map/ppermute | solution.py:585
  406.8 25.5 %collective-permute-start.32 = (bf16[2,96,768]{2,1,0:T(8,128)(2,1)S(1)}, bf16[2,96,768]{2,1,0:T(8,128)(2,1)S(1)}, u32[]{:S(2)}, u32[]{:S(2)}) collective-permute-start(bf16[2,96,768]{2,1,0:T(8,128)(2,1)S(1)} %add_convert_fusion.10), channel_id=1, source_target_pairs={{0,3},{1,0},{2,1},{3,2},{4,7},{5,4},{6,5},{7,6},{8,11},{9,8},{10,9... | collective-permute-start | bytes 884744 | tf_op jit(solution)/shard_map/ppermute | solution.py:585
  408.3 28.1 %collective-permute-start.41 = (f32[2,6912]{1,0:T(2,128)S(1)}, f32[2,6912]{1,0:T(2,128)S(1)}, u32[]{:S(2)}, u32[]{:S(2)}) collective-permute-start(f32[2,6912]{1,0:T(2,128)S(1)} %pad_maximum_fusion.8), channel_id=1, source_target_pairs={{0,16},{16,0},{1,17},{17,1},{2,18},{18,2},{3,19},{19,3},{4,20},{20... | collective-permute-start | bytes 165896 | tf_op jit(solution)/shard_map/ppermute | solution.py:826
  415.1 34.5 %collective-permute-start.39 = (bf16[384,768]{1,0:T(8,128)(2,1)S(1)}, bf16[384,768]{1,0:T(8,128)(2,1)S(1)}, u32[]{:S(2)}, u32[]{:S(2)}) collective-permute-start(bf16[384,768]{1,0:T(8,128)(2,1)S(1)} %fusion.14), channel_id=1, source_target_pairs={{0,8},{4,12},{8,0},{12,4},{1,9},{5,13},{9,1},{13,5},{2,10},{6,14},... | collective-permute-start | bytes 1769480 | tf_op jit(solution)/shard_map/ppermute | solution.py:582
  452.4 34.2 %collective-permute-start.44 = (bf16[2,96,768]{2,1,0:T(8,128)(2,1)S(1)}, bf16[2,96,768]{2,1,0:T(8,128)(2,1)S(1)}, u32[]{:S(2)}, u32[]{:S(2)}) collective-permute-start(bf16[2,96,768]{2,1,0:T(8,128)(2,1)S(1)} %get-tuple-element.469), channel_id=1, source_target_pairs={{0,2},{1,3},{2,0},{3,1},{4,6},{5,7},{6,4},{7,5},{8,10},{9,11},{10,... | collective-permute-start | bytes 884744 | tf_op jit(solution)/shard_map/ppermute | solution.py:585
  453.5 34.1 %collective-permute-start.45 = (bf16[2,96,768]{2,1,0:T(8,128)(2,1)S(1)}, bf16[2,96,768]{2,1,0:T(8,128)(2,1)S(1)}, u32[]{:S(2)}, u32[]{:S(2)}) collective-permute-start(bf16[2,96,768]{2,1,0:T(8,128)(2,1)S(1)} %get-tuple-element.466), channel_id=1, source_target_pairs={{0,3},{1,0},{2,1},{3,2},{4,7},{5,4},{6,5},{7,6},{8,11},{9,8},{10,9... | collective-permute-start | bytes 884744 | tf_op jit(solution)/shard_map/ppermute | solution.py:585
  456.4 42.1 %collective-permute-start.36 = (bf16[1024,384]{1,0:T(8,128)(2,1)S(1)}, bf16[1024,384]{1,0:T(8,128)(2,1)S(1)}, u32[]{:S(2)}, u32[]{:S(2)}) collective-permute-start(bf16[1024,384]{1,0:T(8,128)(2,1)S(1)} %get-tuple-element.460), channel_id=1, source_target_pairs={{0,16},{16,0},{1,17},{17,1},{2,18},{18,2},{3,19},{19,3},{4,20},{20... | collective-permute-start | bytes 2359304 | tf_op jit(solution)/shard_map/ppermute | solution.py:27
  459.7 39.2 %collective-permute-start.37 = (bf16[1024,384]{1,0:T(8,128)(2,1)S(1)}, bf16[1024,384]{1,0:T(8,128)(2,1)S(1)}, u32[]{:S(2)}, u32[]{:S(2)}) collective-permute-start(bf16[1024,384]{1,0:T(8,128)(2,1)S(1)} %get-tuple-element.461), channel_id=1, source_target_pairs={{16,3},{17,2},{2,1},{3,0},{20,7},{21,6},{6,5},{7,4},{24,11},{25,10... | collective-permute-start | bytes 2359304 | tf_op jit(solution)/shard_map/ppermute | solution.py:715
  460.5 28.5 %collective-permute-start.53 = (bf16[4,96,768]{2,1,0:T(8,128)(2,1)S(1)}, bf16[4,96,768]{2,1,0:T(8,128)(2,1)S(1)}, u32[]{:S(2)}, u32[]{:S(2)}) collective-permute-start(bf16[4,96,768]{2,1,0:T(8,128)(2,1)S(1)} %pad_maximum_fusion.5), channel_id=1, source_target_pairs={{0,4},{4,0},{8,12},{12,8},{1,5},{5,1},{9,13},{13,9},{2,6},{6,2},{1... | collective-permute-start | bytes 1769480 | tf_op jit(solution)/shard_map/ppermute | solution.py:582
  487.6 14.6 %collective-permute-start.38 = (bf16[1024,384]{1,0:T(8,128)(2,1)S(1)}, bf16[1024,384]{1,0:T(8,128)(2,1)S(1)}, u32[]{:S(2)}, u32[]{:S(2)}) collective-permute-start(bf16[1024,384]{1,0:T(8,128)(2,1)S(1)} %get-tuple-element.458), channel_id=1, source_target_pairs={{16,19},{17,18},{2,17},{3,16},{20,23},{21,22},{6,21},{7,20},{24,27... | collective-permute-start | bytes 2359304 | tf_op jit(solution)/shard_map/ppermute | solution.py:716
  489.0 20.9 %collective-permute-start.56 = (bf16[4,96,768]{2,1,0:T(8,128)(2,1)S(1)}, bf16[4,96,768]{2,1,0:T(8,128)(2,1)S(1)}, u32[]{:S(2)}, u32[]{:S(2)}) collective-permute-start(bf16[4,96,768]{2,1,0:T(8,128)(2,1)S(1)} %pad_maximum_fusion.5), channel_id=1, source_target_pairs={{0,8},{4,12},{8,0},{12,4},{1,9},{5,13},{9,1},{13,5},{2,10},{6,14},... | collective-permute-start | bytes 1769480 | tf_op jit(solution)/shard_map/ppermute | solution.py:582
  497.3 25.6 %collective-permute-start.54 = (bf16[4,96,768]{2,1,0:T(8,128)(2,1)S(1)}, bf16[4,96,768]{2,1,0:T(8,128)(2,1)S(1)}, u32[]{:S(2)}, u32[]{:S(2)}) collective-permute-start(bf16[4,96,768]{2,1,0:T(8,128)(2,1)S(1)} %pad_maximum_fusion.4), channel_id=1, source_target_pairs={{0,4},{4,0},{8,12},{12,8},{1,5},{5,1},{9,13},{13,9},{2,6},{6,2},{1... | collective-permute-start | bytes 1769480 | tf_op jit(solution)/shard_map/ppermute | solution.py:582
  498.5 25.9 %collective-permute-start.57 = (bf16[4,96,768]{2,1,0:T(8,128)(2,1)S(1)}, bf16[4,96,768]{2,1,0:T(8,128)(2,1)S(1)}, u32[]{:S(2)}, u32[]{:S(2)}) collective-permute-start(bf16[4,96,768]{2,1,0:T(8,128)(2,1)S(1)} %collective-permute-done.53), channel_id=1, source_target_pairs={{0,8},{4,12},{8,0},{12,4},{1,9},{5,13},{9,1},{13,5},{2,10},{6,14},... | collective-permute-start | bytes 1769480 | tf_op jit(solution)/shard_map/ppermute | solution.py:582
  498.9 25.5 %collective-permute-start.55 = (bf16[4,96,768]{2,1,0:T(8,128)(2,1)S(1)}, bf16[4,96,768]{2,1,0:T(8,128)(2,1)S(1)}, u32[]{:S(2)}, u32[]{:S(2)}) collective-permute-start(bf16[4,96,768]{2,1,0:T(8,128)(2,1)S(1)} %collective-permute-done.52), channel_id=1, source_target_pairs={{0,4},{4,0},{8,12},{12,8},{1,5},{5,1},{9,13},{13,9},{2,6},{6,2},{1... | collective-permute-start | bytes 1769480 | tf_op jit(solution)/shard_map/ppermute | solution.py:582
  502.3 23.2 %collective-permute-start.49 = (bf16[2,96,768]{2,1,0:T(8,128)(2,1)S(1)}, bf16[2,96,768]{2,1,0:T(8,128)(2,1)S(1)}, u32[]{:S(2)}, u32[]{:S(2)}) collective-permute-start(bf16[2,96,768]{2,1,0:T(8,128)(2,1)S(1)} %add_convert_fusion.9), channel_id=1, source_target_pairs={{0,1},{1,2},{2,3},{3,0},{4,5},{5,6},{6,7},{7,4},{8,9},{9,10},{10,1... | collective-permute-start | bytes 884744 | tf_op jit(solution)/shard_map/ppermute | solution.py:585
  509.9 37.8 %collective-permute-start.50 = (bf16[2,96,768]{2,1,0:T(8,128)(2,1)S(1)}, bf16[2,96,768]{2,1,0:T(8,128)(2,1)S(1)}, u32[]{:S(2)}, u32[]{:S(2)}) collective-permute-start(bf16[2,96,768]{2,1,0:T(8,128)(2,1)S(1)} %add_convert_fusion.9), channel_id=1, source_target_pairs={{0,2},{1,3},{2,0},{3,1},{4,6},{5,7},{6,4},{7,5},{8,10},{9,11},{10,... | collective-permute-start | bytes 884744 | tf_op jit(solution)/shard_map/ppermute | solution.py:585
  522.9 24.9 %collective-permute-start.51 = (bf16[2,96,768]{2,1,0:T(8,128)(2,1)S(1)}, bf16[2,96,768]{2,1,0:T(8,128)(2,1)S(1)}, u32[]{:S(2)}, u32[]{:S(2)}) collective-permute-start(bf16[2,96,768]{2,1,0:T(8,128)(2,1)S(1)} %add_convert_fusion.9), channel_id=1, source_target_pairs={{0,3},{1,0},{2,1},{3,2},{4,7},{5,4},{6,5},{7,6},{8,11},{9,8},{10,9... | collective-permute-start | bytes 884744 | tf_op jit(solution)/shard_map/ppermute | solution.py:585
  547.9 14.4 %collective-permute-start.59 = (bf16[4,96,768]{2,1,0:T(8,128)(2,1)S(1)}, bf16[4,96,768]{2,1,0:T(8,128)(2,1)S(1)}, u32[]{:S(2)}, u32[]{:S(2)}) collective-permute-start(bf16[4,96,768]{2,1,0:T(8,128)(2,1)S(1)} %pad_maximum_fusion.7), channel_id=1, source_target_pairs={{0,4},{4,0},{8,12},{12,8},{1,5},{5,1},{9,13},{13,9},{2,6},{6,2},{1... | collective-permute-start | bytes 1769480 | tf_op jit(solution)/shard_map/ppermute | solution.py:582
  549.3 15.0 %collective-permute-start.58 = (bf16[4,96,768]{2,1,0:T(8,128)(2,1)S(1)}, bf16[4,96,768]{2,1,0:T(8,128)(2,1)S(1)}, u32[]{:S(2)}, u32[]{:S(2)}) collective-permute-start(bf16[4,96,768]{2,1,0:T(8,128)(2,1)S(1)} %pad_maximum_fusion.6), channel_id=1, source_target_pairs={{0,8},{4,12},{8,0},{12,4},{1,9},{5,13},{9,1},{13,5},{2,10},{6,14},... | collective-permute-start | bytes 1769480 | tf_op jit(solution)/shard_map/ppermute | solution.py:582
  550.2 25.9 %collective-permute-start.62 = (bf16[4,96,768]{2,1,0:T(8,128)(2,1)S(1)}, bf16[4,96,768]{2,1,0:T(8,128)(2,1)S(1)}, u32[]{:S(2)}, u32[]{:S(2)}) collective-permute-start(bf16[4,96,768]{2,1,0:T(8,128)(2,1)S(1)} %pad_maximum_fusion.7), channel_id=1, source_target_pairs={{0,8},{4,12},{8,0},{12,4},{1,9},{5,13},{9,1},{13,5},{2,10},{6,14},... | collective-permute-start | bytes 1769480 | tf_op jit(solution)/shard_map/ppermute | solution.py:582
  550.9 25.2 %collective-permute-start.60 = (bf16[4,96,768]{2,1,0:T(8,128)(2,1)S(1)}, bf16[4,96,768]{2,1,0:T(8,128)(2,1)S(1)}, u32[]{:S(2)}, u32[]{:S(2)}) collective-permute-start(bf16[4,96,768]{2,1,0:T(8,128)(2,1)S(1)} %pad_maximum_fusion.6), channel_id=1, source_target_pairs={{0,4},{4,0},{8,12},{12,8},{1,5},{5,1},{9,13},{13,9},{2,6},{6,2},{1... | collective-permute-start | bytes 1769480 | tf_op jit(solution)/shard_map/ppermute | solution.py:582
  562.4 26.3 %collective-permute-start.63 = (bf16[4,96,768]{2,1,0:T(8,128)(2,1)S(1)}, bf16[4,96,768]{2,1,0:T(8,128)(2,1)S(1)}, u32[]{:S(2)}, u32[]{:S(2)}) collective-permute-start(bf16[4,96,768]{2,1,0:T(8,128)(2,1)S(1)} %collective-permute-done.59), channel_id=1, source_target_pairs={{0,8},{4,12},{8,0},{12,4},{1,9},{5,13},{9,1},{13,5},{2,10},{6,14},... | collective-permute-start | bytes 1769480 | tf_op jit(solution)/shard_map/ppermute | solution.py:582
  564.3 24.4 %collective-permute-start.61 = (bf16[4,96,768]{2,1,0:T(8,128)(2,1)S(1)}, bf16[4,96,768]{2,1,0:T(8,128)(2,1)S(1)}, u32[]{:S(2)}, u32[]{:S(2)}) collective-permute-start(bf16[4,96,768]{2,1,0:T(8,128)(2,1)S(1)} %collective-permute-done.58), channel_id=1, source_target_pairs={{0,4},{4,0},{8,12},{12,8},{1,5},{5,1},{9,13},{13,9},{2,6},{6,2},{1... | collective-permute-start | bytes 1769480 | tf_op jit(solution)/shard_map/ppermute | solution.py:582
  564.5 30.6 %collective-permute-start.65 = (bf16[4,2,4,96,768]{4,3,2,1,0:T(8,128)(2,1)S(1)}, bf16[4,2,4,96,768]{4,3,2,1,0:T(8,128)(2,1)S(1)}, u32[]{:S(2)}, u32[]{:S(2)}) collective-permute-start(bf16[4,2,4,96,768]{4,3,2,1,0:T(8,128)(2,1)S(1)} %pad_maximum_fusion.d_ref), channel_id=1, source_target_pairs={{0,16},{1,17},{2,18},{3,19},{4,20},{5,21},{6,22},{7,23},{8,24},{9,... | collective-permute-start | bytes 14155784 | tf_op jit(solution)/shard_map/ppermute | solution.py:834
  (109 other events, 781.7 us)
Sparse Core Ops, SparseCore 0:
  9.6 23.5 all-gather.2
  34.7 22.9 all-gather.4

commit v2 on v1

--- a/solution.py
+++ b/solution.py
@@ -12,6 +12,7 @@
 PAD = 16
 ROWS = 256
 CHUNK = 768
+COST = 64
 
 
 def product(left, right):
@@ -95,15 +96,16 @@
     return pl.BlockSpec((1, *shape), lambda i: (layer,) + (0,) * len(shape), pipeline_mode=pl.Buffered(1))
 
 
-def call(body, grid, in_specs, out_specs, out_shape, flops, moved, name, vmem):
+def call(body, grid, in_specs, out_specs, out_shape, flops, moved, name, vmem, scratch=()):
     return pl.pallas_call(
         body,
         grid=grid,
         in_specs=in_specs,
         out_specs=out_specs,
         out_shape=out_shape,
+        scratch_shapes=scratch,
         compiler_params=pltpu.CompilerParams(vmem_limit_bytes=vmem << 20),
-        cost_estimate=pl.CostEstimate(flops=flops, bytes_accessed=moved, transcendentals=0),
+        cost_estimate=pl.CostEstimate(flops=flops // COST, bytes_accessed=moved // COST, transcendentals=0),
         name=name,
     )
 
@@ -266,7 +268,7 @@
     )(x, spread)
 
 
-def forward(core, layer, x, mixed, unfold, w1, w2, b1, vec, spread):
+def forward(core, layer, x, mixed, unfold, w1, w2, b1, vec, spread, ahead):
     rows, width = x.shape
     hidden = w1.shape[2]
     half = width // 2
@@ -275,7 +277,7 @@
     factor = 1.0 / math.sqrt(width)
 
     def body(core_ref, x_ref, m0, t0, m1, t1, unfold_ref, w1_ref, w2_ref, b1_ref, vec_ref, spread_ref, *outs):
-        out_ref, own_ref, other_ref, low_ref, act_ref, slope_ref, unit1_ref, scale1_ref, unit2_ref, scale2_ref = outs
+        out_ref, low_ref, act_ref, slope_ref, unit1_ref, scale1_ref, unit2_ref, scale2_ref = outs[:8]
         mixture = mixture_tile(core_ref, m0, t0, m1, t1, unfold_ref).astype(BF).astype(F32)
         unit, scale = standardize(x_ref[...].astype(F32) + mixture)
         b2, mg, ms, og, os = (vec_ref[0, i : i + 1] for i in range(5))
@@ -298,9 +300,11 @@
         scale2_ref[...] = jnp.broadcast_to(scale, scale2_ref.shape)
         out = (unit * og + os).astype(BF)
         out_ref[...] = out
-        spectra = product(out, spread_ref[...]) * factor
-        own_ref[...] = spectra[:, :half].astype(BF)
-        other_ref[...] = spectra[:, half:].astype(BF)
+        if ahead:
+            own_ref, other_ref = outs[8:]
+            spectra = product(out, spread_ref[...]) * factor
+            own_ref[...] = spectra[:, :half].astype(BF)
+            other_ref[...] = spectra[:, half:].astype(BF)
 
     mine, theirs = mixed
     return call(
@@ -317,8 +321,6 @@
         ],
         [
             row_block(tile, width),
-            row_block(tile, half),
-            row_block(tile, half),
             row_block(tile, width),
             row_block(tile, hidden),
             row_block(tile, hidden),
@@ -326,11 +328,10 @@
             row_block(tile, 128),
             row_block(tile, width),
             row_block(tile, 128),
-        ],
+        ]
+        + [row_block(tile, half)] * (2 if ahead else 0),
         [
             like(rows, width),
-            like(rows, half),
-            like(rows, half),
             like(rows, width),
             like(rows, hidden),
             like(rows, hidden),
@@ -338,15 +339,121 @@
             like(rows, 128, dtype=F32),
             like(rows, width),
             like(rows, 128, dtype=F32),
-        ],
+        ]
+        + [like(rows, half)] * (2 if ahead else 0),
         4 * rows * width * (hidden + width),
         4 * width * hidden + 4 * rows * hidden + 14 * rows * width,
         "layer_forward",
-        34,
+        58,
     )(core, x, mine, mine, theirs, theirs, unfold, w1, w2, b1, vec, spread)
 
 
-def backward(core, layer, grad, mixed, unfold, kept, w1, w2, vec, spread):
+def backward(scalars, layer, grad, mixed, unfold, kept, w1, w2, vec, spread):
+    low, act, slope, unit1, scale1, unit2, scale2 = kept
+    rows, width = grad.shape
+    hidden = w1.shape[2]
+    half = width // 2
+    tile = min(ROWS, rows)
+    squares = hidden // width
+    factor = 1.0 / math.sqrt(width)
+    count = 0 if mixed is None else 5
+
+    def body(scalar_ref, grad_ref, *refs):
+        low_ref, act_ref, slope_ref, unit1_ref, scale1_ref, unit2_ref, scale2_ref, w1_ref, w2_ref, vec_ref, spread_ref = refs[
+            count : 11 + count
+        ]
+        gh_ref, own_ref, other_ref, wide_ref, sums_ref, *block_refs = refs[11 + count : -2]
+        in_sum, out_sum = refs[-2:]
+
+        @pl.when(pl.program_id(0) == 0)
+        def _():
+            for ref in (wide_ref, sums_ref, in_sum, out_sum):
+                ref[...] = jnp.zeros_like(ref)
+
+        grad = grad_ref[...].astype(F32)
+        if count:
+            grad = (grad + mixture_tile(scalar_ref, *refs[:count])).astype(BF).astype(F32)
+        mg, og = vec_ref[0, 1:2], vec_ref[0, 3:4]
+        unit2 = unit2_ref[...].astype(F32)
+        g_branch = standardize_back(grad * og, unit2, scale2_ref[:, :1])
+        gb = g_branch.astype(BF)
+        total = g_branch
+        for square in range(squares):
+            span = slice(square * width, (square + 1) * width)
+            g_act = contract(gb, w2_ref[0, span, :], 1, 1)
+            gp = (g_act * slope_ref[:, span].astype(F32)).astype(BF)
+            wide_ref[:, span] += jnp.sum(gp.astype(F32), axis=0, keepdims=True)
+            total = total + contract(gp, w1_ref[0, :, span], 1, 1)
+            out_sum[square] += contract(act_ref[:, span], gb, 0, 0)
+            in_sum[square] += contract(low_ref[...], gp, 0, 0)
+        unit1 = unit1_ref[...].astype(F32)
+        g_h = standardize_back(total * mg, unit1, scale1_ref[:, :1])
+        gh_ref[...] = g_h
+        for at, terms in enumerate((gb.astype(F32), total * unit1, total, grad * unit2, grad)):
+            sums_ref[at : at + 1] += jnp.sum(terms, axis=0, keepdims=True)
+        spectra = product(g_h.astype(BF), spread_ref[...]) * factor
+        own_ref[...] = spectra[:, :half].astype(BF)
+        other_ref[...] = spectra[:, half:].astype(BF)
+
+        @pl.when(pl.program_id(0) == pl.num_programs(0) - 1)
+        def _():
+            for owner in range(2):
+                part = pl.ds(pl.multiple_of((scalar_ref[0] ^ owner) * half, half), half)
+                for use in range(2):
+                    for at in range(2):
+                        ref = block_refs[2 * owner + use]
+                        ref[0, at] = out_sum[(2 * at + 1 - use) ^ scalar_ref[1], part, :].astype(BF)
+                        ref[1, at] = in_sum[(2 - 2 * use + at) ^ scalar_ref[1], part, :].astype(BF)
+
+    if count:
+        mine, theirs = mixed
+        extra = [mine, mine, theirs, theirs, unfold]
+        extra_specs = mixture_specs(rows, half, tile)
+    else:
+        extra, extra_specs = [], []
+    return call(
+        body,
+        (rows // tile,),
+        [scalar_block(), row_block(tile, width)]
+        + extra_specs
+        + [
+            row_block(tile, width),
+            row_block(tile, hidden),
+            row_block(tile, hidden),
+            row_block(tile, width),
+            row_block(tile, 128),
+            row_block(tile, width),
+            row_block(tile, 128),
+            layer_block(layer, width, hidden),
+            layer_block(layer, hidden, width),
+            layer_block(layer, 5, width),
+            whole(width, width),
+        ],
+        [
+            row_block(tile, width),
+            row_block(tile, half),
+            row_block(tile, half),
+            whole(1, hidden),
+            whole(8, width),
+        ]
+        + [whole(2, 2, half, width)] * 4,
+        [
+            like(rows, width, dtype=F32),
+            like(rows, half),
+            like(rows, half),
+            like(1, hidden, dtype=F32),
+            like(8, width, dtype=F32),
+        ]
+        + [like(2, 2, half, width)] * 4,
+        8 * rows * width * (hidden + width),
+        4 * width * hidden + 4 * rows * hidden + 14 * rows * width,
+        "layer_backward",
+        60,
+        [pltpu.VMEM((squares, width, width), F32)] * 2,
+    )(scalars, grad, *extra, low, act, slope, unit1, scale1, unit2, scale2, w1, w2, vec, spread)
+
+
+def backward_last(layer, grad, kept, w1, w2, vec, spread):
     low, act, slope, unit1, scale1, unit2, scale2 = kept
     rows, width = grad.shape
     hidden = w1.shape[2]
@@ -354,12 +461,11 @@
     tile = min(ROWS, rows)
     chunk = min(CHUNK, hidden)
     factor = 1.0 / math.sqrt(width)
-    count = 0 if mixed is None else 6
 
     def body(*refs):
         grad_ref = refs[0]
-        slope_ref, unit1_ref, scale1_ref, unit2_ref, scale2_ref, w1_ref, w2_ref, vec_ref, spread_ref = refs[1 + count : 10 + count]
-        gh_ref, gb_ref, gp_ref, own_ref, other_ref, wide_ref, sums_ref = refs[10 + count :]
+        slope_ref, unit1_ref, scale1_ref, unit2_ref, scale2_ref, w1_ref, w2_ref, vec_ref, spread_ref = refs[1:10]
+        gh_ref, gb_ref, gp_ref, own_ref, other_ref, wide_ref, sums_ref = refs[10:]
 
         @pl.when(pl.program_id(0) == 0)
         def _():
@@ -367,8 +473,6 @@
             sums_ref[...] = jnp.zeros_like(sums_ref)
 
         grad = grad_ref[...].astype(F32)
-        if count:
-            grad = (grad + mixture_tile(*refs[1 : 1 + count])).astype(BF).astype(F32)
         mg, og = vec_ref[0, 1:2], vec_ref[0, 3:4]
         unit2 = unit2_ref[...].astype(F32)
         g_branch = standardize_back(grad * og, unit2, scale2_ref[:, :1])
@@ -391,18 +495,11 @@
         own_ref[...] = spectra[:, :half].astype(BF)
         other_ref[...] = spectra[:, half:].astype(BF)
 
-    if count:
-        mine, theirs = mixed
-        extra = [core, mine, mine, theirs, theirs, unfold]
-        extra_specs = [scalar_block()] + mixture_specs(rows, half, tile)
-    else:
-        extra, extra_specs = [], []
     return call(
         body,
         (rows // tile,),
-        [row_block(tile, width)]
-        + extra_specs
-        + [
+        [
+            row_block(tile, width),
             row_block(tile, hidden),
             row_block(tile, width),
             row_block(tile, 128),
@@ -433,99 +530,100 @@
         ],
         4 * rows * width * (hidden + width),
         4 * width * hidden + 4 * rows * hidden + 14 * rows * width,
-        "layer_backward",
-        34,
-    )(grad, *extra, slope, unit1, scale1, unit2, scale2, w1, w2, vec, spread)
-
-
-def weight_grad(scalars, low, gp, act, gb, start, count, recv=None):
+        "last_backward",
+        58,
+    )(grad, slope, unit1, scale1, unit2, scale2, w1, w2, vec, spread)
+
+
+def grad_blocks(scalars, low, gp, act, gb):
     rows, width = low.shape
-
-    def body(scalar_ref, low_ref, gp_ref, act_ref, gb_ref, *refs):
-        def write(value):
-            if recv is None:
-                refs[0][0] = value.astype(BF)
-            else:
-                value = (value + refs[0][0].astype(F32)).astype(BF)
-                refs[1][0] = value[: width // 2]
-                refs[2][0] = value[width // 2 :]
-
-        @pl.when(scalar_ref[0] == 0)
+    half = width // 2
+
+    def body(scalar_ref, act_ref, gb_ref, low_ref, gp_ref, sent_ref, kept_ref):
+        outer = contract(act_ref[...], gb_ref[...], 0, 0).astype(BF)
+        inner = contract(low_ref[...], gp_ref[...], 0, 0).astype(BF)
+
+        @pl.when(pl.program_id(0) < 2)
         def _():
-            write(contract(low_ref[...], gp_ref[...], 0, 0))
-
-        @pl.when(scalar_ref[0] != 0)
+            sent_ref[0, 0] = outer
+            sent_ref[1, 0] = inner
+
+        @pl.when(pl.program_id(0) >= 2)
         def _():
-            write(contract(act_ref[...], gb_ref[...], 0, 0))
-
-    full = pl.BlockSpec((rows, width), lambda j, s: (0, 0))
-    block = pl.BlockSpec((1, width, width), lambda j, s: (j, 0, 0))
-    half = pl.BlockSpec((1, width // 2, width), lambda j, s: (j, 0, 0))
+            kept_ref[0, 0] = outer
+            kept_ref[1, 0] = inner
+
+    def out_square(i, s):
+        return ((2 * i + 1 - i // 2) % 4) ^ s[1]
+
+    def in_square(i, s):
+        return ((i + 2) % 4) ^ s[1]
+
     return pl.pallas_call(
         body,
         grid_spec=pltpu.PrefetchScalarGridSpec(
             num_scalar_prefetch=1,
-            grid=(count,),
+            grid=(4,),
             in_specs=[
-                full,
-                pl.BlockSpec((rows, width), lambda j, s: (0, jnp.where(s[0] == 0, (j + start) ^ s[1], 0))),
-                pl.BlockSpec((rows, width), lambda j, s: (0, jnp.where(s[0] == 0, 0, (j + start) ^ s[1]))),
-                full,
-            ]
-            + ([] if recv is None else [block]),
-            out_specs=block if recv is None else [half, half],
+                pl.BlockSpec((rows, half), lambda i, s: (0, 2 * out_square(i, s) + s[0])),
+                pl.BlockSpec((rows, width), lambda i, s: (0, 0)),
+                pl.BlockSpec((rows, half), lambda i, s: (0, s[0])),
+                pl.BlockSpec((rows, width), lambda i, s: (0, in_square(i, s))),
+            ],
+            out_specs=[
+                pl.BlockSpec((2, 1, half, width), lambda i, s: (0, jnp.minimum(i, 1), 0, 0)),
+                pl.BlockSpec((2, 1, half, width), lambda i, s: (0, jnp.maximum(i - 2, 0), 0, 0)),
+            ],
         ),
-        out_shape=like(count, width, width) if recv is None else [like(count, width // 2, width)] * 2,
-        compiler_params=pltpu.CompilerParams(vmem_limit_bytes=26 << 20),
-        cost_estimate=pl.CostEstimate(
-            flops=2 * rows * width * width * count, bytes_accessed=2 * rows * width * (count + 2) + 2 * width * width * count, transcendentals=0
-        ),
-        name="weight_grad",
-    )(scalars, low, gp, act, gb, *([] if recv is None else [recv]))
-
-
-def write_weights(scalars, first_mine, first_far, second_far, second_mine):
-    count, halves, slots, piece, width = first_mine.shape
-    tall = slots * piece
-
-    def body(s, a_ref, b_ref, c_ref, d_ref, in_ref, out_ref):
-        def write(source, target):
+        out_shape=[like(2, 2, half, width)] * 2,
+        compiler_params=pltpu.CompilerParams(vmem_limit_bytes=58 << 20),
+        cost_estimate=pl.CostEstimate(flops=16 * rows * width * half // COST, bytes_accessed=20 * rows * width // COST, transcendentals=0),
+        name="grad_blocks",
+    )(scalars, act, gb, low, gp)
+
+
+def write_weights(scalars, far, sources, begun=None):
+    _, slots, piece, width = sources[0][0][0].shape
+    half = slots * piece
+    flat = [array for pair in sources for source in pair for array in source]
+
+    def body(s, *refs):
+        in_ref, out_ref = refs[-2:]
+
+        def write(target, source, top):
             for slot in range(slots):
                 at = pl.multiple_of((s[2] + slots - slot) % slots * piece, piece)
-                target[0, pl.ds(at, piece), :] = source[0, 0, slot].astype(F32)
-
-        @pl.when(s[0] == 0)
-        def _():
-            write(a_ref, in_ref)
-            write(b_ref, out_ref)
-
-        @pl.when(s[0] != 0)
-        def _():
-            write(c_ref, in_ref)
-            write(d_ref, out_ref)
+                target[0, pl.ds(at + top, piece), :] = source[0, slot].astype(F32)
+
+        for core in range(2):
+
+            @pl.when(s[0] == core)
+            def _():
+                for at, top in ((0, core * half), (2, (1 - core) * half)):
+                    write(out_ref, refs[4 * core + at], top)
+                    write(in_ref, refs[4 * core + at + 1], top)
 
     def source(core):
-        return pl.BlockSpec(
-            (1, 1, slots, piece, width),
-            lambda q, h, s: (jnp.where(s[0] == core, q, 0), jnp.where(s[0] == core, h, 0), 0, 0, 0),
-        )
-
+        return pl.BlockSpec((1, slots, piece, width), lambda k, s: (jnp.where(s[0] == core, k, 0), 0, 0, 0))
+
+    extra = [] if begun is None else list(begun)
     return pl.pallas_call(
         body,
         grid_spec=pltpu.PrefetchScalarGridSpec(
             num_scalar_prefetch=1,
-            grid=(count, halves),
-            in_specs=[source(0), source(0), source(1), source(1)],
+            grid=(2,),
+            in_specs=[source(0)] * 4 + [source(1)] * 4 + [pl.BlockSpec(memory_space=pl.ANY)] * len(extra),
             out_specs=[
-                pl.BlockSpec((1, tall, width), lambda q, h, s: (0, h, q ^ s[1])),
-                pl.BlockSpec((1, tall, width), lambda q, h, s: (0, (q ^ s[1]) * halves + h, 0)),
+                pl.BlockSpec((1, width, width), lambda k, s: (0, 0, (k + 2 * far) ^ s[1])),
+                pl.BlockSpec((1, width, width), lambda k, s: (0, (2 * k + far) ^ s[1], 0)),
             ],
         ),
-        out_shape=[like(1, tall * halves, width * count, dtype=F32), like(1, tall * halves * count, width, dtype=F32)],
-        compiler_params=pltpu.CompilerParams(vmem_limit_bytes=20 << 20),
-        cost_estimate=pl.CostEstimate(flops=0, bytes_accessed=12 * width * width * count, transcendentals=0),
+        out_shape=[like(1, width, 4 * width, dtype=F32), like(1, 4 * width, width, dtype=F32)],
+        input_output_aliases={9: 0, 10: 1} if extra else {},
+        compiler_params=pltpu.CompilerParams(vmem_limit_bytes=40 << 20),
+        cost_estimate=pl.CostEstimate(flops=0, bytes_accessed=24 * width * width // COST, transcendentals=0),
         name="write_weights",
-    )(scalars, first_mine, first_far, second_far, second_mine)
+    )(scalars, *flat, *extra)
 
 
 def finish(core, g_h, mixed, unfold):
@@ -575,38 +673,41 @@
 
 class ChipSum:
     def __init__(self):
+        self.count = lax.axis_size("dp")
         self.peers = lax.axis_size("seq")
-        self.z = lax.axis_index("seq")
 
     def across(self, bit, value):
-        return lax.ppermute(value, "dp", bit_pairs(4, bit))
+        return lax.ppermute(value, "dp", bit_pairs(self.count, bit))
+
+    def sent(self, mine, theirs):
+        return (lambda a, b: [added(a[stream], b[stream]) for stream in range(2)]), (mine, theirs)
+
+    def start_first(self, sent):
+        self.first = [self.across(stream, sent[stream]) for stream in range(2)]
+
+    def first_sums(self, mine, theirs):
+        def step(a, b, *got):
+            sums = [(a[m].astype(F32) + b[m].astype(F32) + got[m].astype(F32)).astype(BF) for m in range(2)]
+            return [(part[1], part[0]) for part in sums]
+
+        return step, (mine, theirs, *self.first)
+
+    def start_second(self, sums):
+        self.second = [(sums[stream][1], self.across(1 - stream, sums[stream][0])) for stream in range(2)]
+
+    def second_sums(self):
+        def step(z, *pairs):
+            sums = [added(*pair) for pair in pairs]
+            for bit in range(2, self.count.bit_length() - 1):
+                sums = [added(part, self.across(bit, part)) for part in sums]
+            both = jnp.stack(sums)
+            both = both.reshape(2, self.peers, -1, both.shape[-1])
+            return [lax.dynamic_index_in_dim(both, (z + d) % self.peers, 1, keepdims=False) for d in range(self.peers)]
+
+        return step, (lax.axis_index("seq"), *self.second)
 
     def along(self, value, by):
         return lax.ppermute(value, "seq", [(i, (i + by) % self.peers) for i in range(self.peers)])
-
-    def start_upper(self, upper):
-        self.upper = upper
-        self.got = [self.across(0, upper[0][1]), self.across(1, upper[1])]
-
-    def start_lower(self, lower):
-        self.lower = lower
-        self.got.append(self.across(0, lower[0][1]))
-
-    def first_sums(self):
-        args = (self.upper[0], self.lower[0], self.lower[1], *self.got)
-        return (lambda u, a, b, g3, g23, g1: (added(u[0], g3), added(a[0], g1), added(b[1], g23[1]), added(b[0], g23[0]))), args
-
-    def start_second(self, sums):
-        self.kept = (sums[1], sums[3])
-        self.got = (self.across(1, sums[0]), self.across(0, sums[2]))
-
-    def second_sums(self):
-        def step(a, b, g0, g1, z):
-            both = jnp.stack([added(a, g0), added(b, g1)])
-            both = both.reshape(2, self.peers, -1, both.shape[-1])
-            return [lax.dynamic_index_in_dim(both, (z + d) % self.peers, 1, keepdims=False) for d in range(self.peers)]
-
-        return step, (*self.kept, *self.got, self.z)
 
     def start_scatter(self, pieces):
         self.kept = pieces[0]
@@ -628,22 +729,19 @@
 
         return step, (self.kept, *self.got)
 
-    def start_back(self, halves):
-        self.own = halves
-        self.near = (self.across(1, halves[0]), self.across(0, halves[1]))
-
-    def start_last(self):
-        self.far = [
-            (self.across(0, self.own[0]), self.across(0, self.near[0])),
-            (self.across(1, self.own[1]), self.across(1, self.near[1])),
-        ]
-
-    def pieces(self):
-        def step(a, b, a2, b1, a1, a3, b2, b3):
-            return jnp.stack([jnp.stack([a, b]), jnp.stack([a1, b1]), jnp.stack([a2, b2]), jnp.stack([a3, b3])])
-
-        return step, (*self.own, *self.near, *self.far[0], *self.far[1])
-
+    def start_back(self, streams):
+        self.own = streams
+        self.near = [self.across(1 - stream, streams[stream]) for stream in range(2)]
+
+    def paired(self):
+        def step(a, b, c, d):
+            return jnp.stack([a, b]), jnp.stack([c, d])
+
+        return step, (self.own[0], self.near[0], self.own[1], self.near[1])
+
+    def start_last(self, pairs):
+        self.pairs = pairs
+        self.far = [self.across(stream, pairs[stream]) for stream in range(2)]
 
 def small_hops():
     hops = []
@@ -686,43 +784,42 @@
         for d in range(1, blocks)
     ]
     in_pairs = []
-    out_pairs = ([], [])
+    out_pairs = []
     for i in range(peers):
         facing = peers - 1 - i
         source = peers + i if i < blocks else i
         in_pairs.append((source, facing if i < blocks else peers + facing))
-        out_pairs[0].append((source, facing))
-        out_pairs[1].append((source, peers + facing))
+        out_pairs.append((source, peers + facing if source < peers else facing))
 
     row_ids = lax.broadcasted_iota(jnp.int32, (rows, rows), 0)
     col_ids = lax.broadcasted_iota(jnp.int32, (rows, rows), 1)
     order = (col_ids == jnp.where(first, row_ids, (rows - row_ids) % rows)).astype(BF)
 
-    def send_in(items):
-        sent = jnp.where(low, items[1], items[0])
-        kept = jnp.where(low, items[0], items[1])
-        return kept, lax.ppermute(sent, ("pipe", "seq"), in_pairs)
+    def picked(items):
+        return jnp.where(low, items[1], items[0]), jnp.where(low, items[0], items[1])
 
     def arranged(kept, moved):
         return product(order, jnp.where(local, kept, moved)).astype(BF)
 
+    turned = z >= blocks
+    back_order = (col_ids == jnp.where(turned, (rows - row_ids) % rows, row_ids)).astype(BF)
+
     def give_start(value):
-        mine = jnp.where(first, value[:, :half], value[:, half:])
-        theirs = jnp.where(first, value[:, half:], value[:, :half])
-        return (
-            mine,
-            swap_cores(theirs),
-            lax.ppermute(value[:, :half], ("pipe", "seq"), out_pairs[0]),
-            lax.ppermute(value[:, half:], ("pipe", "seq"), out_pairs[1]),
+        return value, lax.ppermute(value, ("pipe", "seq"), out_pairs)
+
+    def give_cut(value, moved):
+        block = jnp.where(local, value, moved)
+        return jnp.where(first, block[:, :half], block[:, half:]), jnp.where(first, block[:, half:], block[:, :half])
+
+    def give_end(mine, beside):
+        near = jnp.where(local, mine, beside)
+        far = jnp.where(local, beside, mine)
+        return jnp.stack(
+            [product(back_order, part).astype(BF) for part in (jnp.where(low, near, far), jnp.where(low, far, near))]
         )
 
-    def give_end(moved):
-        mine, beside, far0, far1 = moved
-        near_part = jnp.where(local, mine, beside)
-        far_part = jnp.where(first, far0, far1)
-        return jnp.stack([jnp.where(low, near_part, far_part), jnp.where(low, far_part, near_part)])
-
-    x = arranged(*send_in(inputs))
+    sent, x = picked(inputs)
+    x = arranged(x, lax.ppermute(sent, ("pipe", "seq"), in_pairs))
     vectors = jnp.concatenate([in_bias[0], out_bias[0], mix_gain[0], mix_shift[0], out_gain[0], out_shift[0]])
     other_vectors = swap_cores(vectors)
     vectors = jnp.where(first, jnp.stack([vectors, other_vectors]), jnp.stack([other_vectors, vectors]))
@@ -736,52 +833,44 @@
 
     line = Line()
 
-    def fold(own, other):
-        folded = line(lambda a, b: fold_spectra(which, a, b), own, swap_cores(other))
-        return folded, [lax.ppermute(folded, "seq", pairs) for pairs in group_shifts]
+    def fold(own, came):
+        return line(lambda a, b: fold_spectra(which, a, b), own, came)
+
+    def spread_out(folded):
+        return [lax.ppermute(folded, "seq", pairs) for pairs in group_shifts]
 
     def part(folded):
         return line(lambda f: transform_part(cos, sin, 0, f), folded)
 
     def rest(begun, parts):
-        mixed = line(lambda a, *b: transform_rest(which, cos, sin, a, list(b), factor), begun, *parts)
-        return mixed, swap_cores(mixed)
+        return line(lambda a, *b: transform_rest(which, cos, sin, a, list(b), factor), begun, *parts)
 
     kept = []
     own, other = line(lambda v: spectra_call(which, v, spread), x)
+    cot_sent, cot_kept = line.after(picked(cotangent))
     for layer in range(2):
-        folded, parts = fold(own, other)
+        folded = fold(own, swap_cores(other))
+        parts = spread_out(folded)
         begun = part(folded)
         if layer == 1:
-            grad = line(lambda v, w: arranged(v, w), *cot)
+            grad = line(arranged, cot_kept, cot_moved)
         mixed = rest(begun, parts)
+        came = swap_cores(mixed)
         if layer == 0:
-            cot = send_in(line.after(cotangent))
-        x, own, other, *saved = line(
-            lambda v, m, l=layer: forward(which, l, v, m, unfold, w1, w2, b1, vec, spread), x, mixed
+            cot_moved = lax.ppermute(line.after(cot_sent), ("pipe", "seq"), in_pairs)
+        x, *saved = line(
+            lambda v, m, l=layer: forward(which, l, v, m, unfold, w1, w2, b1, vec, spread, l == 0), x, (mixed, came)
         )
-        kept.append(saved)
+        kept.append(saved[:7])
+        if layer == 0:
+            own, other = saved[7:]
+
+    index = lax.axis_index("dp") & 3
+    scalars = jnp.stack([core, index]).astype(jnp.int32)
 
     def back(layer, grad, mixed):
         return line(
-            lambda g, m, k: backward(which, layer, g, m, unfold, k, w1, w2, vec, spread), grad, mixed, kept[layer]
-        )
-
-    index = lax.axis_index("dp")
-    zero = jnp.zeros((), jnp.int32)
-    quick = lax.axis_size("dp") == 4 and hidden == 4 * width and (width // 2) % peers == 0
-    begin = index if quick else zero
-    to_mine = jnp.stack([core, begin]).astype(jnp.int32)
-    to_theirs = jnp.stack([1 - core, begin]).astype(jnp.int32)
-
-    def theirs(layer, start, count, gp, gb):
-        return swap_cores(
-            line(lambda t, a, c, p, b: weight_grad(t, a, p, c, b, start, count), to_theirs, *kept[layer][:2], gp, gb)
-        )
-
-    def mine(layer, start, count, gp, gb, recv):
-        return line(
-            lambda t, a, c, p, b, r: weight_grad(t, a, p, c, b, start, count, r), to_mine, *kept[layer][:2], gp, gb, recv
+            lambda g, m, k: backward(scalars, layer, g, m, unfold, k, w1, w2, vec, spread), grad, mixed, kept[layer]
         )
 
     def run(work):
@@ -790,54 +879,112 @@
     def flat_small(wide, narrow):
         return jnp.concatenate([wide.reshape(-1), narrow[:5].reshape(-1)])
 
-    sums = [ChipSum(), ChipSum()]
-    early = sums[1]
-    late = sums[0]
-    grad, gb1, gp1, own, other, wide1, narrow1 = back(1, grad, None)
-    folded, parts = fold(own, other)
-    half_count = hidden // width // 2
-    upper = theirs(1, half_count, half_count, gp1, gb1)
-    lower = theirs(1, 0, half_count, gp1, gb1)
+    late, early = ChipSum(), ChipSum()
+    to_theirs = jnp.stack([1 - core, index]).astype(jnp.int32)
+
+    def blocks_of(target, gp, gb):
+        return line(grad_blocks, target, kept[1][0], gp, kept[1][1], gb)
+
+    out_moved = give_start(x)
+    grad, gb, gp, own, other, wide1, narrow1 = line(
+        lambda g, k: backward_last(1, g, k, w1, w2, vec, spread), grad, kept[1]
+    )
+
+    came = swap_cores(other)
+    other_sent, other_kept = blocks_of(to_theirs, gp, gb)
+    folded = fold(own, came)
+
+    parts = spread_out(line.after(folded))
+    got_sent, got_kept1 = swap_cores(line.after((other_sent, other_kept)))
+    my_sent, my_kept1 = blocks_of(scalars, gp, gb)
     begun = part(folded)
-    early.start_upper(mine(1, half_count, half_count, gp1, gb1, upper))
-    early.start_lower(mine(1, 0, half_count, gp1, gb1, lower))
-    out_ready = line(lambda v: product(order, v).astype(BF), x)
     mixed = rest(begun, parts)
-    out_moved = give_start(line.after(out_ready))
-    grad, gb0, gp0, own, other, wide0, narrow0 = back(0, grad, mixed)
-    folded, parts = fold(own, other)
-    early.start_second(run(early.first_sums()))
-    upper = theirs(0, half_count, half_count, gp0, gb0)
-    lower = theirs(0, 0, half_count, gp0, gb0)
-    late.start_upper(mine(0, half_count, half_count, gp0, gb0, upper))
-    late.start_lower(mine(0, 0, half_count, gp0, gb0, lower))
+
+    came = swap_cores(mixed)
+    sent = run(early.sent(my_sent, got_sent))
+
+    early.start_first(line.after(sent))
+    grad, own, other, wide0, narrow0, my_sent, my_kept, other_sent, other_kept = back(0, grad, (mixed, came))
+
+    sums = run(early.first_sums(my_kept1, got_kept1))
+    out_mine, out_theirs = line(give_cut, *out_moved)
+
+    got_sent = swap_cores(line.after(other_sent))
+    came = swap_cores(line.after(other))
+    early.start_second(line.after(sums))
+    folded = fold(own, came)
+    sent = run(late.sent(my_sent, got_sent))
+    pieces = run(early.second_sums())
+
+    hops = iter(small_hops())
+    small = jnp.stack([flat_small(wide0, narrow0), flat_small(wide1, narrow1)])
+
+    def start_hop():
+        axis, pairs = next(hops)
+        return lax.ppermute(line.after(small), axis, pairs)
+
+    def end_hop(got):
+        return line(lambda a, b: a + b, small, got)
+
+    late.start_first(line.after(sent))
+    parts = spread_out(line.after(folded))
+    early.start_scatter(line.after(pieces))
+    got_kept0 = swap_cores(line.after(other_kept))
+    hop = start_hop()
     begun = part(folded)
-    out = line(give_end, out_moved)
-    early.start_scatter(run(early.second_sums()))
     mixed = rest(begun, parts)
-    in_ready = line(lambda g, m: product(order, finish(which, g, m, unfold)).astype(BF), grad, mixed)
-    early.start_gather(run(early.scattered()))
-    small = line(lambda *v: jnp.stack([flat_small(*v[:2]), flat_small(*v[2:])]), wide0, narrow0, wide1, narrow1)
-    hops = small_hops()
-    late.start_second(run(late.first_sums()))
-    early.start_back(run(early.gathered()))
+    piece = run(early.scattered())
+    small = end_hop(hop)
+    sums = run(late.first_sums(my_kept, got_kept0))
+
+    late.start_second(line.after(sums))
+    early.start_gather(line.after(piece))
+    out_beside, came = swap_cores(line.after((out_theirs, mixed)))
+    pieces = run(late.second_sums())
+    in_ready = line(lambda g, m: finish(which, g, m, unfold), grad, (mixed, came))
+    streams = run(early.gathered())
+
+    late.start_scatter(line.after(pieces))
+    early.start_back(line.after(streams))
+    hop = start_hop()
+    out = line(give_end, out_mine, out_beside)
+    pairs = run(early.paired())
+
+    early.start_last(line.after(pairs))
+    piece = run(late.scattered())
+    small = end_hop(hop)
+
+    late.start_gather(line.after(piece))
+    pairs_far1 = lax.ppermute(line.after(pairs), "pipe", [(0, 1)])
+    hop = start_hop()
+    streams = run(late.gathered())
+    small = end_hop(hop)
+    far1 = line.after(early.far)
+
+    streams, far1 = lax.optimization_barrier((streams, far1))
+    late.start_back(streams)
+    hop = start_hop()
+    far1_far = lax.ppermute(line.after(far1), "pipe", [(0, 1)])
     in_moved = give_start(line.after(in_ready))
-    for axis, pairs in hops[:2]:
-        small = line(lambda a, b: a + b, small, lax.ppermute(small, axis, pairs))
-    late.start_scatter(run(late.second_sums()))
-    early.start_last()
-    for axis, pairs in hops[2:]:
-        small = line(lambda a, b: a + b, small, lax.ppermute(small, axis, pairs))
-    late.start_gather(run(late.scattered()))
-    in_grad = line(give_end, in_moved)
-    early_sum = run(early.pieces())
-    to_second = lax.ppermute(early_sum, "pipe", [(0, 1)])
-    late.start_back(run(late.gathered()))
-    late.start_last()
-    late_sum = run(late.pieces())
-    to_first = lax.ppermute(late_sum, "pipe", [(1, 0)])
+    pairs0 = run(late.paired())
+    small = end_hop(hop)
+
+    late.start_last(line.after(pairs0))
+    pairs_far0 = lax.ppermute(line.after(pairs0), "pipe", [(1, 0)])
+    hop = start_hop()
     scalars = jnp.stack([core, index, z]).astype(jnp.int32)
-    g_w1, g_w2 = line(write_weights, scalars, late_sum, to_first, to_second, early_sum)
+    begun = line(lambda *v: write_weights(scalars, 0, v), (pairs0, pairs_far0), (pairs, pairs_far1))
+    far0 = line.after(late.far)
+
+    far0_far = lax.ppermute(far0, "pipe", [(1, 0)])
+    small, far0_far = lax.optimization_barrier((small, far0_far))
+    small = end_hop(hop)
+    in_mine, in_theirs = line(give_cut, *in_moved)
+    in_beside = swap_cores(line.after(in_theirs))
+    g_w1, g_w2 = line(lambda b, *v: write_weights(scalars, 1, v, b), begun, (far0, far0_far), (far1, far1_far))
+    in_grad = line(give_end, in_mine, in_beside)
+    for axis, hop in hops:
+        small = line(lambda a, b: a + b, small, lax.ppermute(small, axis, hop))
     small = jnp.where(first, small[0], small[1])
     g_b1 = small[:hidden]
     g_b2, g_mg, g_ms, g_og, g_os = (small[hidden + i * width : hidden + (i + 1) * width] for i in range(5))

time: 625 us -> 551 us (0.88)
  the two profiles are of different devices: /device:TPU:25 before, /device:TPU:0 now
where the time goes in v2:
time: 551 us; the launch traced here: 542 us
  Pallas kernels  169 us (31%)
  waiting for transfers between devices  150 us (27%)
  starting transfers between devices  110 us (20%)
  other arithmetic  49 us (9%)
  local copies, waits for them, and re-layouts  31.2 us (6%)
  matrix products  16 us (3%)
  between operations  15.8 us (3%)
    ppermute x16, waiting for transfers between devices, across(): return lax.ppermute(value, 'dp', bit_pairs(self.count, bit))  51.3 us
    ppermute x12, waiting for transfers between devices, along(): lax.ppermute(value, 'seq', [(i, (i + by) % self.peers) for i in range(sel...  50.9 us
    pallas_call x2, Pallas kernels, forward(): call(body, (rows // tile,), [scalar_block(), row_block(tile, width)] + mi...  50 us
    pallas_call x1, Pallas kernels, backward(): call(body, (rows // tile,), [scalar_block(), row_block(tile, width)] + ex...  39.3 us
    ppermute x12, starting transfers between devices, along(): lax.ppermute(value, 'seq', [(i, (i + by) % self.peers) for i in range(sel...  33.4 us
    ppermute x4, waiting for transfers between devices, spread_out(): return [lax.ppermute(folded, 'seq', pairs) for pairs in group_shifts]  26 us
    unnamed x119, local copies, waits for them, and re-layouts  24.5 us
    pallas_call x2, Pallas kernels, grad_blocks(): pl.pallas_call(body, grid_spec=pltpu.PrefetchScalarGridSpec(num_scalar_pr...  22.7 us
  transfers between devices with their start and end apart: 66, of which 30 were waited for; matrix products, arithmetic and copies ran while one was open for 11% of the time, Pallas kernels for 22%

profile of v2, /device:TPU:0, one launch (start us, length us, event | category | flops | bytes accessed | tf_op | source)
XLA Modules:
  0.0 541.6 jit_solution(14401613542737962431)
XLA Ops:
  12.2 6.4 %collective-permute-start.4 = (f32[6912]{0:T(1024)S(1)}, f32[6912]{0:T(1024)S(1)}, u32[]{:S(2)}, u32[]{:S(2)}) collective-permute-start(f32[6912]{0:T(1024)S(1)} %constant_dynamic-update-slice_fusion), channel_id=1, source_target_pairs={{0,16},{16,0},{1,17},{17,1},{2,18},{18,2},{3,19},{19,3},{4,20},{20... | collective-permute-start | bytes 82952 | tf_op jit(solution)/shard_map/ppermute | solution.py:28
  18.7 11.8 %select_convert_fusion = (bf16[768,768]{1,0:T(8,128)(2,1)}, bf16[768,768]{1,0:T(8,128)(2,1)S(1)}) fusion(s32[768]{0:T(1024)S(1)} %get-tuple-element.555, s32[768]{0:T(1024)S(1)} %get-tuple-element.556, f32[]{:T(128)S(6)} %select_n.299, pred[768]{0:T(1024)(128)(4,1)S(1)} %select_compare_fusion, f32[]{:T(128)S(6)} %neg.3), kind=kLoop, calls=%fused_computation.23 | loop fusion | flops 12976128 | bytes 2366216 | tf_op jit(solution)/shard_map/convert_element_type | solution.py:64
  30.5 4.4 fusion.24.x_ref
  34.9 2.8 spectra.1
  37.8 5.8 %collective-permute-start.1 = (bf16[1024,384]{1,0:T(8,128)(2,1)}, bf16[1024,384]{1,0:T(8,128)(2,1)S(1)}, u32[]{:S(2)}, u32[]{:S(2)}) collective-permute-start(bf16[1024,384]{1,0:T(8,128)(2,1)} %get-tuple-element.255), channel_id=1, source_target_pairs={{0,16},{16,0},{1,17},{17,1},{2,18},{18,2},{3,19},{19,3},{4,20},{20... | collective-permute-start | bytes 2359304 | tf_op jit(solution)/shard_map/ppermute | solution.py:28
  44.2 2.6 fusion.57
  47.2 17.3 %collective-permute-start.2 = (bf16[1040,384]{1,0:T(8,128)(2,1)S(1)}, bf16[1040,384]{1,0:T(8,128)(2,1)S(1)}, u32[]{:S(2)}, u32[]{:S(2)}) collective-permute-start(bf16[1040,384]{1,0:T(8,128)(2,1)S(1)} %fold_spectra.4.part_ref), channel_id=1, source_target_pairs={{0,1},{1,0},{3,2},{2,3},{4,5},{5,4},{7,6},{6,7},{8,9},{9,8},{11,10... | collective-permute-start | bytes 2396168 | tf_op jit(solution)/shard_map/ppermute | solution.py:840
  64.5 3.3 add_convert_fusion
  70.1 12.4 %collective-permute-done.2.refs_4_ = bf16[1040,384]{1,0:T(8,128)(2,1)S(1)} collective-permute-done((bf16[1040,384]{1,0:T(8,128)(2,1)S(1)}, bf16[1040,384]{1,0:T(8,128)(2,1)S(1)}, u32[]{:S(2)}, u32[]{:S(2)}) %collective-permute-start.2) | collective-permute-done | bytes 798752 | tf_op jit(solution)/shard_map/ppermute | solution.py:840
  91.2 25.6 %layer_forward.2 = (bf16[1024,768]{1,0:T(8,128)(2,1)}, bf16[1024,768]{1,0:T(8,128)(2,1)}, bf16[1024,3072]{1,0:T(8,128)(2,1)}, bf16[1024,3072]{1,0:T(8,128)(2,1)}...) custom-call(s32[1]{0:T(128)} %bitcast.core_ref.refs_0_, ...), custom_call_target="tpu_custom_call" | custom-call | flops 188743680 | bytes 516096 | tf_op jit(solution)/shard_map/layer_forward/pallas_call | solution.py:310
  116.8 3.3 collective-permute-start.5
  124.7 2.4 copy-done.3
  129.3 3.6 fusion.27.refs_0_
  132.9 11.0 %collective-permute-done.6.refs_4_ = bf16[1040,384]{1,0:T(8,128)(2,1)S(1)} collective-permute-done((bf16[1040,384]{1,0:T(8,128)(2,1)S(1)}, bf16[1040,384]{1,0:T(8,128)(2,1)S(1)}, u32[]{:S(2)}, u32[]{:S(2)}) %collective-permute-start.6) | collective-permute-done | bytes 798752 | tf_op jit(solution)/shard_map/ppermute | solution.py:840
  149.5 24.4 %layer_forward.3 = (bf16[1024,768]{1,0:T(8,128)(2,1)}, bf16[1024,768]{1,0:T(8,128)(2,1)}, bf16[1024,3072]{1,0:T(8,128)(2,1)}, bf16[1024,3072]{1,0:T(8,128)(2,1)}...) custom-call(s32[1]{0:T(128)} %bitcast.core_ref.refs_0_, ...), custom_call_target="tpu_custom_call" | custom-call | flops 188743680 | bytes 516096 | tf_op jit(solution)/shard_map/layer_forward/pallas_call | solution.py:310
  173.9 21.8 %last_backward.1 = (f32[1024,768]{1,0:T(8,128)}, bf16[1024,768]{1,0:T(8,128)(2,1)}, bf16[1024,3072]{1,0:T(8,128)(2,1)}, bf16[1024,384]{1,0:T(8,128)(2,1)}, bf16[...) custom-call(bf16[1024,768]{1,0:T(8,128)(2,1)} %fusion.27.refs_0_, ...), custom_call_target="tpu_custom_call" | custom-call | flops 188743680 | bytes 516096 | tf_op jit(solution)/shard_map/last_backward/pallas_call | solution.py:498
  196.4 11.3 %grad_blocks.2 = (bf16[2,2,384,768]{3,2,1,0:T(8,128)(2,1)}, bf16[2,2,384,768]{3,2,1,0:T(8,128)(2,1)}) custom-call(s32[2]{0:T(128)} %pad_add_fusion.1.scalar_ref, bf16[1024,3072]{1,0:T(8,128)(2,1)} %get-tuple-element.309.act_ref, bf16[1024,768]{1,0:T(8,128)(2,1)} %get-tuple-element.310.gb_ref, bf16[1024,768]{1,0:T(8,128)(2,1)} %get-tuple-element.311.low_ref, ...), custom_call_target="tpu_custom_call" | custom-call | flops 75497472 | bytes 245760 | tf_op jit(solution)/shard_map/grad_blocks/pallas_call | solution.py:562
  213.2 11.4 %grad_blocks.3 = (bf16[2,2,384,768]{3,2,1,0:T(8,128)(2,1)}, bf16[2,2,384,768]{3,2,1,0:T(8,128)(2,1)}) custom-call(s32[2]{0:T(128)} %pad_add_fusion.scalar_ref, bf16[1024,3072]{1,0:T(8,128)(2,1)} %get-tuple-element.309.act_ref, bf16[1024,768]{1,0:T(8,128)(2,1)} %get-tuple-element.310.gb_ref, bf16[1024,768]{1,0:T(8,128)(2,1)} %get-tuple-element.311.low_ref, ...), custom_call_target="tpu_custom_call" | custom-call | flops 75497472 | bytes 245760 | tf_op jit(solution)/shard_map/grad_blocks/pallas_call | solution.py:562
  224.7 2.3 copy-done.4
  229.3 2.7 collective-permute-done.13.refs_4_
  232.0 2.4 copy-done.5
  234.4 3.6 transform_rest.6.refs_0_.refs_1_
  238.0 3.9 fusion.42
  250.7 39.3 %layer_backward.1 = (f32[1024,768]{1,0:T(8,128)}, bf16[1024,384]{1,0:T(8,128)(2,1)}, bf16[1024,384]{1,0:T(8,128)(2,1)}, f32[1,3072]{1,0:T(1,128)}, f32[8,768]{1,...) custom-call(s32[2]{0:T(128)} %pad_add_fusion.scalar_ref, ...), custom_call_target="tpu_custom_call" | custom-call | flops 377487360 | bytes 516096 | tf_op jit(solution)/shard_map/layer_backward/pallas_call | solution.py:414
  290.0 3.3 fusion.10
  299.0 3.9 collective-permute-done.17.recv_ref
  305.2 8.4 %collective-permute-done.18 = bf16[384,768]{1,0:T(8,128)(2,1)} collective-permute-done((bf16[384,768]{1,0:T(8,128)(2,1)S(1)}, bf16[384,768]{1,0:T(8,128)(2,1)}, u32[]{:S(2)}, u32[]{:S(2)}) %collective-permute-start.18) | collective-permute-done | bytes 589856 | tf_op jit(solution)/shard_map/ppermute | solution.py:680
  320.5 22.4 %collective-permute-done.26 = bf16[2,96,768]{2,1,0:T(8,128)(2,1)} collective-permute-done((bf16[2,96,768]{2,1,0:T(8,128)(2,1)}, bf16[2,96,768]{2,1,0:T(8,128)(2,1)}, u32[]{:S(2)}, u32[]{:S(2)}) %collective-permute-start.26) | collective-permute-done | bytes 294944 | tf_op jit(solution)/shard_map/ppermute | solution.py:710
  342.9 2.7 collective-permute-start.28
  348.0 2.4 copy-done.6
  360.9 2.9 fusion.8
  367.7 6.8 %collective-permute-start.30 = (bf16[2,96,768]{2,1,0:T(8,128)(2,1)S(1)}, bf16[2,96,768]{2,1,0:T(8,128)(2,1)S(1)}, u32[]{:S(2)}, u32[]{:S(2)}) collective-permute-start(bf16[2,96,768]{2,1,0:T(8,128)(2,1)S(1)} %copy-done.30), channel_id=1, source_target_pairs={{0,1},{1,2},{2,3},{3,0},{4,5},{5,6},{6,7},{7,4},{8,9},{9,10},{10,1... | collective-permute-start | bytes 884744 | tf_op jit(solution)/shard_map/ppermute | solution.py:710
  375.9 5.8 %collective-permute-done.34 = bf16[384,768]{1,0:T(8,128)(2,1)} collective-permute-done((bf16[384,768]{1,0:T(8,128)(2,1)}, bf16[384,768]{1,0:T(8,128)(2,1)}, u32[]{:S(2)}, u32[]{:S(2)}) %collective-permute-start.34) | collective-permute-done | bytes 589856 | tf_op jit(solution)/shard_map/ppermute | solution.py:680
  381.6 7.6 %collective-permute-start.32 = (bf16[2,96,768]{2,1,0:T(8,128)(2,1)S(1)}, bf16[2,96,768]{2,1,0:T(8,128)(2,1)}, u32[]{:S(2)}, u32[]{:S(2)}) collective-permute-start(bf16[2,96,768]{2,1,0:T(8,128)(2,1)S(1)} %copy-done.30), channel_id=1, source_target_pairs={{0,3},{1,0},{2,1},{3,2},{4,7},{5,4},{6,5},{7,6},{8,11},{9,8},{10,9... | collective-permute-start | bytes 884744 | tf_op jit(solution)/shard_map/ppermute | solution.py:710
  395.8 4.8 collective-permute-done.32
  409.4 2.6 fusion.37
  412.0 2.6 fusion.38
  417.5 2.8 collective-permute-start.36
  420.4 6.9 %collective-permute-done.38 = bf16[2,96,768]{2,1,0:T(8,128)(2,1)S(1)} collective-permute-done((bf16[2,96,768]{2,1,0:T(8,128)(2,1)S(1)}, bf16[2,96,768]{2,1,0:T(8,128)(2,1)S(1)}, u32[]{:S(2)}, u32[]{:S(2)}) %collective-permute-start.38) | collective-permute-done | bytes 294944 | tf_op jit(solution)/shard_map/ppermute | solution.py:710
  428.3 6.0 %collective-permute-start.43 = (bf16[2,96,768]{2,1,0:T(8,128)(2,1)S(1)}, bf16[2,96,768]{2,1,0:T(8,128)(2,1)S(1)}, u32[]{:S(2)}, u32[]{:S(2)}) collective-permute-start(bf16[2,96,768]{2,1,0:T(8,128)(2,1)S(1)} %add_convert_fusion.9), channel_id=1, source_target_pairs={{0,1},{1,2},{2,3},{3,0},{4,5},{5,6},{6,7},{7,4},{8,9},{9,10},{10,1... | collective-permute-start | bytes 884744 | tf_op jit(solution)/shard_map/ppermute | solution.py:710
  439.3 4.2 collective-permute-done.43
  444.0 10.7 %collective-permute-done.44 = bf16[2,96,768]{2,1,0:T(8,128)(2,1)S(1)} collective-permute-done((bf16[2,96,768]{2,1,0:T(8,128)(2,1)S(1)}, bf16[2,96,768]{2,1,0:T(8,128)(2,1)S(1)}, u32[]{:S(2)}, u32[]{:S(2)}) %collective-permute-start.44) | collective-permute-done | bytes 294944 | tf_op jit(solution)/shard_map/ppermute | solution.py:710
  456.8 5.9 %collective-permute-done.42 = f32[2,6912]{1,0:T(2,128)S(1)} collective-permute-done((f32[2,6912]{1,0:T(2,128)S(1)}, f32[2,6912]{1,0:T(2,128)S(1)}, u32[]{:S(2)}, u32[]{:S(2)}) %collective-permute-start.42) | collective-permute-done | bytes 55328 | tf_op jit(solution)/shard_map/ppermute | solution.py:924
  469.8 9.7 %collective-permute-done.50 = bf16[4,96,768]{2,1,0:T(8,128)(2,1)S(1)} collective-permute-done((bf16[4,96,768]{2,1,0:T(8,128)(2,1)S(1)}, bf16[4,96,768]{2,1,0:T(8,128)(2,1)S(1)}, u32[]{:S(2)}, u32[]{:S(2)}) %collective-permute-start.50) | collective-permute-done | bytes 589856 | tf_op jit(solution)/shard_map/ppermute | solution.py:680
  487.3 4.6 write_weights.2
  491.9 20.2 %collective-permute-done.52.refs_0_ = bf16[2,4,96,768]{3,2,1,0:T(8,128)(2,1)S(1)} collective-permute-done((bf16[2,4,96,768]{3,2,1,0:T(8,128)(2,1)S(1)}, bf16[2,4,96,768]{3,2,1,0:T(8,128)(2,1)S(1)}, u32[]{:S(2)}, u32[]{:S(2)}) %collective-permute-start.52) | collective-permute-done | bytes 1179680 | tf_op jit(solution)/shard_map/ppermute | solution.py:680
  517.3 3.0 collective-permute-start.62
  524.9 4.6 write_weights.3
  (319 shorter events, 135.7 us)
Async XLA Ops:
  7.2 83.1 %all-gather.3.cloned.1.call-start = ((), (), s32[]{:S(2)}) async-start(), calls=%async_computation | async-start | bytes 14155776 | tf_op jit(solution)/shard_map/all_gather | solution.py:828
  7.9 83.2 %all-gather.5.cloned.1.call-start = ((), (), s32[]{:S(2)}) async-start(), calls=%async_computation.1 | async-start | bytes 14155776 | tf_op jit(solution)/shard_map/all_gather | solution.py:829
  11.2 19.3 %collective-permute-start = (bf16[1024,768]{1,0:T(8,128)(2,1)}, bf16[1024,768]{1,0:T(8,128)(2,1)S(1)}, u32[]{:S(2)}, u32[]{:S(2)}) collective-permute-start(bf16[1024,768]{1,0:T(8,128)(2,1)} %select_bitcast_fusion.2), channel_id=1, source_target_pairs={{16,3},{17,2},{2,17},{3,16},{20,7},{21,6},{6,21},{7,20},{24,11},{2... | collective-permute-start | bytes 4718600 | tf_op jit(solution)/shard_map/ppermute | solution.py:822
  12.2 74.6 %collective-permute-start.4 = (f32[6912]{0:T(1024)S(1)}, f32[6912]{0:T(1024)S(1)}, u32[]{:S(2)}, u32[]{:S(2)}) collective-permute-start(f32[6912]{0:T(1024)S(1)} %constant_dynamic-update-slice_fusion), channel_id=1, source_target_pairs={{0,16},{16,0},{1,17},{17,1},{2,18},{18,2},{3,19},{19,3},{4,20},{20... | collective-permute-start | bytes 82952 | tf_op jit(solution)/shard_map/ppermute | solution.py:28
  47.2 35.3 %collective-permute-start.2 = (bf16[1040,384]{1,0:T(8,128)(2,1)S(1)}, bf16[1040,384]{1,0:T(8,128)(2,1)S(1)}, u32[]{:S(2)}, u32[]{:S(2)}) collective-permute-start(bf16[1040,384]{1,0:T(8,128)(2,1)S(1)} %fold_spectra.4.part_ref), channel_id=1, source_target_pairs={{0,1},{1,0},{3,2},{2,3},{4,5},{5,4},{7,6},{6,7},{8,9},{9,8},{11,10... | collective-permute-start | bytes 2396168 | tf_op jit(solution)/shard_map/ppermute | solution.py:840
  86.9 42.4 %collective-permute-start.7 = (bf16[1024,768]{1,0:T(8,128)(2,1)}, bf16[1024,768]{1,0:T(8,128)(2,1)}, u32[]{:S(2)}, u32[]{:S(2)}) collective-permute-start(bf16[1024,768]{1,0:T(8,128)(2,1)} %get-tuple-element.273), channel_id=1, source_target_pairs={{16,3},{17,2},{2,17},{3,16},{20,7},{21,6},{6,21},{7,20},{24,11},{2... | collective-permute-start | bytes 4718600 | tf_op jit(solution)/shard_map/ppermute | solution.py:860
  123.7 20.1 %collective-permute-start.6 = (bf16[1040,384]{1,0:T(8,128)(2,1)S(1)}, bf16[1040,384]{1,0:T(8,128)(2,1)S(1)}, u32[]{:S(2)}, u32[]{:S(2)}) collective-permute-start(bf16[1040,384]{1,0:T(8,128)(2,1)S(1)} %fold_spectra.5.part_ref), channel_id=1, source_target_pairs={{0,1},{1,0},{3,2},{2,3},{4,5},{5,4},{7,6},{6,7},{8,9},{9,8},{11,10... | collective-permute-start | bytes 2396168 | tf_op jit(solution)/shard_map/ppermute | solution.py:840
  195.6 12.1 %collective-permute-start.10 = (bf16[1024,384]{1,0:T(8,128)(2,1)}, bf16[1024,384]{1,0:T(8,128)(2,1)S(1)}, u32[]{:S(2)}, u32[]{:S(2)}) collective-permute-start(bf16[1024,384]{1,0:T(8,128)(2,1)} %get-tuple-element.298), channel_id=1, source_target_pairs={{0,16},{16,0},{1,17},{17,1},{2,18},{18,2},{3,19},{19,3},{4,20},{20... | collective-permute-start | bytes 2359304 | tf_op jit(solution)/shard_map/ppermute | solution.py:28
  211.2 26.8 %collective-permute-start.12 = (bf16[2,2,384,768]{3,2,1,0:T(8,128)(2,1)}, bf16[2,2,384,768]{3,2,1,0:T(8,128)(2,1)}, u32[]{:S(2)}, u32[]{:S(2)}) collective-permute-start(bf16[2,2,384,768]{3,2,1,0:T(8,128)(2,1)} %get-tuple-element.317), channel_id=1, source_target_pairs={{0,16},{16,0},{1,17},{17,1},{2,18},{18,2},{3,19},{19,3},{4,20},{20... | collective-permute-start | bytes 7077896 | tf_op jit(solution)/shard_map/ppermute | solution.py:28
  211.7 78.3 %collective-permute-start.11 = (bf16[2,2,384,768]{3,2,1,0:T(8,128)(2,1)}, bf16[2,2,384,768]{3,2,1,0:T(8,128)(2,1)}, u32[]{:S(2)}, u32[]{:S(2)}) collective-permute-start(bf16[2,2,384,768]{3,2,1,0:T(8,128)(2,1)} %get-tuple-element.315), channel_id=1, source_target_pairs={{0,16},{16,0},{1,17},{17,1},{2,18},{18,2},{3,19},{19,3},{4,20},{20... | collective-permute-start | bytes 7077896 | tf_op jit(solution)/shard_map/ppermute | solution.py:28
  211.8 20.2 %collective-permute-start.13 = (bf16[1040,384]{1,0:T(8,128)(2,1)S(1)}, bf16[1040,384]{1,0:T(8,128)(2,1)}, u32[]{:S(2)}, u32[]{:S(2)}) collective-permute-start(bf16[1040,384]{1,0:T(8,128)(2,1)S(1)} %fold_spectra.6.part_ref), channel_id=1, source_target_pairs={{0,1},{1,0},{3,2},{2,3},{4,5},{5,4},{7,6},{6,7},{8,9},{9,8},{11,10... | collective-permute-start | bytes 2396168 | tf_op jit(solution)/shard_map/ppermute | solution.py:840
  241.9 48.2 %collective-permute-start.14 = (bf16[2,384,768]{2,1,0:T(8,128)(2,1)}, bf16[2,384,768]{2,1,0:T(8,128)(2,1)}, u32[]{:S(2)}, u32[]{:S(2)}) collective-permute-start(bf16[2,384,768]{2,1,0:T(8,128)(2,1)} %get-tuple-element.324), channel_id=1, source_target_pairs={{0,4},{4,0},{8,12},{12,8},{1,5},{5,1},{9,13},{13,9},{2,6},{6,2},{1... | collective-permute-start | bytes 3538952 | tf_op jit(solution)/shard_map/ppermute | solution.py:680
  243.4 46.7 %collective-permute-start.15 = (bf16[2,384,768]{2,1,0:T(8,128)(2,1)}, bf16[2,384,768]{2,1,0:T(8,128)(2,1)}, u32[]{:S(2)}, u32[]{:S(2)}) collective-permute-start(bf16[2,384,768]{2,1,0:T(8,128)(2,1)} %get-tuple-element.325), channel_id=1, source_target_pairs={{0,8},{4,12},{8,0},{12,4},{1,9},{5,13},{9,1},{13,5},{2,10},{6,14},... | collective-permute-start | bytes 3538952 | tf_op jit(solution)/shard_map/ppermute | solution.py:680
  244.9 48.5 %collective-permute-start.9 = (bf16[1024,768]{1,0:T(8,128)(2,1)}, bf16[1024,768]{1,0:T(8,128)(2,1)}, u32[]{:S(2)}, u32[]{:S(2)}) collective-permute-start(bf16[1024,768]{1,0:T(8,128)(2,1)} %get-tuple-element.347), channel_id=1, source_target_pairs={{16,3},{17,2},{2,17},{3,16},{20,7},{21,6},{6,21},{7,20},{24,11},{2... | collective-permute-start | bytes 4718600 | tf_op jit(solution)/shard_map/ppermute | solution.py:808
  297.9 15.7 %collective-permute-start.18 = (bf16[384,768]{1,0:T(8,128)(2,1)S(1)}, bf16[384,768]{1,0:T(8,128)(2,1)}, u32[]{:S(2)}, u32[]{:S(2)}) collective-permute-start(bf16[384,768]{1,0:T(8,128)(2,1)S(1)} %get-tuple-element.356), channel_id=1, source_target_pairs={{0,8},{4,12},{8,0},{12,4},{1,9},{5,13},{9,1},{13,5},{2,10},{6,14},... | collective-permute-start | bytes 1769480 | tf_op jit(solution)/shard_map/ppermute | solution.py:680
  298.5 15.3 %collective-permute-start.19 = (bf16[384,768]{1,0:T(8,128)(2,1)S(1)}, bf16[384,768]{1,0:T(8,128)(2,1)S(1)}, u32[]{:S(2)}, u32[]{:S(2)}) collective-permute-start(bf16[384,768]{1,0:T(8,128)(2,1)S(1)} %get-tuple-element.358), channel_id=1, source_target_pairs={{0,4},{4,0},{8,12},{12,8},{1,5},{5,1},{9,13},{13,9},{2,6},{6,2},{1... | collective-permute-start | bytes 1769480 | tf_op jit(solution)/shard_map/ppermute | solution.py:680
  316.3 44.5 %collective-permute-start.22 = (bf16[2,2,384,768]{3,2,1,0:T(8,128)(2,1)}, bf16[2,2,384,768]{3,2,1,0:T(8,128)(2,1)}, u32[]{:S(2)}, u32[]{:S(2)}) collective-permute-start(bf16[2,2,384,768]{3,2,1,0:T(8,128)(2,1)} %get-tuple-element.374), channel_id=1, source_target_pairs={{0,16},{16,0},{1,17},{17,1},{2,18},{18,2},{3,19},{19,3},{4,20},{20... | collective-permute-start | bytes 7077896 | tf_op jit(solution)/shard_map/ppermute | solution.py:28
  316.3 26.6 %collective-permute-start.21 = (bf16[1040,384]{1,0:T(8,128)(2,1)S(1)}, bf16[1040,384]{1,0:T(8,128)(2,1)S(1)}, u32[]{:S(2)}, u32[]{:S(2)}) collective-permute-start(bf16[1040,384]{1,0:T(8,128)(2,1)S(1)} %fold_spectra.7.part_ref), channel_id=1, source_target_pairs={{0,1},{1,0},{3,2},{2,3},{4,5},{5,4},{7,6},{6,7},{8,9},{9,8},{11,10... | collective-permute-start | bytes 2396168 | tf_op jit(solution)/shard_map/ppermute | solution.py:840
  316.5 26.4 %collective-permute-start.26 = (bf16[2,96,768]{2,1,0:T(8,128)(2,1)}, bf16[2,96,768]{2,1,0:T(8,128)(2,1)}, u32[]{:S(2)}, u32[]{:S(2)}) collective-permute-start(bf16[2,96,768]{2,1,0:T(8,128)(2,1)} %get-tuple-element.381), channel_id=1, source_target_pairs={{0,1},{1,2},{2,3},{3,0},{4,5},{5,6},{6,7},{7,4},{8,9},{9,10},{10,1... | collective-permute-start | bytes 884744 | tf_op jit(solution)/shard_map/ppermute | solution.py:710
  318.4 42.5 %collective-permute-start.23 = (bf16[2,384,768]{2,1,0:T(8,128)(2,1)}, bf16[2,384,768]{2,1,0:T(8,128)(2,1)S(1)}, u32[]{:S(2)}, u32[]{:S(2)}) collective-permute-start(bf16[2,384,768]{2,1,0:T(8,128)(2,1)} %get-tuple-element.375), channel_id=1, source_target_pairs={{0,4},{4,0},{8,12},{12,8},{1,5},{5,1},{9,13},{13,9},{2,6},{6,2},{1... | collective-permute-start | bytes 3538952 | tf_op jit(solution)/shard_map/ppermute | solution.py:680
  318.9 42.0 %collective-permute-start.24 = (bf16[2,384,768]{2,1,0:T(8,128)(2,1)}, bf16[2,384,768]{2,1,0:T(8,128)(2,1)}, u32[]{:S(2)}, u32[]{:S(2)}) collective-permute-start(bf16[2,384,768]{2,1,0:T(8,128)(2,1)} %get-tuple-element.376), channel_id=1, source_target_pairs={{0,8},{4,12},{8,0},{12,4},{1,9},{5,13},{9,1},{13,5},{2,10},{6,14},... | collective-permute-start | bytes 3538952 | tf_op jit(solution)/shard_map/ppermute | solution.py:680
  342.9 16.0 %collective-permute-start.27 = (bf16[2,96,768]{2,1,0:T(8,128)(2,1)}, bf16[2,96,768]{2,1,0:T(8,128)(2,1)S(1)}, u32[]{:S(2)}, u32[]{:S(2)}) collective-permute-start(bf16[2,96,768]{2,1,0:T(8,128)(2,1)} %get-tuple-element.382), channel_id=1, source_target_pairs={{0,2},{1,3},{2,0},{3,1},{4,6},{5,7},{6,4},{7,5},{8,10},{9,11},{10,... | collective-permute-start | bytes 884744 | tf_op jit(solution)/shard_map/ppermute | solution.py:710
  342.9 16.0 %collective-permute-start.28 = (bf16[2,96,768]{2,1,0:T(8,128)(2,1)}, bf16[2,96,768]{2,1,0:T(8,128)(2,1)S(1)}, u32[]{:S(2)}, u32[]{:S(2)}) collective-permute-start(bf16[2,96,768]{2,1,0:T(8,128)(2,1)} %get-tuple-element.383), channel_id=1, source_target_pairs={{0,3},{1,0},{2,1},{3,2},{4,7},{5,4},{6,5},{7,6},{8,11},{9,8},{10,9... | collective-permute-start | bytes 884744 | tf_op jit(solution)/shard_map/ppermute | solution.py:710
  365.6 16.1 %collective-permute-start.34 = (bf16[384,768]{1,0:T(8,128)(2,1)}, bf16[384,768]{1,0:T(8,128)(2,1)}, u32[]{:S(2)}, u32[]{:S(2)}) collective-permute-start(bf16[384,768]{1,0:T(8,128)(2,1)} %get-tuple-element.399), channel_id=1, source_target_pairs={{0,8},{4,12},{8,0},{12,4},{1,9},{5,13},{9,1},{13,5},{2,10},{6,14},... | collective-permute-start | bytes 1769480 | tf_op jit(solution)/shard_map/ppermute | solution.py:680
  367.1 22.2 %collective-permute-start.35 = (bf16[384,768]{1,0:T(8,128)(2,1)}, bf16[384,768]{1,0:T(8,128)(2,1)}, u32[]{:S(2)}, u32[]{:S(2)}) collective-permute-start(bf16[384,768]{1,0:T(8,128)(2,1)} %get-tuple-element.401), channel_id=1, source_target_pairs={{0,4},{4,0},{8,12},{12,8},{1,5},{5,1},{9,13},{13,9},{2,6},{6,2},{1... | collective-permute-start | bytes 1769480 | tf_op jit(solution)/shard_map/ppermute | solution.py:680
  367.7 24.3 %collective-permute-start.33 = (bf16[1040,384]{1,0:T(8,128)(2,1)S(1)}, bf16[1040,384]{1,0:T(8,128)(2,1)S(1)}, u32[]{:S(2)}, u32[]{:S(2)}) collective-permute-start(bf16[1040,384]{1,0:T(8,128)(2,1)S(1)} %transform_rest.7.refs_1_.refs_2_), channel_id=1, source_target_pairs={{0,16},{16,0},{1,17},{17,1},{2,18},{18,2},{3,19},{19,3},{4,20},{20... | collective-permute-start | bytes 2396168 | tf_op jit(solution)/shard_map/ppermute | solution.py:28
  367.7 27.7 %collective-permute-start.30 = (bf16[2,96,768]{2,1,0:T(8,128)(2,1)S(1)}, bf16[2,96,768]{2,1,0:T(8,128)(2,1)S(1)}, u32[]{:S(2)}, u32[]{:S(2)}) collective-permute-start(bf16[2,96,768]{2,1,0:T(8,128)(2,1)S(1)} %copy-done.30), channel_id=1, source_target_pairs={{0,1},{1,2},{2,3},{3,0},{4,5},{5,6},{6,7},{7,4},{8,9},{9,10},{10,1... | collective-permute-start | bytes 884744 | tf_op jit(solution)/shard_map/ppermute | solution.py:710
  374.4 21.4 %collective-permute-start.31 = (bf16[2,96,768]{2,1,0:T(8,128)(2,1)S(1)}, bf16[2,96,768]{2,1,0:T(8,128)(2,1)}, u32[]{:S(2)}, u32[]{:S(2)}) collective-permute-start(bf16[2,96,768]{2,1,0:T(8,128)(2,1)S(1)} %copy-done.30), channel_id=1, source_target_pairs={{0,2},{1,3},{2,0},{3,1},{4,6},{5,7},{6,4},{7,5},{8,10},{9,11},{10,... | collective-permute-start | bytes 884744 | tf_op jit(solution)/shard_map/ppermute | solution.py:710
  381.6 19.0 %collective-permute-start.32 = (bf16[2,96,768]{2,1,0:T(8,128)(2,1)S(1)}, bf16[2,96,768]{2,1,0:T(8,128)(2,1)}, u32[]{:S(2)}, u32[]{:S(2)}) collective-permute-start(bf16[2,96,768]{2,1,0:T(8,128)(2,1)S(1)} %copy-done.30), channel_id=1, source_target_pairs={{0,3},{1,0},{2,1},{3,2},{4,7},{5,4},{6,5},{7,6},{8,11},{9,8},{10,9... | collective-permute-start | bytes 884744 | tf_op jit(solution)/shard_map/ppermute | solution.py:710
  389.3 15.8 %collective-permute-start.29 = (bf16[1024,384]{1,0:T(8,128)(2,1)}, bf16[1024,384]{1,0:T(8,128)(2,1)}, u32[]{:S(2)}, u32[]{:S(2)}) collective-permute-start(bf16[1024,384]{1,0:T(8,128)(2,1)} %get-tuple-element.393), channel_id=1, source_target_pairs={{0,16},{16,0},{1,17},{17,1},{2,18},{18,2},{3,19},{19,3},{4,20},{20... | collective-permute-start | bytes 2359304 | tf_op jit(solution)/shard_map/ppermute | solution.py:28
  402.9 14.6 %collective-permute-start.40 = (bf16[4,96,768]{2,1,0:T(8,128)(2,1)S(1)}, bf16[4,96,768]{2,1,0:T(8,128)(2,1)S(1)}, u32[]{:S(2)}, u32[]{:S(2)}) collective-permute-start(bf16[4,96,768]{2,1,0:T(8,128)(2,1)S(1)} %pad_maximum_fusion.6), channel_id=1, source_target_pairs={{0,8},{4,12},{8,0},{12,4},{1,9},{5,13},{9,1},{13,5},{2,10},{6,14},... | collective-permute-start | bytes 1769480 | tf_op jit(solution)/shard_map/ppermute | solution.py:680
  404.5 15.8 %collective-permute-start.41 = (bf16[4,96,768]{2,1,0:T(8,128)(2,1)S(1)}, bf16[4,96,768]{2,1,0:T(8,128)(2,1)S(1)}, u32[]{:S(2)}, u32[]{:S(2)}) collective-permute-start(bf16[4,96,768]{2,1,0:T(8,128)(2,1)S(1)} %pad_maximum_fusion.7), channel_id=1, source_target_pairs={{0,4},{4,0},{8,12},{12,8},{1,5},{5,1},{9,13},{13,9},{2,6},{6,2},{1... | collective-permute-start | bytes 1769480 | tf_op jit(solution)/shard_map/ppermute | solution.py:680
  405.1 15.4 %collective-permute-start.37 = (bf16[2,96,768]{2,1,0:T(8,128)(2,1)S(1)}, bf16[2,96,768]{2,1,0:T(8,128)(2,1)S(1)}, u32[]{:S(2)}, u32[]{:S(2)}) collective-permute-start(bf16[2,96,768]{2,1,0:T(8,128)(2,1)S(1)} %get-tuple-element.418), channel_id=1, source_target_pairs={{0,1},{1,2},{2,3},{3,0},{4,5},{5,6},{6,7},{7,4},{8,9},{9,10},{10,1... | collective-permute-start | bytes 884744 | tf_op jit(solution)/shard_map/ppermute | solution.py:710
  407.0 20.3 %collective-permute-start.38 = (bf16[2,96,768]{2,1,0:T(8,128)(2,1)S(1)}, bf16[2,96,768]{2,1,0:T(8,128)(2,1)S(1)}, u32[]{:S(2)}, u32[]{:S(2)}) collective-permute-start(bf16[2,96,768]{2,1,0:T(8,128)(2,1)S(1)} %get-tuple-element.419), channel_id=1, source_target_pairs={{0,2},{1,3},{2,0},{3,1},{4,6},{5,7},{6,4},{7,5},{8,10},{9,11},{10,... | collective-permute-start | bytes 884744 | tf_op jit(solution)/shard_map/ppermute | solution.py:710
  408.5 18.8 %collective-permute-start.39 = (bf16[2,96,768]{2,1,0:T(8,128)(2,1)S(1)}, bf16[2,96,768]{2,1,0:T(8,128)(2,1)S(1)}, u32[]{:S(2)}, u32[]{:S(2)}) collective-permute-start(bf16[2,96,768]{2,1,0:T(8,128)(2,1)S(1)} %get-tuple-element.420), channel_id=1, source_target_pairs={{0,3},{1,0},{2,1},{3,2},{4,7},{5,4},{6,5},{7,6},{8,11},{9,8},{10,9... | collective-permute-start | bytes 884744 | tf_op jit(solution)/shard_map/ppermute | solution.py:710
  428.3 15.2 %collective-permute-start.43 = (bf16[2,96,768]{2,1,0:T(8,128)(2,1)S(1)}, bf16[2,96,768]{2,1,0:T(8,128)(2,1)S(1)}, u32[]{:S(2)}, u32[]{:S(2)}) collective-permute-start(bf16[2,96,768]{2,1,0:T(8,128)(2,1)S(1)} %add_convert_fusion.9), channel_id=1, source_target_pairs={{0,1},{1,2},{2,3},{3,0},{4,5},{5,6},{6,7},{7,4},{8,9},{9,10},{10,1... | collective-permute-start | bytes 884744 | tf_op jit(solution)/shard_map/ppermute | solution.py:710
  434.3 20.4 %collective-permute-start.44 = (bf16[2,96,768]{2,1,0:T(8,128)(2,1)S(1)}, bf16[2,96,768]{2,1,0:T(8,128)(2,1)S(1)}, u32[]{:S(2)}, u32[]{:S(2)}) collective-permute-start(bf16[2,96,768]{2,1,0:T(8,128)(2,1)S(1)} %add_convert_fusion.9), channel_id=1, source_target_pairs={{0,2},{1,3},{2,0},{3,1},{4,6},{5,7},{6,4},{7,5},{8,10},{9,11},{10,... | collective-permute-start | bytes 884744 | tf_op jit(solution)/shard_map/ppermute | solution.py:710
  436.0 20.7 %collective-permute-start.45 = (bf16[2,96,768]{2,1,0:T(8,128)(2,1)S(1)}, bf16[2,96,768]{2,1,0:T(8,128)(2,1)S(1)}, u32[]{:S(2)}, u32[]{:S(2)}) collective-permute-start(bf16[2,96,768]{2,1,0:T(8,128)(2,1)S(1)} %add_convert_fusion.9), channel_id=1, source_target_pairs={{0,3},{1,0},{2,1},{3,2},{4,7},{5,4},{6,5},{7,6},{8,11},{9,8},{10,9... | collective-permute-start | bytes 884744 | tf_op jit(solution)/shard_map/ppermute | solution.py:710
  437.1 27.4 %collective-permute-start.48 = (bf16[2,4,96,768]{3,2,1,0:T(8,128)(2,1)S(1)}, bf16[2,4,96,768]{3,2,1,0:T(8,128)(2,1)S(1)}, u32[]{:S(2)}, u32[]{:S(2)}) collective-permute-start(bf16[2,4,96,768]{3,2,1,0:T(8,128)(2,1)S(1)} %pad_maximum_fusion.2.refs_4_), channel_id=1, source_target_pairs={{0,4},{4,0},{8,12},{12,8},{1,5},{5,1},{9,13},{13,9},{2,6},{6,2},{1... | collective-permute-start | bytes 3538952 | tf_op jit(solution)/shard_map/ppermute | solution.py:680
  438.9 27.0 %collective-permute-start.49 = (bf16[2,4,96,768]{3,2,1,0:T(8,128)(2,1)S(1)}, bf16[2,4,96,768]{3,2,1,0:T(8,128)(2,1)S(1)}, u32[]{:S(2)}, u32[]{:S(2)}) collective-permute-start(bf16[2,4,96,768]{3,2,1,0:T(8,128)(2,1)S(1)} %pad_maximum_fusion.3.refs_5_), channel_id=1, source_target_pairs={{0,8},{4,12},{8,0},{12,4},{1,9},{5,13},{9,1},{13,5},{2,10},{6,14},... | collective-permute-start | bytes 3538952 | tf_op jit(solution)/shard_map/ppermute | solution.py:680
  443.5 19.2 %collective-permute-start.42 = (f32[2,6912]{1,0:T(2,128)S(1)}, f32[2,6912]{1,0:T(2,128)S(1)}, u32[]{:S(2)}, u32[]{:S(2)}) collective-permute-start(f32[2,6912]{1,0:T(2,128)S(1)} %add.322), channel_id=1, source_target_pairs={{0,2},{1,3},{2,0},{3,1},{4,6},{5,7},{6,4},{7,5},{8,10},{9,11},{10,... | collective-permute-start | bytes 165896 | tf_op jit(solution)/shard_map/ppermute | solution.py:924
  454.7 30.2 %collective-permute-start.56 = (bf16[2,4,96,768]{3,2,1,0:T(8,128)(2,1)S(1)}, bf16[2,4,96,768]{3,2,1,0:T(8,128)(2,1)S(1)}, u32[]{:S(2)}, u32[]{:S(2)}) collective-permute-start(bf16[2,4,96,768]{3,2,1,0:T(8,128)(2,1)S(1)} %pad_maximum_fusion.2.refs_4_), channel_id=1, source_target_pairs={{0,16},{1,17},{2,18},{3,19},{4,20},{5,21},{6,22},{7,23},{8,24},{9,... | collective-permute-start | bytes 3538952 | tf_op jit(solution)/shard_map/ppermute | solution.py:958
  466.0 13.5 %collective-permute-start.50 = (bf16[4,96,768]{2,1,0:T(8,128)(2,1)S(1)}, bf16[4,96,768]{2,1,0:T(8,128)(2,1)S(1)}, u32[]{:S(2)}, u32[]{:S(2)}) collective-permute-start(bf16[4,96,768]{2,1,0:T(8,128)(2,1)S(1)} %pad_maximum_fusion.8), channel_id=1, source_target_pairs={{0,8},{4,12},{8,0},{12,4},{1,9},{5,13},{9,1},{13,5},{2,10},{6,14},... | collective-permute-start | bytes 1769480 | tf_op jit(solution)/shard_map/ppermute | solution.py:680
  466.4 13.8 %collective-permute-start.51 = (bf16[4,96,768]{2,1,0:T(8,128)(2,1)S(1)}, bf16[4,96,768]{2,1,0:T(8,128)(2,1)S(1)}, u32[]{:S(2)}, u32[]{:S(2)}) collective-permute-start(bf16[4,96,768]{2,1,0:T(8,128)(2,1)S(1)} %pad_maximum_fusion.9), channel_id=1, source_target_pairs={{0,4},{4,0},{8,12},{12,8},{1,5},{5,1},{9,13},{13,9},{2,6},{6,2},{1... | collective-permute-start | bytes 1769480 | tf_op jit(solution)/shard_map/ppermute | solution.py:680
  467.8 18.0 %collective-permute-start.57 = (bf16[2,4,96,768]{3,2,1,0:T(8,128)(2,1)S(1)}, bf16[2,4,96,768]{3,2,1,0:T(8,128)(2,1)S(1)}, u32[]{:S(2)}, u32[]{:S(2)}) collective-permute-start(bf16[2,4,96,768]{3,2,1,0:T(8,128)(2,1)S(1)} %pad_maximum_fusion.3.refs_5_), channel_id=1, source_target_pairs={{0,16},{1,17},{2,18},{3,19},{4,20},{5,21},{6,22},{7,23},{8,24},{9,... | collective-permute-start | bytes 3538952 | tf_op jit(solution)/shard_map/ppermute | solution.py:958
  483.5 28.6 %collective-permute-start.52 = (bf16[2,4,96,768]{3,2,1,0:T(8,128)(2,1)S(1)}, bf16[2,4,96,768]{3,2,1,0:T(8,128)(2,1)S(1)}, u32[]{:S(2)}, u32[]{:S(2)}) collective-permute-start(bf16[2,4,96,768]{3,2,1,0:T(8,128)(2,1)S(1)} %pad_maximum_fusion.4.refs_0_), channel_id=1, source_target_pairs={{0,4},{4,0},{8,12},{12,8},{1,5},{5,1},{9,13},{13,9},{2,6},{6,2},{1... | collective-permute-start | bytes 3538952 | tf_op jit(solution)/shard_map/ppermute | solution.py:680
  485.0 28.8 %collective-permute-start.53 = (bf16[2,4,96,768]{3,2,1,0:T(8,128)(2,1)S(1)}, bf16[2,4,96,768]{3,2,1,0:T(8,128)(2,1)S(1)}, u32[]{:S(2)}, u32[]{:S(2)}) collective-permute-start(bf16[2,4,96,768]{3,2,1,0:T(8,128)(2,1)S(1)} %pad_maximum_fusion.5.refs_1_), channel_id=1, source_target_pairs={{0,8},{4,12},{8,0},{12,4},{1,9},{5,13},{9,1},{13,5},{2,10},{6,14},... | collective-permute-start | bytes 3538952 | tf_op jit(solution)/shard_map/ppermute | solution.py:680
  485.8 35.9 %collective-permute-start.46 = (bf16[1024,768]{1,0:T(8,128)(2,1)S(1)}, bf16[1024,768]{1,0:T(8,128)(2,1)S(1)}, u32[]{:S(2)}, u32[]{:S(2)}) collective-permute-start(bf16[1024,768]{1,0:T(8,128)(2,1)S(1)} %finish.1), channel_id=1, source_target_pairs={{16,3},{17,2},{2,17},{3,16},{20,7},{21,6},{6,21},{7,20},{24,11},{2... | collective-permute-start | bytes 4718600 | tf_op jit(solution)/shard_map/ppermute | solution.py:808
  (75 other events, 501.3 us)
Sparse Core Ops, SparseCore 0:
  9.6 24.5 all-gather.2
  35.7 23.0 all-gather.4

commit v3 on v2

--- a/solution.py
+++ b/solution.py
@@ -272,39 +272,48 @@
     rows, width = x.shape
     hidden = w1.shape[2]
     half = width // 2
-    tile = min(ROWS, rows)
+    tile = min(2 * ROWS, rows)
+    sub = min(ROWS, tile)
     chunk = min(CHUNK, hidden)
     factor = 1.0 / math.sqrt(width)
 
     def body(core_ref, x_ref, m0, t0, m1, t1, unfold_ref, w1_ref, w2_ref, b1_ref, vec_ref, spread_ref, *outs):
         out_ref, low_ref, act_ref, slope_ref, unit1_ref, scale1_ref, unit2_ref, scale2_ref = outs[:8]
-        mixture = mixture_tile(core_ref, m0, t0, m1, t1, unfold_ref).astype(BF).astype(F32)
-        unit, scale = standardize(x_ref[...].astype(F32) + mixture)
         b2, mg, ms, og, os = (vec_ref[0, i : i + 1] for i in range(5))
-        normed = unit * mg + ms
-        unit1_ref[...] = unit.astype(BF)
-        scale1_ref[...] = jnp.broadcast_to(scale, scale1_ref.shape)
-        low = normed.astype(BF)
-        low_ref[...] = low
-        total = normed + b2
+        mixture = mixture_tile(core_ref, m0, t0, m1, t1, unfold_ref).astype(BF)
+        lows, totals = [], []
+        for at in range(0, tile, sub):
+            part = slice(at, at + sub)
+            unit, scale = standardize(x_ref[part].astype(F32) + mixture[part].astype(F32))
+            normed = unit * mg + ms
+            unit1_ref[part] = unit.astype(BF)
+            scale1_ref[part] = jnp.broadcast_to(scale, (sub, scale1_ref.shape[1]))
+            lows.append(normed.astype(BF))
+            low_ref[part] = lows[-1]
+            totals.append(normed + b2)
         for start in range(0, hidden, chunk):
             span = slice(start, start + chunk)
-            pre = product(low, w1_ref[0, :, span]) + b1_ref[0, :, span]
-            cdf = 0.5 + 0.5 * lax.erf(pre * (1.0 / math.sqrt(2.0)))
-            act = (pre * cdf).astype(BF)
-            act_ref[:, span] = act
-            slope_ref[:, span] = (cdf + pre * (jnp.exp(-0.5 * pre * pre) * (1.0 / math.sqrt(2.0 * math.pi)))).astype(BF)
-            total = total + product(act, w2_ref[0, span, :])
-        unit, scale = standardize(total)
-        unit2_ref[...] = unit.astype(BF)
-        scale2_ref[...] = jnp.broadcast_to(scale, scale2_ref.shape)
-        out = (unit * og + os).astype(BF)
-        out_ref[...] = out
-        if ahead:
-            own_ref, other_ref = outs[8:]
-            spectra = product(out, spread_ref[...]) * factor
-            own_ref[...] = spectra[:, :half].astype(BF)
-            other_ref[...] = spectra[:, half:].astype(BF)
+            for i, at in enumerate(range(0, tile, sub)):
+                part = slice(at, at + sub)
+                pre = product(lows[i], w1_ref[0, :, span]) + b1_ref[0, :, span]
+                cdf = 0.5 + 0.5 * lax.erf(pre * (1.0 / math.sqrt(2.0)))
+                act = (pre * cdf).astype(BF)
+                act_ref[part, span] = act
+                slope = cdf + pre * (jnp.exp(-0.5 * pre * pre) * (1.0 / math.sqrt(2.0 * math.pi)))
+                slope_ref[part, span] = slope.astype(BF)
+                totals[i] = totals[i] + product(act, w2_ref[0, span, :])
+        for i, at in enumerate(range(0, tile, sub)):
+            part = slice(at, at + sub)
+            unit, scale = standardize(totals[i])
+            unit2_ref[part] = unit.astype(BF)
+            scale2_ref[part] = jnp.broadcast_to(scale, (sub, scale2_ref.shape[1]))
+            out = (unit * og + os).astype(BF)
+            out_ref[part] = out
+            if ahead:
+                own_ref, other_ref = outs[8:]
+                spectra = product(out, spread_ref[...]) * factor
+                own_ref[part] = spectra[:, :half].astype(BF)
+                other_ref[part] = spectra[:, half:].astype(BF)
 
     mine, theirs = mixed
     return call(
@@ -344,7 +353,7 @@
         4 * rows * width * (hidden + width),
         4 * width * hidden + 4 * rows * hidden + 14 * rows * width,
         "layer_forward",
-        58,
+        60,
     )(core, x, mine, mine, theirs, theirs, unfold, w1, w2, b1, vec, spread)
 
 
@@ -807,8 +816,10 @@
     def give_start(value):
         return value, lax.ppermute(value, ("pipe", "seq"), out_pairs)
 
-    def give_cut(value, moved):
-        block = jnp.where(local, value, moved)
+    def give_pick(value, moved):
+        return jnp.where(local, value, moved)
+
+    def give_cut(block):
         return jnp.where(first, block[:, :half], block[:, half:]), jnp.where(first, block[:, half:], block[:, :half])
 
     def give_end(mine, beside):
@@ -907,41 +918,41 @@
     grad, own, other, wide0, narrow0, my_sent, my_kept, other_sent, other_kept = back(0, grad, (mixed, came))
 
     sums = run(early.first_sums(my_kept1, got_kept1))
-    out_mine, out_theirs = line(give_cut, *out_moved)
+    out_block = line(give_pick, *out_moved)
 
     got_sent = swap_cores(line.after(other_sent))
     came = swap_cores(line.after(other))
     early.start_second(line.after(sums))
+    hops = iter(small_hops())
+    small = line.after(jnp.stack([flat_small(wide0, narrow0), flat_small(wide1, narrow1)]))
+
+    def start_hop():
+        axis, pairs = next(hops)
+        return lax.ppermute(line.after(small), axis, pairs)
+
+    def end_hop(got):
+        return line(lambda a, b: a + b, small, got)
+
+    hop = start_hop()
     folded = fold(own, came)
     sent = run(late.sent(my_sent, got_sent))
     pieces = run(early.second_sums())
-
-    hops = iter(small_hops())
-    small = jnp.stack([flat_small(wide0, narrow0), flat_small(wide1, narrow1)])
-
-    def start_hop():
-        axis, pairs = next(hops)
-        return lax.ppermute(line.after(small), axis, pairs)
-
-    def end_hop(got):
-        return line(lambda a, b: a + b, small, got)
+    small = end_hop(hop)
 
     late.start_first(line.after(sent))
-    parts = spread_out(line.after(folded))
     early.start_scatter(line.after(pieces))
     got_kept0 = swap_cores(line.after(other_kept))
     hop = start_hop()
     begun = part(folded)
-    mixed = rest(begun, parts)
+    out_mine, out_theirs = line(give_cut, out_block)
     piece = run(early.scattered())
     small = end_hop(hop)
     sums = run(late.first_sums(my_kept, got_kept0))
 
     late.start_second(line.after(sums))
     early.start_gather(line.after(piece))
-    out_beside, came = swap_cores(line.after((out_theirs, mixed)))
+    out_beside = swap_cores(line.after(out_theirs))
     pieces = run(late.second_sums())
-    in_ready = line(lambda g, m: finish(which, g, m, unfold), grad, (mixed, came))
     streams = run(early.gathered())
 
     late.start_scatter(line.after(pieces))
@@ -956,32 +967,33 @@
 
     late.start_gather(line.after(piece))
     pairs_far1 = lax.ppermute(line.after(pairs), "pipe", [(0, 1)])
-    hop = start_hop()
     streams = run(late.gathered())
-    small = end_hop(hop)
     far1 = line.after(early.far)
 
     streams, far1 = lax.optimization_barrier((streams, far1))
     late.start_back(streams)
-    hop = start_hop()
+    parts = spread_out(line.after(folded))
     far1_far = lax.ppermute(line.after(far1), "pipe", [(0, 1)])
-    in_moved = give_start(line.after(in_ready))
     pairs0 = run(late.paired())
-    small = end_hop(hop)
 
     late.start_last(line.after(pairs0))
     pairs_far0 = lax.ppermute(line.after(pairs0), "pipe", [(1, 0)])
-    hop = start_hop()
+    mixed = rest(begun, parts)
+    came = swap_cores(mixed)
+    in_ready = line(lambda g, m: finish(which, g, m, unfold), grad, (mixed, came))
+    in_moved = give_start(in_ready)
     scalars = jnp.stack([core, index, z]).astype(jnp.int32)
     begun = line(lambda *v: write_weights(scalars, 0, v), (pairs0, pairs_far0), (pairs, pairs_far1))
     far0 = line.after(late.far)
 
     far0_far = lax.ppermute(far0, "pipe", [(1, 0)])
-    small, far0_far = lax.optimization_barrier((small, far0_far))
+    hop = start_hop()
+    g_w1, g_w2 = line(lambda b, *v: write_weights(scalars, 1, v, b), begun, (far0, far0_far), (far1, far1_far))
     small = end_hop(hop)
-    in_mine, in_theirs = line(give_cut, *in_moved)
+    hop = start_hop()
+    in_mine, in_theirs = line(lambda *v: give_cut(give_pick(*v)), *in_moved)
     in_beside = swap_cores(line.after(in_theirs))
-    g_w1, g_w2 = line(lambda b, *v: write_weights(scalars, 1, v, b), begun, (far0, far0_far), (far1, far1_far))
+    small = end_hop(hop)
     in_grad = line(give_end, in_mine, in_beside)
     for axis, hop in hops:
         small = line(lambda a, b: a + b, small, lax.ppermute(small, axis, hop))

time: 551 us -> 534 us (0.969)
  waiting for transfers between devices: 150 us -> 135 us
    ppermute x12, starting transfers between devices: 33.4 us -> 19.3 us  [along(): lax.ppermute(value, 'seq', [(i, (i + by) % self.peers) for i in range(sel...]
    ppermute x16, waiting for transfers between devices: 51.3 us -> 38.4 us  [across(): return lax.ppermute(value, 'dp', bit_pairs(self.count, bit))]
    unnamed x119 -> x127, local copies, waits for them, and re-layouts: 24.5 us -> 24.4 us
  transfers between devices with their start and end apart: 66 -> 66, of which waited for: 30 -> 29; matrix products, arithmetic and copies ran while one was open for 11% -> 12% of each run, Pallas kernels for 22% -> 23%
where the time goes in v3:
time: 534 us; the launch traced here: 524 us
  Pallas kernels  168 us (31%)
  waiting for transfers between devices  135 us (25%)
  starting transfers between devices  109 us (20%)
  other arithmetic  49.4 us (9%)
  local copies, waits for them, and re-layouts  33.9 us (6%)
  between operations  15.8 us (3%)
  matrix products  13.7 us (3%)
    pallas_call x2, Pallas kernels, forward(): call(body, (rows // tile,), [scalar_block(), row_block(tile, width)] + mi...  49 us
    ppermute x12, waiting for transfers between devices, along(): lax.ppermute(value, 'seq', [(i, (i + by) % self.peers) for i in range(sel...  46.2 us
    pallas_call x1, Pallas kernels, backward(): call(body, (rows // tile,), [scalar_block(), row_block(tile, width)] + ex...  39 us
    ppermute x16, waiting for transfers between devices, across(): return lax.ppermute(value, 'dp', bit_pairs(self.count, bit))  38.4 us
    ppermute x4, starting transfers between devices, spread_out(): return [lax.ppermute(folded, 'seq', pairs) for pairs in group_shifts]  24.7 us
    unnamed x127, local copies, waits for them, and re-layouts  24.4 us
    ppermute x4, waiting for transfers between devices, spread_out(): return [lax.ppermute(folded, 'seq', pairs) for pairs in group_shifts]  24.1 us
    pallas_call x2, Pallas kernels, grad_blocks(): pl.pallas_call(body, grid_spec=pltpu.PrefetchScalarGridSpec(num_scalar_pr...  22.9 us
  transfers between devices with their start and end apart: 66, of which 29 were waited for; matrix products, arithmetic and copies ran while one was open for 12% of the time, Pallas kernels for 23%

profile of v3, /device:TPU:0, one launch (start us, length us, event | category | flops | bytes accessed | tf_op | source)
XLA Modules:
  0.0 524.2 jit_solution(13797881063284357188)
XLA Ops:
  13.2 5.3 %collective-permute-start.4 = (f32[6912]{0:T(1024)S(1)}, f32[6912]{0:T(1024)S(1)}, u32[]{:S(2)}, u32[]{:S(2)}) collective-permute-start(f32[6912]{0:T(1024)S(1)} %constant_dynamic-update-slice_fusion), channel_id=1, source_target_pairs={{0,16},{16,0},{1,17},{17,1},{2,18},{18,2},{3,19},{19,3},{4,20},{20... | collective-permute-start | bytes 82952 | tf_op jit(solution)/shard_map/ppermute | solution.py:28
  18.7 11.8 %select_convert_fusion = (bf16[768,768]{1,0:T(8,128)(2,1)}, bf16[768,768]{1,0:T(8,128)(2,1)S(1)}) fusion(s32[768]{0:T(1024)S(1)} %get-tuple-element.551, s32[768]{0:T(1024)S(1)} %get-tuple-element.552, f32[]{:T(128)S(6)} %select_n.299, pred[768]{0:T(1024)(128)(4,1)S(1)} %select_compare_fusion, f32[]{:T(128)S(6)} %neg.3), kind=kLoop, calls=%fused_computation.23 | loop fusion | flops 12976128 | bytes 2366216 | tf_op jit(solution)/shard_map/convert_element_type | solution.py:64
  32.7 2.8 spectra.1
  35.5 7.7 %collective-permute-start.1 = (bf16[1024,384]{1,0:T(8,128)(2,1)}, bf16[1024,384]{1,0:T(8,128)(2,1)S(1)}, u32[]{:S(2)}, u32[]{:S(2)}) collective-permute-start(bf16[1024,384]{1,0:T(8,128)(2,1)} %get-tuple-element.253), channel_id=1, source_target_pairs={{0,16},{16,0},{1,17},{17,1},{2,18},{18,2},{3,19},{19,3},{4,20},{20... | collective-permute-start | bytes 2359304 | tf_op jit(solution)/shard_map/ppermute | solution.py:28
  43.8 2.6 fusion.57
  46.8 16.8 %collective-permute-start.2 = (bf16[1040,384]{1,0:T(8,128)(2,1)S(1)}, bf16[1040,384]{1,0:T(8,128)(2,1)S(1)}, u32[]{:S(2)}, u32[]{:S(2)}) collective-permute-start(bf16[1040,384]{1,0:T(8,128)(2,1)S(1)} %fold_spectra.4.part_ref), channel_id=1, source_target_pairs={{0,1},{1,0},{3,2},{2,3},{4,5},{5,4},{7,6},{6,7},{8,9},{9,8},{11,10... | collective-permute-start | bytes 2396168 | tf_op jit(solution)/shard_map/ppermute | solution.py:851
  63.6 3.3 add_convert_fusion
  69.2 12.4 %collective-permute-done.2.refs_4_ = bf16[1040,384]{1,0:T(8,128)(2,1)S(1)} collective-permute-done((bf16[1040,384]{1,0:T(8,128)(2,1)S(1)}, bf16[1040,384]{1,0:T(8,128)(2,1)S(1)}, u32[]{:S(2)}, u32[]{:S(2)}) %collective-permute-start.2) | collective-permute-done | bytes 798752 | tf_op jit(solution)/shard_map/ppermute | solution.py:851
  89.8 24.6 %layer_forward.2 = (bf16[1024,768]{1,0:T(8,128)(2,1)}, bf16[1024,768]{1,0:T(8,128)(2,1)}, bf16[1024,3072]{1,0:T(8,128)(2,1)}, bf16[1024,3072]{1,0:T(8,128)(2,1)}...) custom-call(s32[1]{0:T(128)} %bitcast.core_ref.refs_0_, ...), custom_call_target="tpu_custom_call" | custom-call | flops 188743680 | bytes 516096 | tf_op jit(solution)/shard_map/layer_forward/pallas_call | solution.py:319
  114.4 3.3 collective-permute-start.5
  122.2 2.4 copy-done.1
  129.3 3.5 fusion.27.refs_0_
  132.8 8.7 %collective-permute-done.6.refs_4_ = bf16[1040,384]{1,0:T(8,128)(2,1)S(1)} collective-permute-done((bf16[1040,384]{1,0:T(8,128)(2,1)S(1)}, bf16[1040,384]{1,0:T(8,128)(2,1)S(1)}, u32[]{:S(2)}, u32[]{:S(2)}) %collective-permute-start.6) | collective-permute-done | bytes 798752 | tf_op jit(solution)/shard_map/ppermute | solution.py:851
  147.1 24.4 %layer_forward.3 = (bf16[1024,768]{1,0:T(8,128)(2,1)}, bf16[1024,768]{1,0:T(8,128)(2,1)}, bf16[1024,3072]{1,0:T(8,128)(2,1)}, bf16[1024,3072]{1,0:T(8,128)(2,1)}...) custom-call(s32[1]{0:T(128)} %bitcast.core_ref.refs_0_, ...), custom_call_target="tpu_custom_call" | custom-call | flops 188743680 | bytes 516096 | tf_op jit(solution)/shard_map/layer_forward/pallas_call | solution.py:319
  171.6 21.4 %last_backward.1 = (f32[1024,768]{1,0:T(8,128)}, bf16[1024,768]{1,0:T(8,128)(2,1)}, bf16[1024,3072]{1,0:T(8,128)(2,1)}, bf16[1024,384]{1,0:T(8,128)(2,1)}, bf16[...) custom-call(bf16[1024,768]{1,0:T(8,128)(2,1)} %fusion.27.refs_0_, ...), custom_call_target="tpu_custom_call" | custom-call | flops 188743680 | bytes 516096 | tf_op jit(solution)/shard_map/last_backward/pallas_call | solution.py:507
  193.7 11.4 %grad_blocks.2 = (bf16[2,2,384,768]{3,2,1,0:T(8,128)(2,1)}, bf16[2,2,384,768]{3,2,1,0:T(8,128)(2,1)}) custom-call(s32[2]{0:T(128)} %pad_add_fusion.1.scalar_ref, bf16[1024,3072]{1,0:T(8,128)(2,1)} %get-tuple-element.307.act_ref, bf16[1024,768]{1,0:T(8,128)(2,1)} %get-tuple-element.308.gb_ref, bf16[1024,768]{1,0:T(8,128)(2,1)} %get-tuple-element.309.low_ref, ...), custom_call_target="tpu_custom_call" | custom-call | flops 75497472 | bytes 245760 | tf_op jit(solution)/shard_map/grad_blocks/pallas_call | solution.py:571
  210.7 11.4 %grad_blocks.3 = (bf16[2,2,384,768]{3,2,1,0:T(8,128)(2,1)}, bf16[2,2,384,768]{3,2,1,0:T(8,128)(2,1)}) custom-call(s32[2]{0:T(128)} %pad_add_fusion.scalar_ref, bf16[1024,3072]{1,0:T(8,128)(2,1)} %get-tuple-element.307.act_ref, bf16[1024,768]{1,0:T(8,128)(2,1)} %get-tuple-element.308.gb_ref, bf16[1024,768]{1,0:T(8,128)(2,1)} %get-tuple-element.309.low_ref, ...), custom_call_target="tpu_custom_call" | custom-call | flops 75497472 | bytes 245760 | tf_op jit(solution)/shard_map/grad_blocks/pallas_call | solution.py:571
  226.8 2.7 collective-permute-done.13.refs_4_
  229.4 2.4 copy-done.6
  231.8 3.6 transform_rest.6.refs_0_.refs_1_
  235.4 3.9 fusion.42
  248.2 39.0 %layer_backward.1 = (f32[1024,768]{1,0:T(8,128)}, bf16[1024,384]{1,0:T(8,128)(2,1)}, bf16[1024,384]{1,0:T(8,128)(2,1)}, f32[1,3072]{1,0:T(1,128)}, f32[8,768]{1,...) custom-call(s32[2]{0:T(128)} %pad_add_fusion.scalar_ref, ...), custom_call_target="tpu_custom_call" | custom-call | flops 377487360 | bytes 516096 | tf_op jit(solution)/shard_map/layer_backward/pallas_call | solution.py:423
  288.2 3.7 fusion.10
  292.9 2.8 broadcast_select_fusion.1
  298.5 3.1 collective-permute-done.17.recv_ref
  302.0 3.6 fusion.44
  305.6 7.5 %collective-permute-done.19 = bf16[384,768]{1,0:T(8,128)(2,1)S(1)} collective-permute-done((bf16[384,768]{1,0:T(8,128)(2,1)}, bf16[384,768]{1,0:T(8,128)(2,1)S(1)}, u32[]{:S(2)}, u32[]{:S(2)}) %collective-permute-start.19) | collective-permute-done | bytes 589856 | tf_op jit(solution)/shard_map/ppermute | solution.py:689
  320.0 9.7 %collective-permute-done.26 = bf16[2,96,768]{2,1,0:T(8,128)(2,1)S(1)} collective-permute-done((bf16[2,96,768]{2,1,0:T(8,128)(2,1)S(1)}, bf16[2,96,768]{2,1,0:T(8,128)(2,1)S(1)}, u32[]{:S(2)}, u32[]{:S(2)}) %collective-permute-start.26) | collective-permute-done | bytes 294944 | tf_op jit(solution)/shard_map/ppermute | solution.py:719
  329.7 2.4 copy-done.2
  340.4 6.6 %collective-permute-start.25 = (f32[2,6912]{1,0:T(2,128)S(1)}, f32[2,6912]{1,0:T(2,128)S(1)}, u32[]{:S(2)}, u32[]{:S(2)}) collective-permute-start(f32[2,6912]{1,0:T(2,128)S(1)} %add.286), channel_id=1, source_target_pairs={{0,1},{1,0},{2,3},{3,2},{4,5},{5,4},{6,7},{7,6},{8,9},{9,8},{10,11... | collective-permute-start | bytes 165896 | tf_op jit(solution)/shard_map/ppermute | solution.py:931
  356.7 4.0 collective-permute-start.31
  366.9 8.2 %collective-permute-done.31 = bf16[2,96,768]{2,1,0:T(8,128)(2,1)} collective-permute-done((bf16[2,96,768]{2,1,0:T(8,128)(2,1)}, bf16[2,96,768]{2,1,0:T(8,128)(2,1)}, u32[]{:S(2)}, u32[]{:S(2)}) %collective-permute-start.31) | collective-permute-done | bytes 294944 | tf_op jit(solution)/shard_map/ppermute | solution.py:719
  380.5 3.7 collective-permute-start.35
  386.6 2.5 fusion.37
  389.1 2.7 fusion.38
  394.8 8.7 %collective-permute-done.36 = bf16[2,96,768]{2,1,0:T(8,128)(2,1)S(1)} collective-permute-done((bf16[2,96,768]{2,1,0:T(8,128)(2,1)S(1)}, bf16[2,96,768]{2,1,0:T(8,128)(2,1)S(1)}, u32[]{:S(2)}, u32[]{:S(2)}) %collective-permute-start.36) | collective-permute-done | bytes 294944 | tf_op jit(solution)/shard_map/ppermute | solution.py:719
  403.6 7.8 %collective-permute-done.40 = f32[2,6912]{1,0:T(2,128)S(1)} collective-permute-done((f32[2,6912]{1,0:T(2,128)S(1)}, f32[2,6912]{1,0:T(2,128)S(1)}, u32[]{:S(2)}, u32[]{:S(2)}) %collective-permute-start.40) | collective-permute-done | bytes 55328 | tf_op jit(solution)/shard_map/ppermute | solution.py:931
  411.8 3.8 collective-permute-start.43
  417.7 5.7 %collective-permute-done.41 = bf16[2,96,768]{2,1,0:T(8,128)(2,1)S(1)} collective-permute-done((bf16[2,96,768]{2,1,0:T(8,128)(2,1)S(1)}, bf16[2,96,768]{2,1,0:T(8,128)(2,1)S(1)}, u32[]{:S(2)}, u32[]{:S(2)}) %collective-permute-start.41) | collective-permute-done | bytes 294944 | tf_op jit(solution)/shard_map/ppermute | solution.py:719
  423.3 11.7 %collective-permute-done.42 = bf16[2,96,768]{2,1,0:T(8,128)(2,1)S(1)} collective-permute-done((bf16[2,96,768]{2,1,0:T(8,128)(2,1)S(1)}, bf16[2,96,768]{2,1,0:T(8,128)(2,1)S(1)}, u32[]{:S(2)}, u32[]{:S(2)}) %collective-permute-start.42) | collective-permute-done | bytes 294944 | tf_op jit(solution)/shard_map/ppermute | solution.py:719
  435.2 6.0 %collective-permute-start.44 = (bf16[1040,384]{1,0:T(8,128)(2,1)S(1)}, bf16[1040,384]{1,0:T(8,128)(2,1)S(1)}, u32[]{:S(2)}, u32[]{:S(2)}) collective-permute-start(bf16[1040,384]{1,0:T(8,128)(2,1)S(1)} %fold_spectra.7.part_ref), channel_id=1, source_target_pairs={{0,1},{1,0},{3,2},{2,3},{4,5},{5,4},{7,6},{6,7},{8,9},{9,8},{11,10... | collective-permute-start | bytes 2396168 | tf_op jit(solution)/shard_map/ppermute | solution.py:851
  446.6 11.0 %collective-permute-done.47 = bf16[4,96,768]{2,1,0:T(8,128)(2,1)S(1)} collective-permute-done((bf16[4,96,768]{2,1,0:T(8,128)(2,1)S(1)}, bf16[4,96,768]{2,1,0:T(8,128)(2,1)S(1)}, u32[]{:S(2)}, u32[]{:S(2)}) %collective-permute-start.47) | collective-permute-done | bytes 589856 | tf_op jit(solution)/shard_map/ppermute | solution.py:689
  460.9 2.5 collective-permute-start.54
  471.2 3.8 collective-permute-start.60
  476.5 4.6 write_weights.2
  481.1 13.7 %collective-permute-done.56.refs_0_ = bf16[2,4,96,768]{3,2,1,0:T(8,128)(2,1)S(1)} collective-permute-done((bf16[2,4,96,768]{3,2,1,0:T(8,128)(2,1)S(1)}, bf16[2,4,96,768]{3,2,1,0:T(8,128)(2,1)S(1)}, u32[]{:S(2)}, u32[]{:S(2)}) %collective-permute-start.56) | collective-permute-done | bytes 1179680 | tf_op jit(solution)/shard_map/ppermute | solution.py:689
  502.7 4.6 write_weights.3
  508.4 3.1 collective-permute-done.63
  (328 shorter events, 135.7 us)
Async XLA Ops:
  7.2 81.7 %all-gather.3.cloned.1.call-start = ((), (), s32[]{:S(2)}) async-start(), calls=%async_computation | async-start | bytes 14155776 | tf_op jit(solution)/shard_map/all_gather | solution.py:839
  7.9 81.0 %all-gather.5.cloned.1.call-start = ((), (), s32[]{:S(2)}) async-start(), calls=%async_computation.1 | async-start | bytes 14155776 | tf_op jit(solution)/shard_map/all_gather | solution.py:840
  11.2 19.3 %collective-permute-start = (bf16[1024,768]{1,0:T(8,128)(2,1)}, bf16[1024,768]{1,0:T(8,128)(2,1)}, u32[]{:S(2)}, u32[]{:S(2)}) collective-permute-start(bf16[1024,768]{1,0:T(8,128)(2,1)} %select_bitcast_fusion.2), channel_id=1, source_target_pairs={{16,3},{17,2},{2,17},{3,16},{20,7},{21,6},{6,21},{7,20},{24,11},{2... | collective-permute-start | bytes 4718600 | tf_op jit(solution)/shard_map/ppermute | solution.py:833
  13.2 72.2 %collective-permute-start.4 = (f32[6912]{0:T(1024)S(1)}, f32[6912]{0:T(1024)S(1)}, u32[]{:S(2)}, u32[]{:S(2)}) collective-permute-start(f32[6912]{0:T(1024)S(1)} %constant_dynamic-update-slice_fusion), channel_id=1, source_target_pairs={{0,16},{16,0},{1,17},{17,1},{2,18},{18,2},{3,19},{19,3},{4,20},{20... | collective-permute-start | bytes 82952 | tf_op jit(solution)/shard_map/ppermute | solution.py:28
  35.5 10.9 %collective-permute-start.1 = (bf16[1024,384]{1,0:T(8,128)(2,1)}, bf16[1024,384]{1,0:T(8,128)(2,1)S(1)}, u32[]{:S(2)}, u32[]{:S(2)}) collective-permute-start(bf16[1024,384]{1,0:T(8,128)(2,1)} %get-tuple-element.253), channel_id=1, source_target_pairs={{0,16},{16,0},{1,17},{17,1},{2,18},{18,2},{3,19},{19,3},{4,20},{20... | collective-permute-start | bytes 2359304 | tf_op jit(solution)/shard_map/ppermute | solution.py:28
  46.8 34.8 %collective-permute-start.2 = (bf16[1040,384]{1,0:T(8,128)(2,1)S(1)}, bf16[1040,384]{1,0:T(8,128)(2,1)S(1)}, u32[]{:S(2)}, u32[]{:S(2)}) collective-permute-start(bf16[1040,384]{1,0:T(8,128)(2,1)S(1)} %fold_spectra.4.part_ref), channel_id=1, source_target_pairs={{0,1},{1,0},{3,2},{2,3},{4,5},{5,4},{7,6},{6,7},{8,9},{9,8},{11,10... | collective-permute-start | bytes 2396168 | tf_op jit(solution)/shard_map/ppermute | solution.py:851
  85.5 43.8 %collective-permute-start.7 = (bf16[1024,768]{1,0:T(8,128)(2,1)}, bf16[1024,768]{1,0:T(8,128)(2,1)}, u32[]{:S(2)}, u32[]{:S(2)}) collective-permute-start(bf16[1024,768]{1,0:T(8,128)(2,1)} %get-tuple-element.271), channel_id=1, source_target_pairs={{16,3},{17,2},{2,17},{3,16},{20,7},{21,6},{6,21},{7,20},{24,11},{2... | collective-permute-start | bytes 4718600 | tf_op jit(solution)/shard_map/ppermute | solution.py:871
  121.3 20.1 %collective-permute-start.6 = (bf16[1040,384]{1,0:T(8,128)(2,1)S(1)}, bf16[1040,384]{1,0:T(8,128)(2,1)S(1)}, u32[]{:S(2)}, u32[]{:S(2)}) collective-permute-start(bf16[1040,384]{1,0:T(8,128)(2,1)S(1)} %fold_spectra.5.part_ref), channel_id=1, source_target_pairs={{0,1},{1,0},{3,2},{2,3},{4,5},{5,4},{7,6},{6,7},{8,9},{9,8},{11,10... | collective-permute-start | bytes 2396168 | tf_op jit(solution)/shard_map/ppermute | solution.py:851
  192.9 12.2 %collective-permute-start.10 = (bf16[1024,384]{1,0:T(8,128)(2,1)}, bf16[1024,384]{1,0:T(8,128)(2,1)S(1)}, u32[]{:S(2)}, u32[]{:S(2)}) collective-permute-start(bf16[1024,384]{1,0:T(8,128)(2,1)} %get-tuple-element.296), channel_id=1, source_target_pairs={{0,16},{16,0},{1,17},{17,1},{2,18},{18,2},{3,19},{19,3},{4,20},{20... | collective-permute-start | bytes 2359304 | tf_op jit(solution)/shard_map/ppermute | solution.py:28
  208.7 26.7 %collective-permute-start.12 = (bf16[2,2,384,768]{3,2,1,0:T(8,128)(2,1)}, bf16[2,2,384,768]{3,2,1,0:T(8,128)(2,1)}, u32[]{:S(2)}, u32[]{:S(2)}) collective-permute-start(bf16[2,2,384,768]{3,2,1,0:T(8,128)(2,1)} %get-tuple-element.315), channel_id=1, source_target_pairs={{0,16},{16,0},{1,17},{17,1},{2,18},{18,2},{3,19},{19,3},{4,20},{20... | collective-permute-start | bytes 7077896 | tf_op jit(solution)/shard_map/ppermute | solution.py:28
  209.1 78.1 %collective-permute-start.11 = (bf16[2,2,384,768]{3,2,1,0:T(8,128)(2,1)}, bf16[2,2,384,768]{3,2,1,0:T(8,128)(2,1)}, u32[]{:S(2)}, u32[]{:S(2)}) collective-permute-start(bf16[2,2,384,768]{3,2,1,0:T(8,128)(2,1)} %get-tuple-element.313), channel_id=1, source_target_pairs={{0,16},{16,0},{1,17},{17,1},{2,18},{18,2},{3,19},{19,3},{4,20},{20... | collective-permute-start | bytes 7077896 | tf_op jit(solution)/shard_map/ppermute | solution.py:28
  209.3 20.2 %collective-permute-start.13 = (bf16[1040,384]{1,0:T(8,128)(2,1)S(1)}, bf16[1040,384]{1,0:T(8,128)(2,1)}, u32[]{:S(2)}, u32[]{:S(2)}) collective-permute-start(bf16[1040,384]{1,0:T(8,128)(2,1)S(1)} %fold_spectra.6.part_ref), channel_id=1, source_target_pairs={{0,1},{1,0},{3,2},{2,3},{4,5},{5,4},{7,6},{6,7},{8,9},{9,8},{11,10... | collective-permute-start | bytes 2396168 | tf_op jit(solution)/shard_map/ppermute | solution.py:851
  239.4 47.8 %collective-permute-start.14 = (bf16[2,384,768]{2,1,0:T(8,128)(2,1)}, bf16[2,384,768]{2,1,0:T(8,128)(2,1)S(1)}, u32[]{:S(2)}, u32[]{:S(2)}) collective-permute-start(bf16[2,384,768]{2,1,0:T(8,128)(2,1)} %get-tuple-element.322), channel_id=1, source_target_pairs={{0,4},{4,0},{8,12},{12,8},{1,5},{5,1},{9,13},{13,9},{2,6},{6,2},{1... | collective-permute-start | bytes 3538952 | tf_op jit(solution)/shard_map/ppermute | solution.py:689
  240.9 46.4 %collective-permute-start.15 = (bf16[2,384,768]{2,1,0:T(8,128)(2,1)}, bf16[2,384,768]{2,1,0:T(8,128)(2,1)S(1)}, u32[]{:S(2)}, u32[]{:S(2)}) collective-permute-start(bf16[2,384,768]{2,1,0:T(8,128)(2,1)} %get-tuple-element.323), channel_id=1, source_target_pairs={{0,8},{4,12},{8,0},{12,4},{1,9},{5,13},{9,1},{13,5},{2,10},{6,14},... | collective-permute-start | bytes 3538952 | tf_op jit(solution)/shard_map/ppermute | solution.py:689
  242.4 50.5 %collective-permute-start.9 = (bf16[1024,768]{1,0:T(8,128)(2,1)}, bf16[1024,768]{1,0:T(8,128)(2,1)}, u32[]{:S(2)}, u32[]{:S(2)}) collective-permute-start(bf16[1024,768]{1,0:T(8,128)(2,1)} %get-tuple-element.345), channel_id=1, source_target_pairs={{16,3},{17,2},{2,17},{3,16},{20,7},{21,6},{6,21},{7,20},{24,11},{2... | collective-permute-start | bytes 4718600 | tf_op jit(solution)/shard_map/ppermute | solution.py:817
  297.3 15.8 %collective-permute-start.19 = (bf16[384,768]{1,0:T(8,128)(2,1)}, bf16[384,768]{1,0:T(8,128)(2,1)S(1)}, u32[]{:S(2)}, u32[]{:S(2)}) collective-permute-start(bf16[384,768]{1,0:T(8,128)(2,1)} %get-tuple-element.358), channel_id=1, source_target_pairs={{0,8},{4,12},{8,0},{12,4},{1,9},{5,13},{9,1},{13,5},{2,10},{6,14},... | collective-permute-start | bytes 1769480 | tf_op jit(solution)/shard_map/ppermute | solution.py:689
  297.8 15.4 %collective-permute-start.20 = (bf16[384,768]{1,0:T(8,128)(2,1)S(1)}, bf16[384,768]{1,0:T(8,128)(2,1)}, u32[]{:S(2)}, u32[]{:S(2)}) collective-permute-start(bf16[384,768]{1,0:T(8,128)(2,1)S(1)} %get-tuple-element.360), channel_id=1, source_target_pairs={{0,4},{4,0},{8,12},{12,8},{1,5},{5,1},{9,13},{13,9},{2,6},{6,2},{1... | collective-permute-start | bytes 1769480 | tf_op jit(solution)/shard_map/ppermute | solution.py:689
  298.4 16.4 %collective-permute-start.18 = (f32[2,6912]{1,0:T(2,128)S(1)}, f32[2,6912]{1,0:T(2,128)S(1)}, u32[]{:S(2)}, u32[]{:S(2)}) collective-permute-start(f32[2,6912]{1,0:T(2,128)S(1)} %pad_maximum_fusion.10), channel_id=1, source_target_pairs={{0,16},{16,0},{1,17},{17,1},{2,18},{18,2},{3,19},{19,3},{4,20},{20... | collective-permute-start | bytes 165896 | tf_op jit(solution)/shard_map/ppermute | solution.py:931
  314.8 34.9 %collective-permute-start.22 = (bf16[2,2,384,768]{3,2,1,0:T(8,128)(2,1)}, bf16[2,2,384,768]{3,2,1,0:T(8,128)(2,1)S(1)}, u32[]{:S(2)}, u32[]{:S(2)}) collective-permute-start(bf16[2,2,384,768]{3,2,1,0:T(8,128)(2,1)} %get-tuple-element.377), channel_id=1, source_target_pairs={{0,16},{16,0},{1,17},{17,1},{2,18},{18,2},{3,19},{19,3},{4,20},{20... | collective-permute-start | bytes 7077896 | tf_op jit(solution)/shard_map/ppermute | solution.py:28
  315.8 33.9 %collective-permute-start.23 = (bf16[2,384,768]{2,1,0:T(8,128)(2,1)S(1)}, bf16[2,384,768]{2,1,0:T(8,128)(2,1)S(1)}, u32[]{:S(2)}, u32[]{:S(2)}) collective-permute-start(bf16[2,384,768]{2,1,0:T(8,128)(2,1)S(1)} %copy-done.33), channel_id=1, source_target_pairs={{0,4},{4,0},{8,12},{12,8},{1,5},{5,1},{9,13},{13,9},{2,6},{6,2},{1... | collective-permute-start | bytes 3538952 | tf_op jit(solution)/shard_map/ppermute | solution.py:689
  316.4 33.3 %collective-permute-start.24 = (bf16[2,384,768]{2,1,0:T(8,128)(2,1)S(1)}, bf16[2,384,768]{2,1,0:T(8,128)(2,1)S(1)}, u32[]{:S(2)}, u32[]{:S(2)}) collective-permute-start(bf16[2,384,768]{2,1,0:T(8,128)(2,1)S(1)} %copy-done.32), channel_id=1, source_target_pairs={{0,8},{4,12},{8,0},{12,4},{1,9},{5,13},{9,1},{13,5},{2,10},{6,14},... | collective-permute-start | bytes 3538952 | tf_op jit(solution)/shard_map/ppermute | solution.py:689
  317.9 11.8 %collective-permute-start.26 = (bf16[2,96,768]{2,1,0:T(8,128)(2,1)S(1)}, bf16[2,96,768]{2,1,0:T(8,128)(2,1)S(1)}, u32[]{:S(2)}, u32[]{:S(2)}) collective-permute-start(bf16[2,96,768]{2,1,0:T(8,128)(2,1)S(1)} %get-tuple-element.382), channel_id=1, source_target_pairs={{0,1},{1,2},{2,3},{3,0},{4,5},{5,6},{6,7},{7,4},{8,9},{9,10},{10,1... | collective-permute-start | bytes 884744 | tf_op jit(solution)/shard_map/ppermute | solution.py:719
  318.1 22.3 %collective-permute-start.27 = (bf16[2,96,768]{2,1,0:T(8,128)(2,1)S(1)}, bf16[2,96,768]{2,1,0:T(8,128)(2,1)S(1)}, u32[]{:S(2)}, u32[]{:S(2)}) collective-permute-start(bf16[2,96,768]{2,1,0:T(8,128)(2,1)S(1)} %get-tuple-element.383), channel_id=1, source_target_pairs={{0,2},{1,3},{2,0},{3,1},{4,6},{5,7},{6,4},{7,5},{8,10},{9,11},{10,... | collective-permute-start | bytes 884744 | tf_op jit(solution)/shard_map/ppermute | solution.py:719
  329.7 17.2 %collective-permute-start.28 = (bf16[2,96,768]{2,1,0:T(8,128)(2,1)S(1)}, bf16[2,96,768]{2,1,0:T(8,128)(2,1)S(1)}, u32[]{:S(2)}, u32[]{:S(2)}) collective-permute-start(bf16[2,96,768]{2,1,0:T(8,128)(2,1)S(1)} %get-tuple-element.384), channel_id=1, source_target_pairs={{0,3},{1,0},{2,1},{3,2},{4,7},{5,4},{6,5},{7,6},{8,11},{9,8},{10,9... | collective-permute-start | bytes 884744 | tf_op jit(solution)/shard_map/ppermute | solution.py:719
  354.7 12.2 %collective-permute-start.30 = (bf16[2,96,768]{2,1,0:T(8,128)(2,1)}, bf16[2,96,768]{2,1,0:T(8,128)(2,1)}, u32[]{:S(2)}, u32[]{:S(2)}) collective-permute-start(bf16[2,96,768]{2,1,0:T(8,128)(2,1)} %add_convert_fusion.10), channel_id=1, source_target_pairs={{0,1},{1,2},{2,3},{3,0},{4,5},{5,6},{6,7},{7,4},{8,9},{9,10},{10,1... | collective-permute-start | bytes 884744 | tf_op jit(solution)/shard_map/ppermute | solution.py:719
  356.7 18.3 %collective-permute-start.31 = (bf16[2,96,768]{2,1,0:T(8,128)(2,1)}, bf16[2,96,768]{2,1,0:T(8,128)(2,1)}, u32[]{:S(2)}, u32[]{:S(2)}) collective-permute-start(bf16[2,96,768]{2,1,0:T(8,128)(2,1)} %add_convert_fusion.10), channel_id=1, source_target_pairs={{0,2},{1,3},{2,0},{3,1},{4,6},{5,7},{6,4},{7,5},{8,10},{9,11},{10,... | collective-permute-start | bytes 884744 | tf_op jit(solution)/shard_map/ppermute | solution.py:719
  360.7 14.3 %collective-permute-start.32 = (bf16[2,96,768]{2,1,0:T(8,128)(2,1)}, bf16[2,96,768]{2,1,0:T(8,128)(2,1)}, u32[]{:S(2)}, u32[]{:S(2)}) collective-permute-start(bf16[2,96,768]{2,1,0:T(8,128)(2,1)} %add_convert_fusion.10), channel_id=1, source_target_pairs={{0,3},{1,0},{2,1},{3,2},{4,7},{5,4},{6,5},{7,6},{8,11},{9,8},{10,9... | collective-permute-start | bytes 884744 | tf_op jit(solution)/shard_map/ppermute | solution.py:719
  362.9 23.6 %collective-permute-start.29 = (bf16[1024,384]{1,0:T(8,128)(2,1)}, bf16[1024,384]{1,0:T(8,128)(2,1)}, u32[]{:S(2)}, u32[]{:S(2)}) collective-permute-start(bf16[1024,384]{1,0:T(8,128)(2,1)} %get-tuple-element.394), channel_id=1, source_target_pairs={{0,16},{16,0},{1,17},{17,1},{2,18},{18,2},{3,19},{19,3},{4,20},{20... | collective-permute-start | bytes 2359304 | tf_op jit(solution)/shard_map/ppermute | solution.py:28
  378.3 14.9 %collective-permute-start.38 = (bf16[4,96,768]{2,1,0:T(8,128)(2,1)S(1)}, bf16[4,96,768]{2,1,0:T(8,128)(2,1)S(1)}, u32[]{:S(2)}, u32[]{:S(2)}) collective-permute-start(bf16[4,96,768]{2,1,0:T(8,128)(2,1)S(1)} %pad_maximum_fusion.6), channel_id=1, source_target_pairs={{0,8},{4,12},{8,0},{12,4},{1,9},{5,13},{9,1},{13,5},{2,10},{6,14},... | collective-permute-start | bytes 1769480 | tf_op jit(solution)/shard_map/ppermute | solution.py:689
  379.9 14.7 %collective-permute-start.39 = (bf16[4,96,768]{2,1,0:T(8,128)(2,1)S(1)}, bf16[4,96,768]{2,1,0:T(8,128)(2,1)S(1)}, u32[]{:S(2)}, u32[]{:S(2)}) collective-permute-start(bf16[4,96,768]{2,1,0:T(8,128)(2,1)S(1)} %pad_maximum_fusion.7), channel_id=1, source_target_pairs={{0,4},{4,0},{8,12},{12,8},{1,5},{5,1},{9,13},{13,9},{2,6},{6,2},{1... | collective-permute-start | bytes 1769480 | tf_op jit(solution)/shard_map/ppermute | solution.py:689
  380.5 14.3 %collective-permute-start.35 = (bf16[2,96,768]{2,1,0:T(8,128)(2,1)S(1)}, bf16[2,96,768]{2,1,0:T(8,128)(2,1)S(1)}, u32[]{:S(2)}, u32[]{:S(2)}) collective-permute-start(bf16[2,96,768]{2,1,0:T(8,128)(2,1)S(1)} %get-tuple-element.414), channel_id=1, source_target_pairs={{0,1},{1,2},{2,3},{3,0},{4,5},{5,6},{6,7},{7,4},{8,9},{9,10},{10,1... | collective-permute-start | bytes 884744 | tf_op jit(solution)/shard_map/ppermute | solution.py:719
  384.2 19.3 %collective-permute-start.36 = (bf16[2,96,768]{2,1,0:T(8,128)(2,1)S(1)}, bf16[2,96,768]{2,1,0:T(8,128)(2,1)S(1)}, u32[]{:S(2)}, u32[]{:S(2)}) collective-permute-start(bf16[2,96,768]{2,1,0:T(8,128)(2,1)S(1)} %get-tuple-element.415), channel_id=1, source_target_pairs={{0,2},{1,3},{2,0},{3,1},{4,6},{5,7},{6,4},{7,5},{8,10},{9,11},{10,... | collective-permute-start | bytes 884744 | tf_op jit(solution)/shard_map/ppermute | solution.py:719
  386.5 16.9 %collective-permute-start.37 = (bf16[2,96,768]{2,1,0:T(8,128)(2,1)S(1)}, bf16[2,96,768]{2,1,0:T(8,128)(2,1)S(1)}, u32[]{:S(2)}, u32[]{:S(2)}) collective-permute-start(bf16[2,96,768]{2,1,0:T(8,128)(2,1)S(1)} %get-tuple-element.416), channel_id=1, source_target_pairs={{0,3},{1,0},{2,1},{3,2},{4,7},{5,4},{6,5},{7,6},{8,11},{9,8},{10,9... | collective-permute-start | bytes 884744 | tf_op jit(solution)/shard_map/ppermute | solution.py:719
  393.2 18.2 %collective-permute-start.40 = (f32[2,6912]{1,0:T(2,128)S(1)}, f32[2,6912]{1,0:T(2,128)S(1)}, u32[]{:S(2)}, u32[]{:S(2)}) collective-permute-start(f32[2,6912]{1,0:T(2,128)S(1)} %copy-done.36), channel_id=1, source_target_pairs={{0,2},{1,3},{2,0},{3,1},{4,6},{5,7},{6,4},{7,5},{8,10},{9,11},{10,... | collective-permute-start | bytes 165896 | tf_op jit(solution)/shard_map/ppermute | solution.py:931
  411.5 11.9 %collective-permute-start.41 = (bf16[2,96,768]{2,1,0:T(8,128)(2,1)S(1)}, bf16[2,96,768]{2,1,0:T(8,128)(2,1)S(1)}, u32[]{:S(2)}, u32[]{:S(2)}) collective-permute-start(bf16[2,96,768]{2,1,0:T(8,128)(2,1)S(1)} %add_convert_fusion.9), channel_id=1, source_target_pairs={{0,1},{1,2},{2,3},{3,0},{4,5},{5,6},{6,7},{7,4},{8,9},{9,10},{10,1... | collective-permute-start | bytes 884744 | tf_op jit(solution)/shard_map/ppermute | solution.py:719
  411.5 23.5 %collective-permute-start.42 = (bf16[2,96,768]{2,1,0:T(8,128)(2,1)S(1)}, bf16[2,96,768]{2,1,0:T(8,128)(2,1)S(1)}, u32[]{:S(2)}, u32[]{:S(2)}) collective-permute-start(bf16[2,96,768]{2,1,0:T(8,128)(2,1)S(1)} %add_convert_fusion.9), channel_id=1, source_target_pairs={{0,2},{1,3},{2,0},{3,1},{4,6},{5,7},{6,4},{7,5},{8,10},{9,11},{10,... | collective-permute-start | bytes 884744 | tf_op jit(solution)/shard_map/ppermute | solution.py:719
  411.8 23.2 %collective-permute-start.43 = (bf16[2,96,768]{2,1,0:T(8,128)(2,1)S(1)}, bf16[2,96,768]{2,1,0:T(8,128)(2,1)S(1)}, u32[]{:S(2)}, u32[]{:S(2)}) collective-permute-start(bf16[2,96,768]{2,1,0:T(8,128)(2,1)S(1)} %add_convert_fusion.9), channel_id=1, source_target_pairs={{0,3},{1,0},{2,1},{3,2},{4,7},{5,4},{6,5},{7,6},{8,11},{9,8},{10,9... | collective-permute-start | bytes 884744 | tf_op jit(solution)/shard_map/ppermute | solution.py:719
  415.7 27.4 %collective-permute-start.45 = (bf16[2,4,96,768]{3,2,1,0:T(8,128)(2,1)S(1)}, bf16[2,4,96,768]{3,2,1,0:T(8,128)(2,1)S(1)}, u32[]{:S(2)}, u32[]{:S(2)}) collective-permute-start(bf16[2,4,96,768]{3,2,1,0:T(8,128)(2,1)S(1)} %pad_maximum_fusion.2.refs_4_), channel_id=1, source_target_pairs={{0,4},{4,0},{8,12},{12,8},{1,5},{5,1},{9,13},{13,9},{2,6},{6,2},{1... | collective-permute-start | bytes 3538952 | tf_op jit(solution)/shard_map/ppermute | solution.py:689
  417.0 27.0 %collective-permute-start.46 = (bf16[2,4,96,768]{3,2,1,0:T(8,128)(2,1)S(1)}, bf16[2,4,96,768]{3,2,1,0:T(8,128)(2,1)S(1)}, u32[]{:S(2)}, u32[]{:S(2)}) collective-permute-start(bf16[2,4,96,768]{3,2,1,0:T(8,128)(2,1)S(1)} %pad_maximum_fusion.3.refs_5_), channel_id=1, source_target_pairs={{0,8},{4,12},{8,0},{12,4},{1,9},{5,13},{9,1},{13,5},{2,10},{6,14},... | collective-permute-start | bytes 3538952 | tf_op jit(solution)/shard_map/ppermute | solution.py:689
  435.2 23.2 %collective-permute-start.44 = (bf16[1040,384]{1,0:T(8,128)(2,1)S(1)}, bf16[1040,384]{1,0:T(8,128)(2,1)S(1)}, u32[]{:S(2)}, u32[]{:S(2)}) collective-permute-start(bf16[1040,384]{1,0:T(8,128)(2,1)S(1)} %fold_spectra.7.part_ref), channel_id=1, source_target_pairs={{0,1},{1,0},{3,2},{2,3},{4,5},{5,4},{7,6},{6,7},{8,9},{9,8},{11,10... | collective-permute-start | bytes 2396168 | tf_op jit(solution)/shard_map/ppermute | solution.py:851
  444.0 13.5 %collective-permute-start.47 = (bf16[4,96,768]{2,1,0:T(8,128)(2,1)S(1)}, bf16[4,96,768]{2,1,0:T(8,128)(2,1)S(1)}, u32[]{:S(2)}, u32[]{:S(2)}) collective-permute-start(bf16[4,96,768]{2,1,0:T(8,128)(2,1)S(1)} %pad_maximum_fusion.8), channel_id=1, source_target_pairs={{0,8},{4,12},{8,0},{12,4},{1,9},{5,13},{9,1},{13,5},{2,10},{6,14},... | collective-permute-start | bytes 1769480 | tf_op jit(solution)/shard_map/ppermute | solution.py:689
  444.7 13.2 %collective-permute-start.48 = (bf16[4,96,768]{2,1,0:T(8,128)(2,1)S(1)}, bf16[4,96,768]{2,1,0:T(8,128)(2,1)S(1)}, u32[]{:S(2)}, u32[]{:S(2)}) collective-permute-start(bf16[4,96,768]{2,1,0:T(8,128)(2,1)S(1)} %pad_maximum_fusion.9), channel_id=1, source_target_pairs={{0,4},{4,0},{8,12},{12,8},{1,5},{5,1},{9,13},{13,9},{2,6},{6,2},{1... | collective-permute-start | bytes 1769480 | tf_op jit(solution)/shard_map/ppermute | solution.py:689
  445.2 20.9 %collective-permute-start.53 = (bf16[2,4,96,768]{3,2,1,0:T(8,128)(2,1)S(1)}, bf16[2,4,96,768]{3,2,1,0:T(8,128)(2,1)S(1)}, u32[]{:S(2)}, u32[]{:S(2)}) collective-permute-start(bf16[2,4,96,768]{3,2,1,0:T(8,128)(2,1)S(1)} %pad_maximum_fusion.2.refs_4_), channel_id=1, source_target_pairs={{0,16},{1,17},{2,18},{3,19},{4,20},{5,21},{6,22},{7,23},{8,24},{9,... | collective-permute-start | bytes 3538952 | tf_op jit(solution)/shard_map/ppermute | solution.py:969
  466.1 28.6 %collective-permute-start.56 = (bf16[2,4,96,768]{3,2,1,0:T(8,128)(2,1)S(1)}, bf16[2,4,96,768]{3,2,1,0:T(8,128)(2,1)S(1)}, u32[]{:S(2)}, u32[]{:S(2)}) collective-permute-start(bf16[2,4,96,768]{3,2,1,0:T(8,128)(2,1)S(1)} %pad_maximum_fusion.4.refs_0_), channel_id=1, source_target_pairs={{0,4},{4,0},{8,12},{12,8},{1,5},{5,1},{9,13},{13,9},{2,6},{6,2},{1... | collective-permute-start | bytes 3538952 | tf_op jit(solution)/shard_map/ppermute | solution.py:689
  467.4 28.8 %collective-permute-start.57 = (bf16[2,4,96,768]{3,2,1,0:T(8,128)(2,1)S(1)}, bf16[2,4,96,768]{3,2,1,0:T(8,128)(2,1)S(1)}, u32[]{:S(2)}, u32[]{:S(2)}) collective-permute-start(bf16[2,4,96,768]{3,2,1,0:T(8,128)(2,1)S(1)} %pad_maximum_fusion.5.refs_1_), channel_id=1, source_target_pairs={{0,8},{4,12},{8,0},{12,4},{1,9},{5,13},{9,1},{13,5},{2,10},{6,14},... | collective-permute-start | bytes 3538952 | tf_op jit(solution)/shard_map/ppermute | solution.py:689
  470.4 37.6 %collective-permute-start.50 = (bf16[1024,768]{1,0:T(8,128)(2,1)S(1)}, bf16[1024,768]{1,0:T(8,128)(2,1)S(1)}, u32[]{:S(2)}, u32[]{:S(2)}) collective-permute-start(bf16[1024,768]{1,0:T(8,128)(2,1)S(1)} %finish.1), channel_id=1, source_target_pairs={{16,3},{17,2},{2,17},{3,16},{20,7},{21,6},{6,21},{7,20},{24,11},{2... | collective-permute-start | bytes 4718600 | tf_op jit(solution)/shard_map/ppermute | solution.py:817
  471.2 27.7 %collective-permute-start.60 = (bf16[2,4,96,768]{3,2,1,0:T(8,128)(2,1)S(1)}, bf16[2,4,96,768]{3,2,1,0:T(8,128)(2,1)S(1)}, u32[]{:S(2)}, u32[]{:S(2)}) collective-permute-start(bf16[2,4,96,768]{3,2,1,0:T(8,128)(2,1)S(1)} %collective-permute-done.45.refs_4_), channel_id=1, source_target_pairs={{0,16},{1,17},{2,18},{3,19},{4,20},{5,21},{6,22},{7,23},{8,24},{9,... | collective-permute-start | bytes 3538952 | tf_op jit(solution)/shard_map/ppermute | solution.py:976
  475.1 24.6 %collective-permute-start.61 = (bf16[2,4,96,768]{3,2,1,0:T(8,128)(2,1)S(1)}, bf16[2,4,96,768]{3,2,1,0:T(8,128)(2,1)S(1)}, u32[]{:S(2)}, u32[]{:S(2)}) collective-permute-start(bf16[2,4,96,768]{3,2,1,0:T(8,128)(2,1)S(1)} %collective-permute-done.46.refs_5_), channel_id=1, source_target_pairs={{0,16},{1,17},{2,18},{3,19},{4,20},{5,21},{6,22},{7,23},{8,24},{9,... | collective-permute-start | bytes 3538952 | tf_op jit(solution)/shard_map/ppermute | solution.py:976
  (79 other events, 693.0 us)
Sparse Core Ops, SparseCore 0:
  9.6 24.5 all-gather.2
  35.7 23.0 all-gather.4

commit v4 on v3

--- a/solution.py
+++ b/solution.py
@@ -548,19 +548,24 @@
     rows, width = low.shape
     half = width // 2
 
-    def body(scalar_ref, act_ref, gb_ref, low_ref, gp_ref, sent_ref, kept_ref):
+    def body(scalar_ref, act_ref, gb_ref, low_ref, gp_ref, *refs):
         outer = contract(act_ref[...], gb_ref[...], 0, 0).astype(BF)
         inner = contract(low_ref[...], gp_ref[...], 0, 0).astype(BF)
 
-        @pl.when(pl.program_id(0) < 2)
-        def _():
-            sent_ref[0, 0] = outer
-            sent_ref[1, 0] = inner
-
-        @pl.when(pl.program_id(0) >= 2)
-        def _():
-            kept_ref[0, 0] = outer
-            kept_ref[1, 0] = inner
+        def write(mine, theirs):
+            mine[0, 0], mine[1, 0] = outer[part], inner[part]
+            theirs[0, 0], theirs[1, 0] = outer[rest], inner[rest]
+
+        for core in range(2):
+            part, rest = slice(core * half, (core + 1) * half), slice((1 - core) * half, (2 - core) * half)
+
+            @pl.when((scalar_ref[0] == core) & (pl.program_id(0) < 2))
+            def _():
+                write(refs[0], refs[2])
+
+            @pl.when((scalar_ref[0] == core) & (pl.program_id(0) >= 2))
+            def _():
+                write(refs[1], refs[3])
 
     def out_square(i, s):
         return ((2 * i + 1 - i // 2) % 4) ^ s[1]
@@ -568,25 +573,24 @@
     def in_square(i, s):
         return ((i + 2) % 4) ^ s[1]
 
+    sent = pl.BlockSpec((2, 1, half, width), lambda i, s: (0, jnp.minimum(i, 1), 0, 0))
+    held = pl.BlockSpec((2, 1, half, width), lambda i, s: (0, jnp.maximum(i - 2, 0), 0, 0))
     return pl.pallas_call(
         body,
         grid_spec=pltpu.PrefetchScalarGridSpec(
             num_scalar_prefetch=1,
             grid=(4,),
             in_specs=[
-                pl.BlockSpec((rows, half), lambda i, s: (0, 2 * out_square(i, s) + s[0])),
+                pl.BlockSpec((rows, width), lambda i, s: (0, out_square(i, s))),
                 pl.BlockSpec((rows, width), lambda i, s: (0, 0)),
-                pl.BlockSpec((rows, half), lambda i, s: (0, s[0])),
+                pl.BlockSpec((rows, width), lambda i, s: (0, 0)),
                 pl.BlockSpec((rows, width), lambda i, s: (0, in_square(i, s))),
             ],
-            out_specs=[
-                pl.BlockSpec((2, 1, half, width), lambda i, s: (0, jnp.minimum(i, 1), 0, 0)),
-                pl.BlockSpec((2, 1, half, width), lambda i, s: (0, jnp.maximum(i - 2, 0), 0, 0)),
-            ],
+            out_specs=[sent, held, sent, held],
         ),
-        out_shape=[like(2, 2, half, width)] * 2,
+        out_shape=[like(2, 2, half, width)] * 4,
         compiler_params=pltpu.CompilerParams(vmem_limit_bytes=58 << 20),
-        cost_estimate=pl.CostEstimate(flops=16 * rows * width * half // COST, bytes_accessed=20 * rows * width // COST, transcendentals=0),
+        cost_estimate=pl.CostEstimate(flops=16 * rows * width * width // COST, bytes_accessed=20 * rows * width // COST, transcendentals=0),
         name="grad_blocks",
     )(scalars, act, gb, low, gp)
 
@@ -891,10 +895,6 @@
         return jnp.concatenate([wide.reshape(-1), narrow[:5].reshape(-1)])
 
     late, early = ChipSum(), ChipSum()
-    to_theirs = jnp.stack([1 - core, index]).astype(jnp.int32)
-
-    def blocks_of(target, gp, gb):
-        return line(grad_blocks, target, kept[1][0], gp, kept[1][1], gb)
 
     out_moved = give_start(x)
     grad, gb, gp, own, other, wide1, narrow1 = line(
@@ -902,17 +902,18 @@
     )
 
     came = swap_cores(other)
-    other_sent, other_kept = blocks_of(to_theirs, gp, gb)
     folded = fold(own, came)
 
     parts = spread_out(line.after(folded))
-    got_sent, got_kept1 = swap_cores(line.after((other_sent, other_kept)))
-    my_sent, my_kept1 = blocks_of(scalars, gp, gb)
+    my_sent, my_kept1, other_sent, other_kept = line(grad_blocks, scalars, kept[1][0], gp, kept[1][1], gb)
     begun = part(folded)
     mixed = rest(begun, parts)
 
     came = swap_cores(mixed)
-    sent = run(early.sent(my_sent, got_sent))
+    got_sent = swap_cores(line.after(other_sent))
+    add_sent, parts = early.sent(my_sent, got_sent)
+    sent = line(lambda a, b, _: add_sent(a, b), *parts, came)
+    got_kept1 = swap_cores(line.after(other_kept))
 
     early.start_first(line.after(sent))
     grad, own, other, wide0, narrow0, my_sent, my_kept, other_sent, other_kept = back(0, grad, (mixed, came))

time: 534 us -> 527 us (0.987)
    ppermute x15, waiting for transfers between devices: 9.51 us -> 15.1 us  [swap_cores(): return lax.ppermute(value, 'pipe', [(0, 1), (1, 0)])]
    pallas_call x2 -> x1, Pallas kernels: 22.9 us -> 18.1 us  [grad_blocks(): pl.pallas_call(body, grid_spec=pltpu.PrefetchScalarGridSpec(num_scalar_pr...]
  transfers between devices with their start and end apart: 66 -> 66, of which waited for: 29 -> 29; matrix products, arithmetic and copies ran while one was open for 12% -> 11% of each run, Pallas kernels for 23% -> 21%
where the time goes in v4:
time: 527 us; the launch traced here: 518 us
  Pallas kernels  163 us (31%)
  waiting for transfers between devices  138 us (26%)
  starting transfers between devices  110 us (21%)
  other arithmetic  46.5 us (9%)
  local copies, waits for them, and re-layouts  31.1 us (6%)
  between operations  15.8 us (3%)
  matrix products  13.7 us (3%)
    pallas_call x2, Pallas kernels, forward(): call(body, (rows // tile,), [scalar_block(), row_block(tile, width)] + mi...  49 us
    ppermute x12, waiting for transfers between devices, along(): lax.ppermute(value, 'seq', [(i, (i + by) % self.peers) for i in range(sel...  45.7 us
    pallas_call x1, Pallas kernels, backward(): call(body, (rows // tile,), [scalar_block(), row_block(tile, width)] + ex...  39.1 us
    ppermute x16, waiting for transfers between devices, across(): return lax.ppermute(value, 'dp', bit_pairs(self.count, bit))  38.8 us
    ppermute x4, starting transfers between devices, spread_out(): return [lax.ppermute(folded, 'seq', pairs) for pairs in group_shifts]  24.7 us
    unnamed x127, local copies, waits for them, and re-layouts  21.5 us
    ppermute x4, waiting for transfers between devices, spread_out(): return [lax.ppermute(folded, 'seq', pairs) for pairs in group_shifts]  21.4 us
    pallas_call x1, Pallas kernels, backward_last(): call(body, (rows // tile,), [row_block(tile, width), row_block(tile, hidd...  21.4 us
  transfers between devices with their start and end apart: 66, of which 29 were waited for; matrix products, arithmetic and copies ran while one was open for 11% of the time, Pallas kernels for 21%

profile of v4, /device:TPU:0, one launch (start us, length us, event | category | flops | bytes accessed | tf_op | source)
XLA Modules:
  0.0 517.7 jit_solution(11575850860374173208)
XLA Ops:
  13.2 5.3 %collective-permute-start.4 = (f32[6912]{0:T(1024)S(1)}, f32[6912]{0:T(1024)S(1)}, u32[]{:S(2)}, u32[]{:S(2)}) collective-permute-start(f32[6912]{0:T(1024)S(1)} %constant_dynamic-update-slice_fusion), channel_id=1, source_target_pairs={{0,16},{16,0},{1,17},{17,1},{2,18},{18,2},{3,19},{19,3},{4,20},{20... | collective-permute-start | bytes 82952 | tf_op jit(solution)/shard_map/ppermute | solution.py:28
  18.7 11.8 %select_convert_fusion = (bf16[768,768]{1,0:T(8,128)(2,1)}, bf16[768,768]{1,0:T(8,128)(2,1)S(1)}) fusion(s32[768]{0:T(1024)S(1)} %get-tuple-element.541, s32[768]{0:T(1024)S(1)} %get-tuple-element.542, f32[]{:T(128)S(6)} %select_n.299, pred[768]{0:T(1024)(128)(4,1)S(1)} %select_compare_fusion, f32[]{:T(128)S(6)} %neg.3), kind=kLoop, calls=%fused_computation.23 | loop fusion | flops 12976128 | bytes 2366216 | tf_op jit(solution)/shard_map/convert_element_type | solution.py:64
  32.7 2.8 spectra.1
  35.5 7.6 %collective-permute-start.1 = (bf16[1024,384]{1,0:T(8,128)(2,1)}, bf16[1024,384]{1,0:T(8,128)(2,1)S(1)}, u32[]{:S(2)}, u32[]{:S(2)}) collective-permute-start(bf16[1024,384]{1,0:T(8,128)(2,1)} %get-tuple-element.248), channel_id=1, source_target_pairs={{0,16},{16,0},{1,17},{17,1},{2,18},{18,2},{3,19},{19,3},{4,20},{20... | collective-permute-start | bytes 2359304 | tf_op jit(solution)/shard_map/ppermute | solution.py:28
  43.8 2.6 fusion.57
  46.8 16.8 %collective-permute-start.2 = (bf16[1040,384]{1,0:T(8,128)(2,1)S(1)}, bf16[1040,384]{1,0:T(8,128)(2,1)S(1)}, u32[]{:S(2)}, u32[]{:S(2)}) collective-permute-start(bf16[1040,384]{1,0:T(8,128)(2,1)S(1)} %fold_spectra.4.part_ref), channel_id=1, source_target_pairs={{0,1},{1,0},{3,2},{2,3},{4,5},{5,4},{7,6},{6,7},{8,9},{9,8},{11,10... | collective-permute-start | bytes 2396168 | tf_op jit(solution)/shard_map/ppermute | solution.py:855
  63.6 3.3 add_convert_fusion
  69.2 12.4 %collective-permute-done.2.refs_4_ = bf16[1040,384]{1,0:T(8,128)(2,1)S(1)} collective-permute-done((bf16[1040,384]{1,0:T(8,128)(2,1)S(1)}, bf16[1040,384]{1,0:T(8,128)(2,1)S(1)}, u32[]{:S(2)}, u32[]{:S(2)}) %collective-permute-start.2) | collective-permute-done | bytes 798752 | tf_op jit(solution)/shard_map/ppermute | solution.py:855
  89.8 24.6 %layer_forward.2 = (bf16[1024,768]{1,0:T(8,128)(2,1)}, bf16[1024,768]{1,0:T(8,128)(2,1)}, bf16[1024,3072]{1,0:T(8,128)(2,1)}, bf16[1024,3072]{1,0:T(8,128)(2,1)}...) custom-call(s32[1]{0:T(128)} %bitcast.core_ref.refs_0_, ...), custom_call_target="tpu_custom_call" | custom-call | flops 188743680 | bytes 516096 | tf_op jit(solution)/shard_map/layer_forward/pallas_call | solution.py:319
  114.4 3.3 collective-permute-start.5
  122.3 2.4 copy-done.1
  124.6 2.4 copy-done.4
  129.3 3.5 fusion.27.refs_0_
  132.8 8.7 %collective-permute-done.6.refs_4_ = bf16[1040,384]{1,0:T(8,128)(2,1)S(1)} collective-permute-done((bf16[1040,384]{1,0:T(8,128)(2,1)S(1)}, bf16[1040,384]{1,0:T(8,128)(2,1)S(1)}, u32[]{:S(2)}, u32[]{:S(2)}) %collective-permute-start.6) | collective-permute-done | bytes 798752 | tf_op jit(solution)/shard_map/ppermute | solution.py:855
  147.2 24.4 %layer_forward.3 = (bf16[1024,768]{1,0:T(8,128)(2,1)}, bf16[1024,768]{1,0:T(8,128)(2,1)}, bf16[1024,3072]{1,0:T(8,128)(2,1)}, bf16[1024,3072]{1,0:T(8,128)(2,1)}...) custom-call(s32[1]{0:T(128)} %bitcast.core_ref.refs_0_, ...), custom_call_target="tpu_custom_call" | custom-call | flops 188743680 | bytes 516096 | tf_op jit(solution)/shard_map/layer_forward/pallas_call | solution.py:319
  171.6 21.4 %last_backward.1 = (f32[1024,768]{1,0:T(8,128)}, bf16[1024,768]{1,0:T(8,128)(2,1)}, bf16[1024,3072]{1,0:T(8,128)(2,1)}, bf16[1024,384]{1,0:T(8,128)(2,1)}, bf16[...) custom-call(bf16[1024,768]{1,0:T(8,128)(2,1)} %fusion.27.refs_0_, ...), custom_call_target="tpu_custom_call" | custom-call | flops 188743680 | bytes 516096 | tf_op jit(solution)/shard_map/last_backward/pallas_call | solution.py:507
  193.2 2.4 collective-permute-done.10.recv_ref
  198.5 18.1 %grad_blocks.1 = (bf16[2,2,384,768]{3,2,1,0:T(8,128)(2,1)}, bf16[2,2,384,768]{3,2,1,0:T(8,128)(2,1)}, bf16[2,2,384,768]{3,2,1,0:T(8,128)(2,1)}, bf16[2,2,384,768]{3,2,1,0:T(8,128)(2,1)}) custom-call(s32[2]{0:T(128)} %pad_add_fusion.scalar_ref, bf16[1024,3072]{1,0:T(8,128)(2,1)} %get-tuple-element.296.act_ref, bf16[1024,768]{1,0:T(8,128)(2,1)} %get-tuple-element.297.gb_ref, ...), custom_call_target="tpu_custom_call" | custom-call | flops 150994944 | bytes 245760 | tf_op jit(solution)/shard_map/grad_blocks/pallas_call | solution.py:578
  223.7 3.6 transform_rest.6.refs_0_.refs_1_
  227.9 5.2 collective-permute-done.13.refs_2_.refs_3_
  240.1 39.1 %layer_backward.1 = (f32[1024,768]{1,0:T(8,128)}, bf16[1024,384]{1,0:T(8,128)(2,1)}, bf16[1024,384]{1,0:T(8,128)(2,1)}, f32[1,3072]{1,0:T(1,128)}, f32[8,768]{1,...) custom-call(s32[2]{0:T(128)} %pad_add_fusion.scalar_ref, ...), custom_call_target="tpu_custom_call" | custom-call | flops 377487360 | bytes 516096 | tf_op jit(solution)/shard_map/layer_backward/pallas_call | solution.py:423
  280.2 3.2 fusion.10
  284.3 2.8 broadcast_select_fusion.1
  290.8 3.1 collective-permute-done.17.recv_ref
  294.3 3.6 fusion.44
  297.9 7.6 %collective-permute-done.19 = bf16[384,768]{1,0:T(8,128)(2,1)S(1)} collective-permute-done((bf16[384,768]{1,0:T(8,128)(2,1)}, bf16[384,768]{1,0:T(8,128)(2,1)S(1)}, u32[]{:S(2)}, u32[]{:S(2)}) %collective-permute-start.19) | collective-permute-done | bytes 589856 | tf_op jit(solution)/shard_map/ppermute | solution.py:693
  310.4 2.5 collective-permute-start.27
  312.9 9.3 %collective-permute-done.26 = bf16[2,96,768]{2,1,0:T(8,128)(2,1)S(1)} collective-permute-done((bf16[2,96,768]{2,1,0:T(8,128)(2,1)S(1)}, bf16[2,96,768]{2,1,0:T(8,128)(2,1)S(1)}, u32[]{:S(2)}, u32[]{:S(2)}) %collective-permute-start.26) | collective-permute-done | bytes 294944 | tf_op jit(solution)/shard_map/ppermute | solution.py:723
  322.2 2.4 copy-done.2
  332.8 7.3 %collective-permute-start.25 = (f32[2,6912]{1,0:T(2,128)S(1)}, f32[2,6912]{1,0:T(2,128)S(1)}, u32[]{:S(2)}, u32[]{:S(2)}) collective-permute-start(f32[2,6912]{1,0:T(2,128)S(1)} %add.286), channel_id=1, source_target_pairs={{0,1},{1,0},{2,3},{3,2},{4,5},{5,4},{6,7},{7,6},{8,9},{9,8},{10,11... | collective-permute-start | bytes 165896 | tf_op jit(solution)/shard_map/ppermute | solution.py:932
  349.9 4.0 collective-permute-start.31
  360.2 8.0 %collective-permute-done.31 = bf16[2,96,768]{2,1,0:T(8,128)(2,1)} collective-permute-done((bf16[2,96,768]{2,1,0:T(8,128)(2,1)}, bf16[2,96,768]{2,1,0:T(8,128)(2,1)}, u32[]{:S(2)}, u32[]{:S(2)}) %collective-permute-start.31) | collective-permute-done | bytes 294944 | tf_op jit(solution)/shard_map/ppermute | solution.py:723
  373.6 3.8 collective-permute-start.35
  379.8 2.6 fusion.37
  382.4 2.7 fusion.38
  388.0 8.8 %collective-permute-done.36 = bf16[2,96,768]{2,1,0:T(8,128)(2,1)S(1)} collective-permute-done((bf16[2,96,768]{2,1,0:T(8,128)(2,1)S(1)}, bf16[2,96,768]{2,1,0:T(8,128)(2,1)S(1)}, u32[]{:S(2)}, u32[]{:S(2)}) %collective-permute-start.36) | collective-permute-done | bytes 294944 | tf_op jit(solution)/shard_map/ppermute | solution.py:723
  397.0 7.8 %collective-permute-done.40 = f32[2,6912]{1,0:T(2,128)S(1)} collective-permute-done((f32[2,6912]{1,0:T(2,128)S(1)}, f32[2,6912]{1,0:T(2,128)S(1)}, u32[]{:S(2)}, u32[]{:S(2)}) %collective-permute-start.40) | collective-permute-done | bytes 55328 | tf_op jit(solution)/shard_map/ppermute | solution.py:932
  405.4 3.6 collective-permute-start.43
  411.1 5.6 %collective-permute-done.41 = bf16[2,96,768]{2,1,0:T(8,128)(2,1)S(1)} collective-permute-done((bf16[2,96,768]{2,1,0:T(8,128)(2,1)S(1)}, bf16[2,96,768]{2,1,0:T(8,128)(2,1)S(1)}, u32[]{:S(2)}, u32[]{:S(2)}) %collective-permute-start.41) | collective-permute-done | bytes 294944 | tf_op jit(solution)/shard_map/ppermute | solution.py:723
  416.7 11.7 %collective-permute-done.42 = bf16[2,96,768]{2,1,0:T(8,128)(2,1)S(1)} collective-permute-done((bf16[2,96,768]{2,1,0:T(8,128)(2,1)S(1)}, bf16[2,96,768]{2,1,0:T(8,128)(2,1)S(1)}, u32[]{:S(2)}, u32[]{:S(2)}) %collective-permute-start.42) | collective-permute-done | bytes 294944 | tf_op jit(solution)/shard_map/ppermute | solution.py:723
  428.6 6.0 %collective-permute-start.44 = (bf16[1040,384]{1,0:T(8,128)(2,1)S(1)}, bf16[1040,384]{1,0:T(8,128)(2,1)S(1)}, u32[]{:S(2)}, u32[]{:S(2)}) collective-permute-start(bf16[1040,384]{1,0:T(8,128)(2,1)S(1)} %fold_spectra.7.part_ref), channel_id=1, source_target_pairs={{0,1},{1,0},{3,2},{2,3},{4,5},{5,4},{7,6},{6,7},{8,9},{9,8},{11,10... | collective-permute-start | bytes 2396168 | tf_op jit(solution)/shard_map/ppermute | solution.py:855
  440.1 10.9 %collective-permute-done.47 = bf16[4,96,768]{2,1,0:T(8,128)(2,1)S(1)} collective-permute-done((bf16[4,96,768]{2,1,0:T(8,128)(2,1)S(1)}, bf16[4,96,768]{2,1,0:T(8,128)(2,1)S(1)}, u32[]{:S(2)}, u32[]{:S(2)}) %collective-permute-start.47) | collective-permute-done | bytes 589856 | tf_op jit(solution)/shard_map/ppermute | solution.py:693
  454.3 2.5 collective-permute-start.54
  464.6 3.8 collective-permute-start.60
  469.9 4.6 write_weights.2
  474.5 13.6 %collective-permute-done.56.refs_0_ = bf16[2,4,96,768]{3,2,1,0:T(8,128)(2,1)S(1)} collective-permute-done((bf16[2,4,96,768]{3,2,1,0:T(8,128)(2,1)S(1)}, bf16[2,4,96,768]{3,2,1,0:T(8,128)(2,1)S(1)}, u32[]{:S(2)}, u32[]{:S(2)}) %collective-permute-start.56) | collective-permute-done | bytes 1179680 | tf_op jit(solution)/shard_map/ppermute | solution.py:693
  496.1 4.6 write_weights.3
  501.9 3.1 collective-permute-done.63
  (326 shorter events, 130.8 us)
Async XLA Ops:
  7.2 81.8 %all-gather.3.cloned.1.call-start = ((), (), s32[]{:S(2)}) async-start(), calls=%async_computation | async-start | bytes 14155776 | tf_op jit(solution)/shard_map/all_gather | solution.py:843
  7.9 81.0 %all-gather.5.cloned.1.call-start = ((), (), s32[]{:S(2)}) async-start(), calls=%async_computation.1 | async-start | bytes 14155776 | tf_op jit(solution)/shard_map/all_gather | solution.py:844
  11.2 19.3 %collective-permute-start = (bf16[1024,768]{1,0:T(8,128)(2,1)}, bf16[1024,768]{1,0:T(8,128)(2,1)}, u32[]{:S(2)}, u32[]{:S(2)}) collective-permute-start(bf16[1024,768]{1,0:T(8,128)(2,1)} %select_bitcast_fusion.2), channel_id=1, source_target_pairs={{16,3},{17,2},{2,17},{3,16},{20,7},{21,6},{6,21},{7,20},{24,11},{2... | collective-permute-start | bytes 4718600 | tf_op jit(solution)/shard_map/ppermute | solution.py:837
  13.2 72.2 %collective-permute-start.4 = (f32[6912]{0:T(1024)S(1)}, f32[6912]{0:T(1024)S(1)}, u32[]{:S(2)}, u32[]{:S(2)}) collective-permute-start(f32[6912]{0:T(1024)S(1)} %constant_dynamic-update-slice_fusion), channel_id=1, source_target_pairs={{0,16},{16,0},{1,17},{17,1},{2,18},{18,2},{3,19},{19,3},{4,20},{20... | collective-permute-start | bytes 82952 | tf_op jit(solution)/shard_map/ppermute | solution.py:28
  35.5 10.9 %collective-permute-start.1 = (bf16[1024,384]{1,0:T(8,128)(2,1)}, bf16[1024,384]{1,0:T(8,128)(2,1)S(1)}, u32[]{:S(2)}, u32[]{:S(2)}) collective-permute-start(bf16[1024,384]{1,0:T(8,128)(2,1)} %get-tuple-element.248), channel_id=1, source_target_pairs={{0,16},{16,0},{1,17},{17,1},{2,18},{18,2},{3,19},{19,3},{4,20},{20... | collective-permute-start | bytes 2359304 | tf_op jit(solution)/shard_map/ppermute | solution.py:28
  46.8 34.8 %collective-permute-start.2 = (bf16[1040,384]{1,0:T(8,128)(2,1)S(1)}, bf16[1040,384]{1,0:T(8,128)(2,1)S(1)}, u32[]{:S(2)}, u32[]{:S(2)}) collective-permute-start(bf16[1040,384]{1,0:T(8,128)(2,1)S(1)} %fold_spectra.4.part_ref), channel_id=1, source_target_pairs={{0,1},{1,0},{3,2},{2,3},{4,5},{5,4},{7,6},{6,7},{8,9},{9,8},{11,10... | collective-permute-start | bytes 2396168 | tf_op jit(solution)/shard_map/ppermute | solution.py:855
  85.5 43.8 %collective-permute-start.7 = (bf16[1024,768]{1,0:T(8,128)(2,1)}, bf16[1024,768]{1,0:T(8,128)(2,1)}, u32[]{:S(2)}, u32[]{:S(2)}) collective-permute-start(bf16[1024,768]{1,0:T(8,128)(2,1)} %get-tuple-element.266), channel_id=1, source_target_pairs={{16,3},{17,2},{2,17},{3,16},{20,7},{21,6},{6,21},{7,20},{24,11},{2... | collective-permute-start | bytes 4718600 | tf_op jit(solution)/shard_map/ppermute | solution.py:875
  121.3 20.1 %collective-permute-start.6 = (bf16[1040,384]{1,0:T(8,128)(2,1)S(1)}, bf16[1040,384]{1,0:T(8,128)(2,1)S(1)}, u32[]{:S(2)}, u32[]{:S(2)}) collective-permute-start(bf16[1040,384]{1,0:T(8,128)(2,1)S(1)} %fold_spectra.5.part_ref), channel_id=1, source_target_pairs={{0,1},{1,0},{3,2},{2,3},{4,5},{5,4},{7,6},{6,7},{8,9},{9,8},{11,10... | collective-permute-start | bytes 2396168 | tf_op jit(solution)/shard_map/ppermute | solution.py:855
  197.0 24.3 %collective-permute-start.11 = (bf16[1040,384]{1,0:T(8,128)(2,1)S(1)}, bf16[1040,384]{1,0:T(8,128)(2,1)}, u32[]{:S(2)}, u32[]{:S(2)}) collective-permute-start(bf16[1040,384]{1,0:T(8,128)(2,1)S(1)} %fold_spectra.6.part_ref), channel_id=1, source_target_pairs={{0,1},{1,0},{3,2},{2,3},{4,5},{5,4},{7,6},{6,7},{8,9},{9,8},{11,10... | collective-permute-start | bytes 2396168 | tf_op jit(solution)/shard_map/ppermute | solution.py:855
  235.1 44.1 %collective-permute-start.14 = (bf16[2,2,384,768]{3,2,1,0:T(8,128)(2,1)}, bf16[2,2,384,768]{3,2,1,0:T(8,128)(2,1)}, u32[]{:S(2)}, u32[]{:S(2)}) collective-permute-start(bf16[2,2,384,768]{3,2,1,0:T(8,128)(2,1)} %get-tuple-element.311), channel_id=1, source_target_pairs={{0,16},{16,0},{1,17},{17,1},{2,18},{18,2},{3,19},{19,3},{4,20},{20... | collective-permute-start | bytes 7077896 | tf_op jit(solution)/shard_map/ppermute | solution.py:28
  235.2 43.9 %collective-permute-start.15 = (bf16[2,384,768]{2,1,0:T(8,128)(2,1)}, bf16[2,384,768]{2,1,0:T(8,128)(2,1)S(1)}, u32[]{:S(2)}, u32[]{:S(2)}) collective-permute-start(bf16[2,384,768]{2,1,0:T(8,128)(2,1)} %get-tuple-element.312), channel_id=1, source_target_pairs={{0,4},{4,0},{8,12},{12,8},{1,5},{5,1},{9,13},{13,9},{2,6},{6,2},{1... | collective-permute-start | bytes 3538952 | tf_op jit(solution)/shard_map/ppermute | solution.py:693
  236.7 42.4 %collective-permute-start.16 = (bf16[2,384,768]{2,1,0:T(8,128)(2,1)}, bf16[2,384,768]{2,1,0:T(8,128)(2,1)}, u32[]{:S(2)}, u32[]{:S(2)}) collective-permute-start(bf16[2,384,768]{2,1,0:T(8,128)(2,1)} %get-tuple-element.313), channel_id=1, source_target_pairs={{0,8},{4,12},{8,0},{12,4},{1,9},{5,13},{9,1},{13,5},{2,10},{6,14},... | collective-permute-start | bytes 3538952 | tf_op jit(solution)/shard_map/ppermute | solution.py:693
  238.3 46.0 %collective-permute-start.9 = (bf16[1024,768]{1,0:T(8,128)(2,1)}, bf16[1024,768]{1,0:T(8,128)(2,1)}, u32[]{:S(2)}, u32[]{:S(2)}) collective-permute-start(bf16[1024,768]{1,0:T(8,128)(2,1)} %get-tuple-element.335), channel_id=1, source_target_pairs={{16,3},{17,2},{2,17},{3,16},{20,7},{21,6},{6,21},{7,20},{24,11},{2... | collective-permute-start | bytes 4718600 | tf_op jit(solution)/shard_map/ppermute | solution.py:821
  289.6 15.9 %collective-permute-start.19 = (bf16[384,768]{1,0:T(8,128)(2,1)}, bf16[384,768]{1,0:T(8,128)(2,1)S(1)}, u32[]{:S(2)}, u32[]{:S(2)}) collective-permute-start(bf16[384,768]{1,0:T(8,128)(2,1)} %get-tuple-element.348), channel_id=1, source_target_pairs={{0,8},{4,12},{8,0},{12,4},{1,9},{5,13},{9,1},{13,5},{2,10},{6,14},... | collective-permute-start | bytes 1769480 | tf_op jit(solution)/shard_map/ppermute | solution.py:693
  290.1 15.6 %collective-permute-start.20 = (bf16[384,768]{1,0:T(8,128)(2,1)S(1)}, bf16[384,768]{1,0:T(8,128)(2,1)}, u32[]{:S(2)}, u32[]{:S(2)}) collective-permute-start(bf16[384,768]{1,0:T(8,128)(2,1)S(1)} %get-tuple-element.350), channel_id=1, source_target_pairs={{0,4},{4,0},{8,12},{12,8},{1,5},{5,1},{9,13},{13,9},{2,6},{6,2},{1... | collective-permute-start | bytes 1769480 | tf_op jit(solution)/shard_map/ppermute | solution.py:693
  290.7 16.5 %collective-permute-start.18 = (f32[2,6912]{1,0:T(2,128)S(1)}, f32[2,6912]{1,0:T(2,128)S(1)}, u32[]{:S(2)}, u32[]{:S(2)}) collective-permute-start(f32[2,6912]{1,0:T(2,128)S(1)} %pad_maximum_fusion.10), channel_id=1, source_target_pairs={{0,16},{16,0},{1,17},{17,1},{2,18},{18,2},{3,19},{19,3},{4,20},{20... | collective-permute-start | bytes 165896 | tf_op jit(solution)/shard_map/ppermute | solution.py:932
  307.2 35.7 %collective-permute-start.22 = (bf16[2,2,384,768]{3,2,1,0:T(8,128)(2,1)}, bf16[2,2,384,768]{3,2,1,0:T(8,128)(2,1)S(1)}, u32[]{:S(2)}, u32[]{:S(2)}) collective-permute-start(bf16[2,2,384,768]{3,2,1,0:T(8,128)(2,1)} %get-tuple-element.367), channel_id=1, source_target_pairs={{0,16},{16,0},{1,17},{17,1},{2,18},{18,2},{3,19},{19,3},{4,20},{20... | collective-permute-start | bytes 7077896 | tf_op jit(solution)/shard_map/ppermute | solution.py:28
  308.3 34.6 %collective-permute-start.23 = (bf16[2,384,768]{2,1,0:T(8,128)(2,1)S(1)}, bf16[2,384,768]{2,1,0:T(8,128)(2,1)S(1)}, u32[]{:S(2)}, u32[]{:S(2)}) collective-permute-start(bf16[2,384,768]{2,1,0:T(8,128)(2,1)S(1)} %copy-done.32), channel_id=1, source_target_pairs={{0,4},{4,0},{8,12},{12,8},{1,5},{5,1},{9,13},{13,9},{2,6},{6,2},{1... | collective-permute-start | bytes 3538952 | tf_op jit(solution)/shard_map/ppermute | solution.py:693
  308.8 34.1 %collective-permute-start.24 = (bf16[2,384,768]{2,1,0:T(8,128)(2,1)S(1)}, bf16[2,384,768]{2,1,0:T(8,128)(2,1)S(1)}, u32[]{:S(2)}, u32[]{:S(2)}) collective-permute-start(bf16[2,384,768]{2,1,0:T(8,128)(2,1)S(1)} %copy-done.31), channel_id=1, source_target_pairs={{0,8},{4,12},{8,0},{12,4},{1,9},{5,13},{9,1},{13,5},{2,10},{6,14},... | collective-permute-start | bytes 3538952 | tf_op jit(solution)/shard_map/ppermute | solution.py:693
  310.4 11.8 %collective-permute-start.26 = (bf16[2,96,768]{2,1,0:T(8,128)(2,1)S(1)}, bf16[2,96,768]{2,1,0:T(8,128)(2,1)S(1)}, u32[]{:S(2)}, u32[]{:S(2)}) collective-permute-start(bf16[2,96,768]{2,1,0:T(8,128)(2,1)S(1)} %get-tuple-element.372), channel_id=1, source_target_pairs={{0,1},{1,2},{2,3},{3,0},{4,5},{5,6},{6,7},{7,4},{8,9},{9,10},{10,1... | collective-permute-start | bytes 884744 | tf_op jit(solution)/shard_map/ppermute | solution.py:723
  310.4 22.4 %collective-permute-start.27 = (bf16[2,96,768]{2,1,0:T(8,128)(2,1)S(1)}, bf16[2,96,768]{2,1,0:T(8,128)(2,1)S(1)}, u32[]{:S(2)}, u32[]{:S(2)}) collective-permute-start(bf16[2,96,768]{2,1,0:T(8,128)(2,1)S(1)} %get-tuple-element.373), channel_id=1, source_target_pairs={{0,2},{1,3},{2,0},{3,1},{4,6},{5,7},{6,4},{7,5},{8,10},{9,11},{10,... | collective-permute-start | bytes 884744 | tf_op jit(solution)/shard_map/ppermute | solution.py:723
  322.2 18.0 %collective-permute-start.28 = (bf16[2,96,768]{2,1,0:T(8,128)(2,1)S(1)}, bf16[2,96,768]{2,1,0:T(8,128)(2,1)S(1)}, u32[]{:S(2)}, u32[]{:S(2)}) collective-permute-start(bf16[2,96,768]{2,1,0:T(8,128)(2,1)S(1)} %get-tuple-element.374), channel_id=1, source_target_pairs={{0,3},{1,0},{2,1},{3,2},{4,7},{5,4},{6,5},{7,6},{8,11},{9,8},{10,9... | collective-permute-start | bytes 884744 | tf_op jit(solution)/shard_map/ppermute | solution.py:723
  345.9 10.2 %collective-permute-start.33 = (bf16[384,768]{1,0:T(8,128)(2,1)}, bf16[384,768]{1,0:T(8,128)(2,1)}, u32[]{:S(2)}, u32[]{:S(2)}) collective-permute-start(bf16[384,768]{1,0:T(8,128)(2,1)} %get-tuple-element.388), channel_id=1, source_target_pairs={{0,8},{4,12},{8,0},{12,4},{1,9},{5,13},{9,1},{13,5},{2,10},{6,14},... | collective-permute-start | bytes 1769480 | tf_op jit(solution)/shard_map/ppermute | solution.py:693
  347.9 12.3 %collective-permute-start.30 = (bf16[2,96,768]{2,1,0:T(8,128)(2,1)}, bf16[2,96,768]{2,1,0:T(8,128)(2,1)}, u32[]{:S(2)}, u32[]{:S(2)}) collective-permute-start(bf16[2,96,768]{2,1,0:T(8,128)(2,1)} %add_convert_fusion.10), channel_id=1, source_target_pairs={{0,1},{1,2},{2,3},{3,0},{4,5},{5,6},{6,7},{7,4},{8,9},{9,10},{10,1... | collective-permute-start | bytes 884744 | tf_op jit(solution)/shard_map/ppermute | solution.py:723
  349.9 18.3 %collective-permute-start.31 = (bf16[2,96,768]{2,1,0:T(8,128)(2,1)}, bf16[2,96,768]{2,1,0:T(8,128)(2,1)}, u32[]{:S(2)}, u32[]{:S(2)}) collective-permute-start(bf16[2,96,768]{2,1,0:T(8,128)(2,1)} %add_convert_fusion.10), channel_id=1, source_target_pairs={{0,2},{1,3},{2,0},{3,1},{4,6},{5,7},{6,4},{7,5},{8,10},{9,11},{10,... | collective-permute-start | bytes 884744 | tf_op jit(solution)/shard_map/ppermute | solution.py:723
  353.9 14.3 %collective-permute-start.32 = (bf16[2,96,768]{2,1,0:T(8,128)(2,1)}, bf16[2,96,768]{2,1,0:T(8,128)(2,1)}, u32[]{:S(2)}, u32[]{:S(2)}) collective-permute-start(bf16[2,96,768]{2,1,0:T(8,128)(2,1)} %add_convert_fusion.10), channel_id=1, source_target_pairs={{0,3},{1,0},{2,1},{3,2},{4,7},{5,4},{6,5},{7,6},{8,11},{9,8},{10,9... | collective-permute-start | bytes 884744 | tf_op jit(solution)/shard_map/ppermute | solution.py:723
  356.1 23.6 %collective-permute-start.29 = (bf16[1024,384]{1,0:T(8,128)(2,1)}, bf16[1024,384]{1,0:T(8,128)(2,1)}, u32[]{:S(2)}, u32[]{:S(2)}) collective-permute-start(bf16[1024,384]{1,0:T(8,128)(2,1)} %get-tuple-element.384), channel_id=1, source_target_pairs={{0,16},{16,0},{1,17},{17,1},{2,18},{18,2},{3,19},{19,3},{4,20},{20... | collective-permute-start | bytes 2359304 | tf_op jit(solution)/shard_map/ppermute | solution.py:28
  371.5 14.9 %collective-permute-start.38 = (bf16[4,96,768]{2,1,0:T(8,128)(2,1)S(1)}, bf16[4,96,768]{2,1,0:T(8,128)(2,1)S(1)}, u32[]{:S(2)}, u32[]{:S(2)}) collective-permute-start(bf16[4,96,768]{2,1,0:T(8,128)(2,1)S(1)} %pad_maximum_fusion.6), channel_id=1, source_target_pairs={{0,8},{4,12},{8,0},{12,4},{1,9},{5,13},{9,1},{13,5},{2,10},{6,14},... | collective-permute-start | bytes 1769480 | tf_op jit(solution)/shard_map/ppermute | solution.py:693
  373.1 14.7 %collective-permute-start.39 = (bf16[4,96,768]{2,1,0:T(8,128)(2,1)S(1)}, bf16[4,96,768]{2,1,0:T(8,128)(2,1)S(1)}, u32[]{:S(2)}, u32[]{:S(2)}) collective-permute-start(bf16[4,96,768]{2,1,0:T(8,128)(2,1)S(1)} %pad_maximum_fusion.7), channel_id=1, source_target_pairs={{0,4},{4,0},{8,12},{12,8},{1,5},{5,1},{9,13},{13,9},{2,6},{6,2},{1... | collective-permute-start | bytes 1769480 | tf_op jit(solution)/shard_map/ppermute | solution.py:693
  373.6 14.3 %collective-permute-start.35 = (bf16[2,96,768]{2,1,0:T(8,128)(2,1)S(1)}, bf16[2,96,768]{2,1,0:T(8,128)(2,1)S(1)}, u32[]{:S(2)}, u32[]{:S(2)}) collective-permute-start(bf16[2,96,768]{2,1,0:T(8,128)(2,1)S(1)} %get-tuple-element.404), channel_id=1, source_target_pairs={{0,1},{1,2},{2,3},{3,0},{4,5},{5,6},{6,7},{7,4},{8,9},{9,10},{10,1... | collective-permute-start | bytes 884744 | tf_op jit(solution)/shard_map/ppermute | solution.py:723
  377.4 19.4 %collective-permute-start.36 = (bf16[2,96,768]{2,1,0:T(8,128)(2,1)S(1)}, bf16[2,96,768]{2,1,0:T(8,128)(2,1)S(1)}, u32[]{:S(2)}, u32[]{:S(2)}) collective-permute-start(bf16[2,96,768]{2,1,0:T(8,128)(2,1)S(1)} %get-tuple-element.405), channel_id=1, source_target_pairs={{0,2},{1,3},{2,0},{3,1},{4,6},{5,7},{6,4},{7,5},{8,10},{9,11},{10,... | collective-permute-start | bytes 884744 | tf_op jit(solution)/shard_map/ppermute | solution.py:723
  379.7 17.1 %collective-permute-start.37 = (bf16[2,96,768]{2,1,0:T(8,128)(2,1)S(1)}, bf16[2,96,768]{2,1,0:T(8,128)(2,1)S(1)}, u32[]{:S(2)}, u32[]{:S(2)}) collective-permute-start(bf16[2,96,768]{2,1,0:T(8,128)(2,1)S(1)} %get-tuple-element.406), channel_id=1, source_target_pairs={{0,3},{1,0},{2,1},{3,2},{4,7},{5,4},{6,5},{7,6},{8,11},{9,8},{10,9... | collective-permute-start | bytes 884744 | tf_op jit(solution)/shard_map/ppermute | solution.py:723
  386.4 18.4 %collective-permute-start.40 = (f32[2,6912]{1,0:T(2,128)S(1)}, f32[2,6912]{1,0:T(2,128)S(1)}, u32[]{:S(2)}, u32[]{:S(2)}) collective-permute-start(f32[2,6912]{1,0:T(2,128)S(1)} %copy-done.35), channel_id=1, source_target_pairs={{0,2},{1,3},{2,0},{3,1},{4,6},{5,7},{6,4},{7,5},{8,10},{9,11},{10,... | collective-permute-start | bytes 165896 | tf_op jit(solution)/shard_map/ppermute | solution.py:932
  404.8 11.9 %collective-permute-start.41 = (bf16[2,96,768]{2,1,0:T(8,128)(2,1)S(1)}, bf16[2,96,768]{2,1,0:T(8,128)(2,1)S(1)}, u32[]{:S(2)}, u32[]{:S(2)}) collective-permute-start(bf16[2,96,768]{2,1,0:T(8,128)(2,1)S(1)} %add_convert_fusion.9), channel_id=1, source_target_pairs={{0,1},{1,2},{2,3},{3,0},{4,5},{5,6},{6,7},{7,4},{8,9},{9,10},{10,1... | collective-permute-start | bytes 884744 | tf_op jit(solution)/shard_map/ppermute | solution.py:723
  404.9 23.5 %collective-permute-start.42 = (bf16[2,96,768]{2,1,0:T(8,128)(2,1)S(1)}, bf16[2,96,768]{2,1,0:T(8,128)(2,1)S(1)}, u32[]{:S(2)}, u32[]{:S(2)}) collective-permute-start(bf16[2,96,768]{2,1,0:T(8,128)(2,1)S(1)} %add_convert_fusion.9), channel_id=1, source_target_pairs={{0,2},{1,3},{2,0},{3,1},{4,6},{5,7},{6,4},{7,5},{8,10},{9,11},{10,... | collective-permute-start | bytes 884744 | tf_op jit(solution)/shard_map/ppermute | solution.py:723
  405.4 23.0 %collective-permute-start.43 = (bf16[2,96,768]{2,1,0:T(8,128)(2,1)S(1)}, bf16[2,96,768]{2,1,0:T(8,128)(2,1)S(1)}, u32[]{:S(2)}, u32[]{:S(2)}) collective-permute-start(bf16[2,96,768]{2,1,0:T(8,128)(2,1)S(1)} %add_convert_fusion.9), channel_id=1, source_target_pairs={{0,3},{1,0},{2,1},{3,2},{4,7},{5,4},{6,5},{7,6},{8,11},{9,8},{10,9... | collective-permute-start | bytes 884744 | tf_op jit(solution)/shard_map/ppermute | solution.py:723
  409.1 27.4 %collective-permute-start.45 = (bf16[2,4,96,768]{3,2,1,0:T(8,128)(2,1)S(1)}, bf16[2,4,96,768]{3,2,1,0:T(8,128)(2,1)S(1)}, u32[]{:S(2)}, u32[]{:S(2)}) collective-permute-start(bf16[2,4,96,768]{3,2,1,0:T(8,128)(2,1)S(1)} %pad_maximum_fusion.2.refs_4_), channel_id=1, source_target_pairs={{0,4},{4,0},{8,12},{12,8},{1,5},{5,1},{9,13},{13,9},{2,6},{6,2},{1... | collective-permute-start | bytes 3538952 | tf_op jit(solution)/shard_map/ppermute | solution.py:693
  410.4 27.0 %collective-permute-start.46 = (bf16[2,4,96,768]{3,2,1,0:T(8,128)(2,1)S(1)}, bf16[2,4,96,768]{3,2,1,0:T(8,128)(2,1)S(1)}, u32[]{:S(2)}, u32[]{:S(2)}) collective-permute-start(bf16[2,4,96,768]{3,2,1,0:T(8,128)(2,1)S(1)} %pad_maximum_fusion.3.refs_5_), channel_id=1, source_target_pairs={{0,8},{4,12},{8,0},{12,4},{1,9},{5,13},{9,1},{13,5},{2,10},{6,14},... | collective-permute-start | bytes 3538952 | tf_op jit(solution)/shard_map/ppermute | solution.py:693
  428.6 23.2 %collective-permute-start.44 = (bf16[1040,384]{1,0:T(8,128)(2,1)S(1)}, bf16[1040,384]{1,0:T(8,128)(2,1)S(1)}, u32[]{:S(2)}, u32[]{:S(2)}) collective-permute-start(bf16[1040,384]{1,0:T(8,128)(2,1)S(1)} %fold_spectra.7.part_ref), channel_id=1, source_target_pairs={{0,1},{1,0},{3,2},{2,3},{4,5},{5,4},{7,6},{6,7},{8,9},{9,8},{11,10... | collective-permute-start | bytes 2396168 | tf_op jit(solution)/shard_map/ppermute | solution.py:855
  437.5 13.5 %collective-permute-start.47 = (bf16[4,96,768]{2,1,0:T(8,128)(2,1)S(1)}, bf16[4,96,768]{2,1,0:T(8,128)(2,1)S(1)}, u32[]{:S(2)}, u32[]{:S(2)}) collective-permute-start(bf16[4,96,768]{2,1,0:T(8,128)(2,1)S(1)} %pad_maximum_fusion.8), channel_id=1, source_target_pairs={{0,8},{4,12},{8,0},{12,4},{1,9},{5,13},{9,1},{13,5},{2,10},{6,14},... | collective-permute-start | bytes 1769480 | tf_op jit(solution)/shard_map/ppermute | solution.py:693
  438.2 13.2 %collective-permute-start.48 = (bf16[4,96,768]{2,1,0:T(8,128)(2,1)S(1)}, bf16[4,96,768]{2,1,0:T(8,128)(2,1)S(1)}, u32[]{:S(2)}, u32[]{:S(2)}) collective-permute-start(bf16[4,96,768]{2,1,0:T(8,128)(2,1)S(1)} %pad_maximum_fusion.9), channel_id=1, source_target_pairs={{0,4},{4,0},{8,12},{12,8},{1,5},{5,1},{9,13},{13,9},{2,6},{6,2},{1... | collective-permute-start | bytes 1769480 | tf_op jit(solution)/shard_map/ppermute | solution.py:693
  438.7 20.8 %collective-permute-start.53 = (bf16[2,4,96,768]{3,2,1,0:T(8,128)(2,1)S(1)}, bf16[2,4,96,768]{3,2,1,0:T(8,128)(2,1)S(1)}, u32[]{:S(2)}, u32[]{:S(2)}) collective-permute-start(bf16[2,4,96,768]{3,2,1,0:T(8,128)(2,1)S(1)} %pad_maximum_fusion.2.refs_4_), channel_id=1, source_target_pairs={{0,16},{1,17},{2,18},{3,19},{4,20},{5,21},{6,22},{7,23},{8,24},{9,... | collective-permute-start | bytes 3538952 | tf_op jit(solution)/shard_map/ppermute | solution.py:970
  458.2 10.4 %collective-permute-start.52 = (bf16[2,4,96,768]{3,2,1,0:T(8,128)(2,1)S(1)}, bf16[2,4,96,768]{3,2,1,0:T(8,128)(2,1)S(1)}, u32[]{:S(2)}, u32[]{:S(2)}) collective-permute-start(bf16[2,4,96,768]{3,2,1,0:T(8,128)(2,1)S(1)} %pad_maximum_fusion.5.refs_1_), channel_id=1, source_target_pairs={{16,0},{17,1},{18,2},{19,3},{20,4},{21,5},{22,6},{23,7},{24,8},{25... | collective-permute-start | bytes 3538952 | tf_op jit(solution)/shard_map/ppermute | solution.py:981
  459.5 28.6 %collective-permute-start.56 = (bf16[2,4,96,768]{3,2,1,0:T(8,128)(2,1)S(1)}, bf16[2,4,96,768]{3,2,1,0:T(8,128)(2,1)S(1)}, u32[]{:S(2)}, u32[]{:S(2)}) collective-permute-start(bf16[2,4,96,768]{3,2,1,0:T(8,128)(2,1)S(1)} %pad_maximum_fusion.4.refs_0_), channel_id=1, source_target_pairs={{0,4},{4,0},{8,12},{12,8},{1,5},{5,1},{9,13},{13,9},{2,6},{6,2},{1... | collective-permute-start | bytes 3538952 | tf_op jit(solution)/shard_map/ppermute | solution.py:693
  460.9 28.8 %collective-permute-start.57 = (bf16[2,4,96,768]{3,2,1,0:T(8,128)(2,1)S(1)}, bf16[2,4,96,768]{3,2,1,0:T(8,128)(2,1)S(1)}, u32[]{:S(2)}, u32[]{:S(2)}) collective-permute-start(bf16[2,4,96,768]{3,2,1,0:T(8,128)(2,1)S(1)} %pad_maximum_fusion.5.refs_1_), channel_id=1, source_target_pairs={{0,8},{4,12},{8,0},{12,4},{1,9},{5,13},{9,1},{13,5},{2,10},{6,14},... | collective-permute-start | bytes 3538952 | tf_op jit(solution)/shard_map/ppermute | solution.py:693
  463.9 37.6 %collective-permute-start.50 = (bf16[1024,768]{1,0:T(8,128)(2,1)S(1)}, bf16[1024,768]{1,0:T(8,128)(2,1)S(1)}, u32[]{:S(2)}, u32[]{:S(2)}) collective-permute-start(bf16[1024,768]{1,0:T(8,128)(2,1)S(1)} %finish.1), channel_id=1, source_target_pairs={{16,3},{17,2},{2,17},{3,16},{20,7},{21,6},{6,21},{7,20},{24,11},{2... | collective-permute-start | bytes 4718600 | tf_op jit(solution)/shard_map/ppermute | solution.py:821
  464.6 27.6 %collective-permute-start.60 = (bf16[2,4,96,768]{3,2,1,0:T(8,128)(2,1)S(1)}, bf16[2,4,96,768]{3,2,1,0:T(8,128)(2,1)S(1)}, u32[]{:S(2)}, u32[]{:S(2)}) collective-permute-start(bf16[2,4,96,768]{3,2,1,0:T(8,128)(2,1)S(1)} %collective-permute-done.45.refs_4_), channel_id=1, source_target_pairs={{0,16},{1,17},{2,18},{3,19},{4,20},{5,21},{6,22},{7,23},{8,24},{9,... | collective-permute-start | bytes 3538952 | tf_op jit(solution)/shard_map/ppermute | solution.py:977
  468.6 24.5 %collective-permute-start.61 = (bf16[2,4,96,768]{3,2,1,0:T(8,128)(2,1)S(1)}, bf16[2,4,96,768]{3,2,1,0:T(8,128)(2,1)S(1)}, u32[]{:S(2)}, u32[]{:S(2)}) collective-permute-start(bf16[2,4,96,768]{3,2,1,0:T(8,128)(2,1)S(1)} %collective-permute-done.46.refs_5_), channel_id=1, source_target_pairs={{0,16},{1,17},{2,18},{3,19},{4,20},{5,21},{6,22},{7,23},{8,24},{9,... | collective-permute-start | bytes 3538952 | tf_op jit(solution)/shard_map/ppermute | solution.py:977
  (79 other events, 752.4 us)
Sparse Core Ops, SparseCore 0:
  9.6 24.5 all-gather.2
  35.7 23.0 all-gather.4

commit v5 on v4

--- a/solution.py
+++ b/solution.py
@@ -918,8 +918,8 @@
     early.start_first(line.after(sent))
     grad, own, other, wide0, narrow0, my_sent, my_kept, other_sent, other_kept = back(0, grad, (mixed, came))
 
-    sums = run(early.first_sums(my_kept1, got_kept1))
-    out_block = line(give_pick, *out_moved)
+    add_first, terms = early.first_sums(my_kept1, got_kept1)
+    sums = line(lambda _, *v: add_first(*v), out_moved[1], *terms)
 
     got_sent = swap_cores(line.after(other_sent))
     came = swap_cores(line.after(other))
@@ -945,7 +945,7 @@
     got_kept0 = swap_cores(line.after(other_kept))
     hop = start_hop()
     begun = part(folded)
-    out_mine, out_theirs = line(give_cut, out_block)
+    out_mine, out_theirs = line(lambda *v: give_cut(give_pick(*v)), *out_moved)
     piece = run(early.scattered())
     small = end_hop(hop)
     sums = run(late.first_sums(my_kept, got_kept0))

time: 527 us -> 528 us (level); the launches traced: 518 us -> 525 us
  Pallas kernels: 163 us -> 174 us
  starting transfers between devices: 110 us -> 117 us
  waiting for transfers between devices: 138 us -> 131 us
    pallas_call x2, Pallas kernels: 49 us -> 60 us  [forward(): call(body, (rows // tile,), [scalar_block(), row_block(tile, width)] + mi...]
    ppermute x12, waiting for transfers between devices: 45.7 us -> 38.3 us  [along(): lax.ppermute(value, 'seq', [(i, (i + by) % self.peers) for i in range(sel...]
  transfers between devices with their start and end apart: 66 -> 66, of which waited for: 29 -> 29; matrix products, arithmetic and copies ran while one was open for 11% -> 10% of each run, Pallas kernels for 21% -> 21%
where the time goes in v5:
time: 528 us; the launch traced here: 525 us
  Pallas kernels  174 us (33%)
  waiting for transfers between devices  131 us (25%)
  starting transfers between devices  117 us (22%)
  other arithmetic  44 us (8%)
  local copies, waits for them, and re-layouts  29.5 us (6%)
  between operations  15.7 us (3%)
  matrix products  13.8 us (3%)
    pallas_call x2, Pallas kernels, forward(): call(body, (rows // tile,), [scalar_block(), row_block(tile, width)] + mi...  60 us
    ppermute x16, waiting for transfers between devices, across(): return lax.ppermute(value, 'dp', bit_pairs(self.count, bit))  41 us
    pallas_call x1, Pallas kernels, backward(): call(body, (rows // tile,), [scalar_block(), row_block(tile, width)] + ex...  39.4 us
    ppermute x12, waiting for transfers between devices, along(): lax.ppermute(value, 'seq', [(i, (i + by) % self.peers) for i in range(sel...  38.3 us
    ppermute x4, starting transfers between devices, spread_out(): return [lax.ppermute(folded, 'seq', pairs) for pairs in group_shifts]  24.7 us
    ppermute x12, starting transfers between devices, along(): lax.ppermute(value, 'seq', [(i, (i + by) % self.peers) for i in range(sel...  24.4 us
    ppermute x4, waiting for transfers between devices, spread_out(): return [lax.ppermute(folded, 'seq', pairs) for pairs in group_shifts]  21.7 us
    pallas_call x1, Pallas kernels, backward_last(): call(body, (rows // tile,), [row_block(tile, width), row_block(tile, hidd...  21.4 us
  transfers between devices with their start and end apart: 66, of which 29 were waited for; matrix products, arithmetic and copies ran while one was open for 10% of the time, Pallas kernels for 21%

profile of v5, /device:TPU:0, one launch (start us, length us, event | category | flops | bytes accessed | tf_op | source)
XLA Modules:
  0.0 524.9 jit_solution(15038980927947167614)
XLA Ops:
  13.2 5.4 %collective-permute-start.4 = (f32[6912]{0:T(1024)S(1)}, f32[6912]{0:T(1024)S(1)}, u32[]{:S(2)}, u32[]{:S(2)}) collective-permute-start(f32[6912]{0:T(1024)S(1)} %constant_dynamic-update-slice_fusion), channel_id=1, source_target_pairs={{0,16},{16,0},{1,17},{17,1},{2,18},{18,2},{3,19},{19,3},{4,20},{20... | collective-permute-start | bytes 82952 | tf_op jit(solution)/shard_map/ppermute | solution.py:28
  18.7 11.8 %select_convert_fusion = (bf16[768,768]{1,0:T(8,128)(2,1)}, bf16[768,768]{1,0:T(8,128)(2,1)S(1)}) fusion(s32[768]{0:T(1024)S(1)} %get-tuple-element.539, s32[768]{0:T(1024)S(1)} %get-tuple-element.540, f32[]{:T(128)S(6)} %select_n.299, pred[768]{0:T(1024)(128)(4,1)S(1)} %select_compare_fusion, f32[]{:T(128)S(6)} %neg.3), kind=kLoop, calls=%fused_computation.23 | loop fusion | flops 12976128 | bytes 2366216 | tf_op jit(solution)/shard_map/convert_element_type | solution.py:64
  32.7 2.8 spectra.1
  35.5 7.7 %collective-permute-start.1 = (bf16[1024,384]{1,0:T(8,128)(2,1)}, bf16[1024,384]{1,0:T(8,128)(2,1)S(1)}, u32[]{:S(2)}, u32[]{:S(2)}) collective-permute-start(bf16[1024,384]{1,0:T(8,128)(2,1)} %get-tuple-element.247), channel_id=1, source_target_pairs={{0,16},{16,0},{1,17},{17,1},{2,18},{18,2},{3,19},{19,3},{4,20},{20... | collective-permute-start | bytes 2359304 | tf_op jit(solution)/shard_map/ppermute | solution.py:28
  43.8 2.6 fusion.57
  46.8 16.8 %collective-permute-start.2 = (bf16[1040,384]{1,0:T(8,128)(2,1)S(1)}, bf16[1040,384]{1,0:T(8,128)(2,1)S(1)}, u32[]{:S(2)}, u32[]{:S(2)}) collective-permute-start(bf16[1040,384]{1,0:T(8,128)(2,1)S(1)} %fold_spectra.4.part_ref), channel_id=1, source_target_pairs={{0,1},{1,0},{3,2},{2,3},{4,5},{5,4},{7,6},{6,7},{8,9},{9,8},{11,10... | collective-permute-start | bytes 2396168 | tf_op jit(solution)/shard_map/ppermute | solution.py:855
  63.6 3.3 add_convert_fusion
  69.2 12.4 %collective-permute-done.2.refs_4_ = bf16[1040,384]{1,0:T(8,128)(2,1)S(1)} collective-permute-done((bf16[1040,384]{1,0:T(8,128)(2,1)S(1)}, bf16[1040,384]{1,0:T(8,128)(2,1)S(1)}, u32[]{:S(2)}, u32[]{:S(2)}) %collective-permute-start.2) | collective-permute-done | bytes 798752 | tf_op jit(solution)/shard_map/ppermute | solution.py:855
  89.9 24.6 %layer_forward.2 = (bf16[1024,768]{1,0:T(8,128)(2,1)}, bf16[1024,768]{1,0:T(8,128)(2,1)}, bf16[1024,3072]{1,0:T(8,128)(2,1)}, bf16[1024,3072]{1,0:T(8,128)(2,1)}...) custom-call(s32[1]{0:T(128)} %bitcast.core_ref.refs_0_, ...), custom_call_target="tpu_custom_call" | custom-call | flops 188743680 | bytes 516096 | tf_op jit(solution)/shard_map/layer_forward/pallas_call | solution.py:319
  114.5 3.3 collective-permute-start.5
  122.4 2.4 copy-done.1
  124.7 2.4 copy-done.4
  129.4 3.6 fusion.27.refs_0_
  133.0 8.6 %collective-permute-done.6.refs_4_ = bf16[1040,384]{1,0:T(8,128)(2,1)S(1)} collective-permute-done((bf16[1040,384]{1,0:T(8,128)(2,1)S(1)}, bf16[1040,384]{1,0:T(8,128)(2,1)S(1)}, u32[]{:S(2)}, u32[]{:S(2)}) %collective-permute-start.6) | collective-permute-done | bytes 798752 | tf_op jit(solution)/shard_map/ppermute | solution.py:855
  147.2 35.4 %layer_forward.3 = (bf16[1024,768]{1,0:T(8,128)(2,1)}, bf16[1024,768]{1,0:T(8,128)(2,1)}, bf16[1024,3072]{1,0:T(8,128)(2,1)}, bf16[1024,3072]{1,0:T(8,128)(2,1)}...) custom-call(s32[1]{0:T(128)} %bitcast.core_ref.refs_0_, ...), custom_call_target="tpu_custom_call" | custom-call | flops 188743680 | bytes 516096 | tf_op jit(solution)/shard_map/layer_forward/pallas_call | solution.py:319
  182.6 21.4 %last_backward.1 = (f32[1024,768]{1,0:T(8,128)}, bf16[1024,768]{1,0:T(8,128)(2,1)}, bf16[1024,3072]{1,0:T(8,128)(2,1)}, bf16[1024,384]{1,0:T(8,128)(2,1)}, bf16[...) custom-call(bf16[1024,768]{1,0:T(8,128)(2,1)} %fusion.27.refs_0_, ...), custom_call_target="tpu_custom_call" | custom-call | flops 188743680 | bytes 516096 | tf_op jit(solution)/shard_map/last_backward/pallas_call | solution.py:507
  204.2 2.4 collective-permute-done.10.recv_ref
  209.6 18.1 %grad_blocks.1 = (bf16[2,2,384,768]{3,2,1,0:T(8,128)(2,1)}, bf16[2,2,384,768]{3,2,1,0:T(8,128)(2,1)}, bf16[2,2,384,768]{3,2,1,0:T(8,128)(2,1)}, bf16[2,2,384,768]{3,2,1,0:T(8,128)(2,1)}) custom-call(s32[2]{0:T(128)} %pad_add_fusion.scalar_ref, bf16[1024,3072]{1,0:T(8,128)(2,1)} %get-tuple-element.296.act_ref, bf16[1024,768]{1,0:T(8,128)(2,1)} %get-tuple-element.297.gb_ref, ...), custom_call_target="tpu_custom_call" | custom-call | flops 150994944 | bytes 245760 | tf_op jit(solution)/shard_map/grad_blocks/pallas_call | solution.py:578
  234.7 3.6 transform_rest.6.refs_0_.refs_1_
  238.9 5.2 collective-permute-done.12.refs_2_.refs_3_
  251.2 39.4 %layer_backward.1 = (f32[1024,768]{1,0:T(8,128)}, bf16[1024,384]{1,0:T(8,128)(2,1)}, bf16[1024,384]{1,0:T(8,128)(2,1)}, f32[1,3072]{1,0:T(1,128)}, f32[8,768]{1,...) custom-call(s32[2]{0:T(128)} %pad_add_fusion.scalar_ref, ...), custom_call_target="tpu_custom_call" | custom-call | flops 377487360 | bytes 516096 | tf_op jit(solution)/shard_map/layer_backward/pallas_call | solution.py:423
  290.6 3.2 fusion.10
  297.9 3.2 collective-permute-done.17.recv_ref
  301.5 3.6 fusion.44
  305.1 7.6 %collective-permute-done.19 = bf16[384,768]{1,0:T(8,128)(2,1)S(1)} collective-permute-done((bf16[384,768]{1,0:T(8,128)(2,1)}, bf16[384,768]{1,0:T(8,128)(2,1)S(1)}, u32[]{:S(2)}, u32[]{:S(2)}) %collective-permute-start.19) | collective-permute-done | bytes 589856 | tf_op jit(solution)/shard_map/ppermute | solution.py:693
  317.5 2.9 collective-permute-start.27
  320.4 2.4 copy-done.2
  330.2 8.4 %collective-permute-done.27 = bf16[2,96,768]{2,1,0:T(8,128)(2,1)S(1)} collective-permute-done((bf16[2,96,768]{2,1,0:T(8,128)(2,1)S(1)}, bf16[2,96,768]{2,1,0:T(8,128)(2,1)S(1)}, u32[]{:S(2)}, u32[]{:S(2)}) %collective-permute-start.27) | collective-permute-done | bytes 294944 | tf_op jit(solution)/shard_map/ppermute | solution.py:723
  338.6 4.4 collective-permute-start.25
  352.8 3.4 collective-permute-start.31
  357.1 6.0 %collective-permute-done.33 = bf16[384,768]{1,0:T(8,128)(2,1)} collective-permute-done((bf16[384,768]{1,0:T(8,128)(2,1)}, bf16[384,768]{1,0:T(8,128)(2,1)}, u32[]{:S(2)}, u32[]{:S(2)}) %collective-permute-start.33) | collective-permute-done | bytes 589856 | tf_op jit(solution)/shard_map/ppermute | solution.py:693
  368.0 5.9 %collective-permute-done.31 = bf16[2,96,768]{2,1,0:T(8,128)(2,1)} collective-permute-done((bf16[2,96,768]{2,1,0:T(8,128)(2,1)}, bf16[2,96,768]{2,1,0:T(8,128)(2,1)}, u32[]{:S(2)}, u32[]{:S(2)}) %collective-permute-start.31) | collective-permute-done | bytes 294944 | tf_op jit(solution)/shard_map/ppermute | solution.py:723
  379.3 6.8 %collective-permute-start.35 = (bf16[2,96,768]{2,1,0:T(8,128)(2,1)S(1)}, bf16[2,96,768]{2,1,0:T(8,128)(2,1)S(1)}, u32[]{:S(2)}, u32[]{:S(2)}) collective-permute-start(bf16[2,96,768]{2,1,0:T(8,128)(2,1)S(1)} %get-tuple-element.402), channel_id=1, source_target_pairs={{0,1},{1,2},{2,3},{3,0},{4,5},{5,6},{6,7},{7,4},{8,9},{9,10},{10,1... | collective-permute-start | bytes 884744 | tf_op jit(solution)/shard_map/ppermute | solution.py:723
  388.4 2.5 fusion.37
  391.0 2.7 fusion.38
  395.1 3.2 collective-permute-start.40
  398.4 6.5 %collective-permute-done.36 = bf16[2,96,768]{2,1,0:T(8,128)(2,1)S(1)} collective-permute-done((bf16[2,96,768]{2,1,0:T(8,128)(2,1)S(1)}, bf16[2,96,768]{2,1,0:T(8,128)(2,1)S(1)}, u32[]{:S(2)}, u32[]{:S(2)}) %collective-permute-start.36) | collective-permute-done | bytes 294944 | tf_op jit(solution)/shard_map/ppermute | solution.py:723
  405.4 7.6 %collective-permute-done.40 = f32[2,6912]{1,0:T(2,128)S(1)} collective-permute-done((f32[2,6912]{1,0:T(2,128)S(1)}, f32[2,6912]{1,0:T(2,128)S(1)}, u32[]{:S(2)}, u32[]{:S(2)}) %collective-permute-start.40) | collective-permute-done | bytes 55328 | tf_op jit(solution)/shard_map/ppermute | solution.py:932
  413.9 3.4 collective-permute-start.42
  419.4 5.4 %collective-permute-done.41 = bf16[2,96,768]{2,1,0:T(8,128)(2,1)S(1)} collective-permute-done((bf16[2,96,768]{2,1,0:T(8,128)(2,1)S(1)}, bf16[2,96,768]{2,1,0:T(8,128)(2,1)S(1)}, u32[]{:S(2)}, u32[]{:S(2)}) %collective-permute-start.41) | collective-permute-done | bytes 294944 | tf_op jit(solution)/shard_map/ppermute | solution.py:723
  424.8 11.8 %collective-permute-done.42 = bf16[2,96,768]{2,1,0:T(8,128)(2,1)S(1)} collective-permute-done((bf16[2,96,768]{2,1,0:T(8,128)(2,1)S(1)}, bf16[2,96,768]{2,1,0:T(8,128)(2,1)S(1)}, u32[]{:S(2)}, u32[]{:S(2)}) %collective-permute-start.42) | collective-permute-done | bytes 294944 | tf_op jit(solution)/shard_map/ppermute | solution.py:723
  436.8 6.0 %collective-permute-start.44 = (bf16[1040,384]{1,0:T(8,128)(2,1)S(1)}, bf16[1040,384]{1,0:T(8,128)(2,1)S(1)}, u32[]{:S(2)}, u32[]{:S(2)}) collective-permute-start(bf16[1040,384]{1,0:T(8,128)(2,1)S(1)} %fold_spectra.7.part_ref), channel_id=1, source_target_pairs={{0,1},{1,0},{3,2},{2,3},{4,5},{5,4},{7,6},{6,7},{8,9},{9,8},{11,10... | collective-permute-start | bytes 2396168 | tf_op jit(solution)/shard_map/ppermute | solution.py:855
  449.0 8.7 %collective-permute-done.47 = bf16[4,96,768]{2,1,0:T(8,128)(2,1)S(1)} collective-permute-done((bf16[4,96,768]{2,1,0:T(8,128)(2,1)S(1)}, bf16[4,96,768]{2,1,0:T(8,128)(2,1)S(1)}, u32[]{:S(2)}, u32[]{:S(2)}) %collective-permute-start.47) | collective-permute-done | bytes 589856 | tf_op jit(solution)/shard_map/ppermute | solution.py:693
  462.3 2.5 collective-permute-start.54
  472.8 3.8 collective-permute-start.60
  478.3 4.6 write_weights.2
  482.9 13.2 %collective-permute-done.56.refs_0_ = bf16[2,4,96,768]{3,2,1,0:T(8,128)(2,1)S(1)} collective-permute-done((bf16[2,4,96,768]{3,2,1,0:T(8,128)(2,1)S(1)}, bf16[2,4,96,768]{3,2,1,0:T(8,128)(2,1)S(1)}, u32[]{:S(2)}, u32[]{:S(2)}) %collective-permute-start.56) | collective-permute-done | bytes 1179680 | tf_op jit(solution)/shard_map/ppermute | solution.py:693
  503.5 4.6 write_weights.3
  (326 shorter events, 132.1 us)
Async XLA Ops:
  7.2 81.8 %all-gather.3.cloned.1.call-start = ((), (), s32[]{:S(2)}) async-start(), calls=%async_computation | async-start | bytes 14155776 | tf_op jit(solution)/shard_map/all_gather | solution.py:843
  7.9 81.1 %all-gather.5.cloned.1.call-start = ((), (), s32[]{:S(2)}) async-start(), calls=%async_computation.1 | async-start | bytes 14155776 | tf_op jit(solution)/shard_map/all_gather | solution.py:844
  11.2 19.3 %collective-permute-start = (bf16[1024,768]{1,0:T(8,128)(2,1)}, bf16[1024,768]{1,0:T(8,128)(2,1)}, u32[]{:S(2)}, u32[]{:S(2)}) collective-permute-start(bf16[1024,768]{1,0:T(8,128)(2,1)} %select_bitcast_fusion.2), channel_id=1, source_target_pairs={{16,3},{17,2},{2,17},{3,16},{20,7},{21,6},{6,21},{7,20},{24,11},{2... | collective-permute-start | bytes 4718600 | tf_op jit(solution)/shard_map/ppermute | solution.py:837
  13.2 72.3 %collective-permute-start.4 = (f32[6912]{0:T(1024)S(1)}, f32[6912]{0:T(1024)S(1)}, u32[]{:S(2)}, u32[]{:S(2)}) collective-permute-start(f32[6912]{0:T(1024)S(1)} %constant_dynamic-update-slice_fusion), channel_id=1, source_target_pairs={{0,16},{16,0},{1,17},{17,1},{2,18},{18,2},{3,19},{19,3},{4,20},{20... | collective-permute-start | bytes 82952 | tf_op jit(solution)/shard_map/ppermute | solution.py:28
  35.5 10.9 %collective-permute-start.1 = (bf16[1024,384]{1,0:T(8,128)(2,1)}, bf16[1024,384]{1,0:T(8,128)(2,1)S(1)}, u32[]{:S(2)}, u32[]{:S(2)}) collective-permute-start(bf16[1024,384]{1,0:T(8,128)(2,1)} %get-tuple-element.247), channel_id=1, source_target_pairs={{0,16},{16,0},{1,17},{17,1},{2,18},{18,2},{3,19},{19,3},{4,20},{20... | collective-permute-start | bytes 2359304 | tf_op jit(solution)/shard_map/ppermute | solution.py:28
  46.8 34.8 %collective-permute-start.2 = (bf16[1040,384]{1,0:T(8,128)(2,1)S(1)}, bf16[1040,384]{1,0:T(8,128)(2,1)S(1)}, u32[]{:S(2)}, u32[]{:S(2)}) collective-permute-start(bf16[1040,384]{1,0:T(8,128)(2,1)S(1)} %fold_spectra.4.part_ref), channel_id=1, source_target_pairs={{0,1},{1,0},{3,2},{2,3},{4,5},{5,4},{7,6},{6,7},{8,9},{9,8},{11,10... | collective-permute-start | bytes 2396168 | tf_op jit(solution)/shard_map/ppermute | solution.py:855
  85.6 43.8 %collective-permute-start.7 = (bf16[1024,768]{1,0:T(8,128)(2,1)}, bf16[1024,768]{1,0:T(8,128)(2,1)}, u32[]{:S(2)}, u32[]{:S(2)}) collective-permute-start(bf16[1024,768]{1,0:T(8,128)(2,1)} %get-tuple-element.265), channel_id=1, source_target_pairs={{16,3},{17,2},{2,17},{3,16},{20,7},{21,6},{6,21},{7,20},{24,11},{2... | collective-permute-start | bytes 4718600 | tf_op jit(solution)/shard_map/ppermute | solution.py:875
  121.4 20.1 %collective-permute-start.6 = (bf16[1040,384]{1,0:T(8,128)(2,1)S(1)}, bf16[1040,384]{1,0:T(8,128)(2,1)S(1)}, u32[]{:S(2)}, u32[]{:S(2)}) collective-permute-start(bf16[1040,384]{1,0:T(8,128)(2,1)S(1)} %fold_spectra.5.part_ref), channel_id=1, source_target_pairs={{0,1},{1,0},{3,2},{2,3},{4,5},{5,4},{7,6},{6,7},{8,9},{9,8},{11,10... | collective-permute-start | bytes 2396168 | tf_op jit(solution)/shard_map/ppermute | solution.py:855
  208.1 24.3 %collective-permute-start.11 = (bf16[1040,384]{1,0:T(8,128)(2,1)S(1)}, bf16[1040,384]{1,0:T(8,128)(2,1)}, u32[]{:S(2)}, u32[]{:S(2)}) collective-permute-start(bf16[1040,384]{1,0:T(8,128)(2,1)S(1)} %fold_spectra.6.part_ref), channel_id=1, source_target_pairs={{0,1},{1,0},{3,2},{2,3},{4,5},{5,4},{7,6},{6,7},{8,9},{9,8},{11,10... | collective-permute-start | bytes 2396168 | tf_op jit(solution)/shard_map/ppermute | solution.py:855
  246.2 44.4 %collective-permute-start.14 = (bf16[2,2,384,768]{3,2,1,0:T(8,128)(2,1)}, bf16[2,2,384,768]{3,2,1,0:T(8,128)(2,1)}, u32[]{:S(2)}, u32[]{:S(2)}) collective-permute-start(bf16[2,2,384,768]{3,2,1,0:T(8,128)(2,1)} %get-tuple-element.329), channel_id=1, source_target_pairs={{0,16},{16,0},{1,17},{17,1},{2,18},{18,2},{3,19},{19,3},{4,20},{20... | collective-permute-start | bytes 7077896 | tf_op jit(solution)/shard_map/ppermute | solution.py:28
  246.3 44.3 %collective-permute-start.9 = (bf16[1024,768]{1,0:T(8,128)(2,1)S(1)}, bf16[1024,768]{1,0:T(8,128)(2,1)}, u32[]{:S(2)}, u32[]{:S(2)}) collective-permute-start(bf16[1024,768]{1,0:T(8,128)(2,1)S(1)} %copy-done.29), channel_id=1, source_target_pairs={{16,3},{17,2},{2,17},{3,16},{20,7},{21,6},{6,21},{7,20},{24,11},{2... | collective-permute-start | bytes 4718600 | tf_op jit(solution)/shard_map/ppermute | solution.py:821
  248.2 42.4 %collective-permute-start.15 = (bf16[2,384,768]{2,1,0:T(8,128)(2,1)}, bf16[2,384,768]{2,1,0:T(8,128)(2,1)}, u32[]{:S(2)}, u32[]{:S(2)}) collective-permute-start(bf16[2,384,768]{2,1,0:T(8,128)(2,1)} %get-tuple-element.330), channel_id=1, source_target_pairs={{0,4},{4,0},{8,12},{12,8},{1,5},{5,1},{9,13},{13,9},{2,6},{6,2},{1... | collective-permute-start | bytes 3538952 | tf_op jit(solution)/shard_map/ppermute | solution.py:693
  249.6 41.0 %collective-permute-start.16 = (bf16[2,384,768]{2,1,0:T(8,128)(2,1)}, bf16[2,384,768]{2,1,0:T(8,128)(2,1)}, u32[]{:S(2)}, u32[]{:S(2)}) collective-permute-start(bf16[2,384,768]{2,1,0:T(8,128)(2,1)} %get-tuple-element.331), channel_id=1, source_target_pairs={{0,8},{4,12},{8,0},{12,4},{1,9},{5,13},{9,1},{13,5},{2,10},{6,14},... | collective-permute-start | bytes 3538952 | tf_op jit(solution)/shard_map/ppermute | solution.py:693
  296.8 15.9 %collective-permute-start.19 = (bf16[384,768]{1,0:T(8,128)(2,1)}, bf16[384,768]{1,0:T(8,128)(2,1)S(1)}, u32[]{:S(2)}, u32[]{:S(2)}) collective-permute-start(bf16[384,768]{1,0:T(8,128)(2,1)} %get-tuple-element.345), channel_id=1, source_target_pairs={{0,8},{4,12},{8,0},{12,4},{1,9},{5,13},{9,1},{13,5},{2,10},{6,14},... | collective-permute-start | bytes 1769480 | tf_op jit(solution)/shard_map/ppermute | solution.py:693
  297.3 15.6 %collective-permute-start.20 = (bf16[384,768]{1,0:T(8,128)(2,1)S(1)}, bf16[384,768]{1,0:T(8,128)(2,1)}, u32[]{:S(2)}, u32[]{:S(2)}) collective-permute-start(bf16[384,768]{1,0:T(8,128)(2,1)S(1)} %get-tuple-element.347), channel_id=1, source_target_pairs={{0,4},{4,0},{8,12},{12,8},{1,5},{5,1},{9,13},{13,9},{2,6},{6,2},{1... | collective-permute-start | bytes 1769480 | tf_op jit(solution)/shard_map/ppermute | solution.py:693
  297.9 16.5 %collective-permute-start.18 = (f32[2,6912]{1,0:T(2,128)S(1)}, f32[2,6912]{1,0:T(2,128)S(1)}, u32[]{:S(2)}, u32[]{:S(2)}) collective-permute-start(f32[2,6912]{1,0:T(2,128)S(1)} %pad_maximum_fusion.10), channel_id=1, source_target_pairs={{0,16},{16,0},{1,17},{17,1},{2,18},{18,2},{3,19},{19,3},{4,20},{20... | collective-permute-start | bytes 165896 | tf_op jit(solution)/shard_map/ppermute | solution.py:932
  314.4 31.4 %collective-permute-start.22 = (bf16[2,2,384,768]{3,2,1,0:T(8,128)(2,1)}, bf16[2,2,384,768]{3,2,1,0:T(8,128)(2,1)S(1)}, u32[]{:S(2)}, u32[]{:S(2)}) collective-permute-start(bf16[2,2,384,768]{3,2,1,0:T(8,128)(2,1)} %get-tuple-element.365), channel_id=1, source_target_pairs={{0,16},{16,0},{1,17},{17,1},{2,18},{18,2},{3,19},{19,3},{4,20},{20... | collective-permute-start | bytes 7077896 | tf_op jit(solution)/shard_map/ppermute | solution.py:28
  314.5 12.9 %collective-permute-start.26 = (bf16[2,96,768]{2,1,0:T(8,128)(2,1)S(1)}, bf16[2,96,768]{2,1,0:T(8,128)(2,1)S(1)}, u32[]{:S(2)}, u32[]{:S(2)}) collective-permute-start(bf16[2,96,768]{2,1,0:T(8,128)(2,1)S(1)} %get-tuple-element.370), channel_id=1, source_target_pairs={{0,1},{1,2},{2,3},{3,0},{4,5},{5,6},{6,7},{7,4},{8,9},{9,10},{10,1... | collective-permute-start | bytes 884744 | tf_op jit(solution)/shard_map/ppermute | solution.py:723
  315.5 30.3 %collective-permute-start.23 = (bf16[2,384,768]{2,1,0:T(8,128)(2,1)S(1)}, bf16[2,384,768]{2,1,0:T(8,128)(2,1)S(1)}, u32[]{:S(2)}, u32[]{:S(2)}) collective-permute-start(bf16[2,384,768]{2,1,0:T(8,128)(2,1)S(1)} %copy-done.32), channel_id=1, source_target_pairs={{0,4},{4,0},{8,12},{12,8},{1,5},{5,1},{9,13},{13,9},{2,6},{6,2},{1... | collective-permute-start | bytes 3538952 | tf_op jit(solution)/shard_map/ppermute | solution.py:693
  316.0 29.8 %collective-permute-start.24 = (bf16[2,384,768]{2,1,0:T(8,128)(2,1)S(1)}, bf16[2,384,768]{2,1,0:T(8,128)(2,1)S(1)}, u32[]{:S(2)}, u32[]{:S(2)}) collective-permute-start(bf16[2,384,768]{2,1,0:T(8,128)(2,1)S(1)} %copy-done.31), channel_id=1, source_target_pairs={{0,8},{4,12},{8,0},{12,4},{1,9},{5,13},{9,1},{13,5},{2,10},{6,14},... | collective-permute-start | bytes 3538952 | tf_op jit(solution)/shard_map/ppermute | solution.py:693
  317.5 21.1 %collective-permute-start.27 = (bf16[2,96,768]{2,1,0:T(8,128)(2,1)S(1)}, bf16[2,96,768]{2,1,0:T(8,128)(2,1)S(1)}, u32[]{:S(2)}, u32[]{:S(2)}) collective-permute-start(bf16[2,96,768]{2,1,0:T(8,128)(2,1)S(1)} %get-tuple-element.371), channel_id=1, source_target_pairs={{0,2},{1,3},{2,0},{3,1},{4,6},{5,7},{6,4},{7,5},{8,10},{9,11},{10,... | collective-permute-start | bytes 884744 | tf_op jit(solution)/shard_map/ppermute | solution.py:723
  327.4 15.6 %collective-permute-start.28 = (bf16[2,96,768]{2,1,0:T(8,128)(2,1)S(1)}, bf16[2,96,768]{2,1,0:T(8,128)(2,1)S(1)}, u32[]{:S(2)}, u32[]{:S(2)}) collective-permute-start(bf16[2,96,768]{2,1,0:T(8,128)(2,1)S(1)} %get-tuple-element.372), channel_id=1, source_target_pairs={{0,3},{1,0},{2,1},{3,2},{4,7},{5,4},{6,5},{7,6},{8,11},{9,8},{10,9... | collective-permute-start | bytes 884744 | tf_op jit(solution)/shard_map/ppermute | solution.py:723
  348.8 14.4 %collective-permute-start.33 = (bf16[384,768]{1,0:T(8,128)(2,1)}, bf16[384,768]{1,0:T(8,128)(2,1)}, u32[]{:S(2)}, u32[]{:S(2)}) collective-permute-start(bf16[384,768]{1,0:T(8,128)(2,1)} %get-tuple-element.386), channel_id=1, source_target_pairs={{0,8},{4,12},{8,0},{12,4},{1,9},{5,13},{9,1},{13,5},{2,10},{6,14},... | collective-permute-start | bytes 1769480 | tf_op jit(solution)/shard_map/ppermute | solution.py:693
  350.3 14.1 %collective-permute-start.34 = (bf16[384,768]{1,0:T(8,128)(2,1)}, bf16[384,768]{1,0:T(8,128)(2,1)}, u32[]{:S(2)}, u32[]{:S(2)}) collective-permute-start(bf16[384,768]{1,0:T(8,128)(2,1)} %get-tuple-element.388), channel_id=1, source_target_pairs={{0,4},{4,0},{8,12},{12,8},{1,5},{5,1},{9,13},{13,9},{2,6},{6,2},{1... | collective-permute-start | bytes 1769480 | tf_op jit(solution)/shard_map/ppermute | solution.py:693
  350.8 17.2 %collective-permute-start.30 = (bf16[2,96,768]{2,1,0:T(8,128)(2,1)}, bf16[2,96,768]{2,1,0:T(8,128)(2,1)}, u32[]{:S(2)}, u32[]{:S(2)}) collective-permute-start(bf16[2,96,768]{2,1,0:T(8,128)(2,1)} %add_convert_fusion.10), channel_id=1, source_target_pairs={{0,1},{1,2},{2,3},{3,0},{4,5},{5,6},{6,7},{7,4},{8,9},{9,10},{10,1... | collective-permute-start | bytes 884744 | tf_op jit(solution)/shard_map/ppermute | solution.py:723
  352.8 21.0 %collective-permute-start.31 = (bf16[2,96,768]{2,1,0:T(8,128)(2,1)}, bf16[2,96,768]{2,1,0:T(8,128)(2,1)}, u32[]{:S(2)}, u32[]{:S(2)}) collective-permute-start(bf16[2,96,768]{2,1,0:T(8,128)(2,1)} %add_convert_fusion.10), channel_id=1, source_target_pairs={{0,2},{1,3},{2,0},{3,1},{4,6},{5,7},{6,4},{7,5},{8,10},{9,11},{10,... | collective-permute-start | bytes 884744 | tf_op jit(solution)/shard_map/ppermute | solution.py:723
  356.2 17.7 %collective-permute-start.32 = (bf16[2,96,768]{2,1,0:T(8,128)(2,1)}, bf16[2,96,768]{2,1,0:T(8,128)(2,1)}, u32[]{:S(2)}, u32[]{:S(2)}) collective-permute-start(bf16[2,96,768]{2,1,0:T(8,128)(2,1)} %add_convert_fusion.10), channel_id=1, source_target_pairs={{0,3},{1,0},{2,1},{3,2},{4,7},{5,4},{6,5},{7,6},{8,11},{9,8},{10,9... | collective-permute-start | bytes 884744 | tf_op jit(solution)/shard_map/ppermute | solution.py:723
  363.1 24.6 %collective-permute-start.29 = (bf16[1024,384]{1,0:T(8,128)(2,1)}, bf16[1024,384]{1,0:T(8,128)(2,1)}, u32[]{:S(2)}, u32[]{:S(2)}) collective-permute-start(bf16[1024,384]{1,0:T(8,128)(2,1)} %get-tuple-element.382), channel_id=1, source_target_pairs={{0,16},{16,0},{1,17},{17,1},{2,18},{18,2},{3,19},{19,3},{4,20},{20... | collective-permute-start | bytes 2359304 | tf_op jit(solution)/shard_map/ppermute | solution.py:28
  377.2 17.9 %collective-permute-start.38 = (bf16[4,96,768]{2,1,0:T(8,128)(2,1)S(1)}, bf16[4,96,768]{2,1,0:T(8,128)(2,1)S(1)}, u32[]{:S(2)}, u32[]{:S(2)}) collective-permute-start(bf16[4,96,768]{2,1,0:T(8,128)(2,1)S(1)} %pad_maximum_fusion.6), channel_id=1, source_target_pairs={{0,8},{4,12},{8,0},{12,4},{1,9},{5,13},{9,1},{13,5},{2,10},{6,14},... | collective-permute-start | bytes 1769480 | tf_op jit(solution)/shard_map/ppermute | solution.py:693
  377.8 20.5 %collective-permute-start.39 = (bf16[4,96,768]{2,1,0:T(8,128)(2,1)S(1)}, bf16[4,96,768]{2,1,0:T(8,128)(2,1)S(1)}, u32[]{:S(2)}, u32[]{:S(2)}) collective-permute-start(bf16[4,96,768]{2,1,0:T(8,128)(2,1)S(1)} %pad_maximum_fusion.7), channel_id=1, source_target_pairs={{0,4},{4,0},{8,12},{12,8},{1,5},{5,1},{9,13},{13,9},{2,6},{6,2},{1... | collective-permute-start | bytes 1769480 | tf_op jit(solution)/shard_map/ppermute | solution.py:693
  379.3 19.1 %collective-permute-start.35 = (bf16[2,96,768]{2,1,0:T(8,128)(2,1)S(1)}, bf16[2,96,768]{2,1,0:T(8,128)(2,1)S(1)}, u32[]{:S(2)}, u32[]{:S(2)}) collective-permute-start(bf16[2,96,768]{2,1,0:T(8,128)(2,1)S(1)} %get-tuple-element.402), channel_id=1, source_target_pairs={{0,1},{1,2},{2,3},{3,0},{4,5},{5,6},{6,7},{7,4},{8,9},{9,10},{10,1... | collective-permute-start | bytes 884744 | tf_op jit(solution)/shard_map/ppermute | solution.py:723
  386.0 18.9 %collective-permute-start.36 = (bf16[2,96,768]{2,1,0:T(8,128)(2,1)S(1)}, bf16[2,96,768]{2,1,0:T(8,128)(2,1)S(1)}, u32[]{:S(2)}, u32[]{:S(2)}) collective-permute-start(bf16[2,96,768]{2,1,0:T(8,128)(2,1)S(1)} %get-tuple-element.403), channel_id=1, source_target_pairs={{0,2},{1,3},{2,0},{3,1},{4,6},{5,7},{6,4},{7,5},{8,10},{9,11},{10,... | collective-permute-start | bytes 884744 | tf_op jit(solution)/shard_map/ppermute | solution.py:723
  387.8 17.5 %collective-permute-start.37 = (bf16[2,96,768]{2,1,0:T(8,128)(2,1)S(1)}, bf16[2,96,768]{2,1,0:T(8,128)(2,1)S(1)}, u32[]{:S(2)}, u32[]{:S(2)}) collective-permute-start(bf16[2,96,768]{2,1,0:T(8,128)(2,1)S(1)} %get-tuple-element.404), channel_id=1, source_target_pairs={{0,3},{1,0},{2,1},{3,2},{4,7},{5,4},{6,5},{7,6},{8,11},{9,8},{10,9... | collective-permute-start | bytes 884744 | tf_op jit(solution)/shard_map/ppermute | solution.py:723
  395.1 17.9 %collective-permute-start.40 = (f32[2,6912]{1,0:T(2,128)S(1)}, f32[2,6912]{1,0:T(2,128)S(1)}, u32[]{:S(2)}, u32[]{:S(2)}) collective-permute-start(f32[2,6912]{1,0:T(2,128)S(1)} %copy-done.35), channel_id=1, source_target_pairs={{0,2},{1,3},{2,0},{3,1},{4,6},{5,7},{6,4},{7,5},{8,10},{9,11},{10,... | collective-permute-start | bytes 165896 | tf_op jit(solution)/shard_map/ppermute | solution.py:932
  413.0 11.9 %collective-permute-start.41 = (bf16[2,96,768]{2,1,0:T(8,128)(2,1)S(1)}, bf16[2,96,768]{2,1,0:T(8,128)(2,1)S(1)}, u32[]{:S(2)}, u32[]{:S(2)}) collective-permute-start(bf16[2,96,768]{2,1,0:T(8,128)(2,1)S(1)} %add_convert_fusion.9), channel_id=1, source_target_pairs={{0,1},{1,2},{2,3},{3,0},{4,5},{5,6},{6,7},{7,4},{8,9},{9,10},{10,1... | collective-permute-start | bytes 884744 | tf_op jit(solution)/shard_map/ppermute | solution.py:723
  413.9 22.7 %collective-permute-start.42 = (bf16[2,96,768]{2,1,0:T(8,128)(2,1)S(1)}, bf16[2,96,768]{2,1,0:T(8,128)(2,1)S(1)}, u32[]{:S(2)}, u32[]{:S(2)}) collective-permute-start(bf16[2,96,768]{2,1,0:T(8,128)(2,1)S(1)} %add_convert_fusion.9), channel_id=1, source_target_pairs={{0,2},{1,3},{2,0},{3,1},{4,6},{5,7},{6,4},{7,5},{8,10},{9,11},{10,... | collective-permute-start | bytes 884744 | tf_op jit(solution)/shard_map/ppermute | solution.py:723
  417.2 19.3 %collective-permute-start.43 = (bf16[2,96,768]{2,1,0:T(8,128)(2,1)S(1)}, bf16[2,96,768]{2,1,0:T(8,128)(2,1)S(1)}, u32[]{:S(2)}, u32[]{:S(2)}) collective-permute-start(bf16[2,96,768]{2,1,0:T(8,128)(2,1)S(1)} %add_convert_fusion.9), channel_id=1, source_target_pairs={{0,3},{1,0},{2,1},{3,2},{4,7},{5,4},{6,5},{7,6},{8,11},{9,8},{10,9... | collective-permute-start | bytes 884744 | tf_op jit(solution)/shard_map/ppermute | solution.py:723
  417.4 27.0 %collective-permute-start.45 = (bf16[2,4,96,768]{3,2,1,0:T(8,128)(2,1)S(1)}, bf16[2,4,96,768]{3,2,1,0:T(8,128)(2,1)S(1)}, u32[]{:S(2)}, u32[]{:S(2)}) collective-permute-start(bf16[2,4,96,768]{3,2,1,0:T(8,128)(2,1)S(1)} %pad_maximum_fusion.2.refs_4_), channel_id=1, source_target_pairs={{0,4},{4,0},{8,12},{12,8},{1,5},{5,1},{9,13},{13,9},{2,6},{6,2},{1... | collective-permute-start | bytes 3538952 | tf_op jit(solution)/shard_map/ppermute | solution.py:693
  418.0 26.6 %collective-permute-start.46 = (bf16[2,4,96,768]{3,2,1,0:T(8,128)(2,1)S(1)}, bf16[2,4,96,768]{3,2,1,0:T(8,128)(2,1)S(1)}, u32[]{:S(2)}, u32[]{:S(2)}) collective-permute-start(bf16[2,4,96,768]{3,2,1,0:T(8,128)(2,1)S(1)} %pad_maximum_fusion.3.refs_5_), channel_id=1, source_target_pairs={{0,8},{4,12},{8,0},{12,4},{1,9},{5,13},{9,1},{13,5},{2,10},{6,14},... | collective-permute-start | bytes 3538952 | tf_op jit(solution)/shard_map/ppermute | solution.py:693
  436.8 23.1 %collective-permute-start.44 = (bf16[1040,384]{1,0:T(8,128)(2,1)S(1)}, bf16[1040,384]{1,0:T(8,128)(2,1)S(1)}, u32[]{:S(2)}, u32[]{:S(2)}) collective-permute-start(bf16[1040,384]{1,0:T(8,128)(2,1)S(1)} %fold_spectra.7.part_ref), channel_id=1, source_target_pairs={{0,1},{1,0},{3,2},{2,3},{4,5},{5,4},{7,6},{6,7},{8,9},{9,8},{11,10... | collective-permute-start | bytes 2396168 | tf_op jit(solution)/shard_map/ppermute | solution.py:855
  444.6 13.1 %collective-permute-start.47 = (bf16[4,96,768]{2,1,0:T(8,128)(2,1)S(1)}, bf16[4,96,768]{2,1,0:T(8,128)(2,1)S(1)}, u32[]{:S(2)}, u32[]{:S(2)}) collective-permute-start(bf16[4,96,768]{2,1,0:T(8,128)(2,1)S(1)} %pad_maximum_fusion.8), channel_id=1, source_target_pairs={{0,8},{4,12},{8,0},{12,4},{1,9},{5,13},{9,1},{13,5},{2,10},{6,14},... | collective-permute-start | bytes 1769480 | tf_op jit(solution)/shard_map/ppermute | solution.py:693
  446.2 12.9 %collective-permute-start.48 = (bf16[4,96,768]{2,1,0:T(8,128)(2,1)S(1)}, bf16[4,96,768]{2,1,0:T(8,128)(2,1)S(1)}, u32[]{:S(2)}, u32[]{:S(2)}) collective-permute-start(bf16[4,96,768]{2,1,0:T(8,128)(2,1)S(1)} %pad_maximum_fusion.9), channel_id=1, source_target_pairs={{0,4},{4,0},{8,12},{12,8},{1,5},{5,1},{9,13},{13,9},{2,6},{6,2},{1... | collective-permute-start | bytes 1769480 | tf_op jit(solution)/shard_map/ppermute | solution.py:693
  447.6 19.9 %collective-permute-start.53 = (bf16[2,4,96,768]{3,2,1,0:T(8,128)(2,1)S(1)}, bf16[2,4,96,768]{3,2,1,0:T(8,128)(2,1)S(1)}, u32[]{:S(2)}, u32[]{:S(2)}) collective-permute-start(bf16[2,4,96,768]{3,2,1,0:T(8,128)(2,1)S(1)} %pad_maximum_fusion.2.refs_4_), channel_id=1, source_target_pairs={{0,16},{1,17},{2,18},{3,19},{4,20},{5,21},{6,22},{7,23},{8,24},{9,... | collective-permute-start | bytes 3538952 | tf_op jit(solution)/shard_map/ppermute | solution.py:970
  467.5 28.6 %collective-permute-start.56 = (bf16[2,4,96,768]{3,2,1,0:T(8,128)(2,1)S(1)}, bf16[2,4,96,768]{3,2,1,0:T(8,128)(2,1)S(1)}, u32[]{:S(2)}, u32[]{:S(2)}) collective-permute-start(bf16[2,4,96,768]{3,2,1,0:T(8,128)(2,1)S(1)} %pad_maximum_fusion.4.refs_0_), channel_id=1, source_target_pairs={{0,4},{4,0},{8,12},{12,8},{1,5},{5,1},{9,13},{13,9},{2,6},{6,2},{1... | collective-permute-start | bytes 3538952 | tf_op jit(solution)/shard_map/ppermute | solution.py:693
  468.3 28.8 %collective-permute-start.57 = (bf16[2,4,96,768]{3,2,1,0:T(8,128)(2,1)S(1)}, bf16[2,4,96,768]{3,2,1,0:T(8,128)(2,1)S(1)}, u32[]{:S(2)}, u32[]{:S(2)}) collective-permute-start(bf16[2,4,96,768]{3,2,1,0:T(8,128)(2,1)S(1)} %pad_maximum_fusion.5.refs_1_), channel_id=1, source_target_pairs={{0,8},{4,12},{8,0},{12,4},{1,9},{5,13},{9,1},{13,5},{2,10},{6,14},... | collective-permute-start | bytes 3538952 | tf_op jit(solution)/shard_map/ppermute | solution.py:693
  472.0 37.6 %collective-permute-start.50 = (bf16[1024,768]{1,0:T(8,128)(2,1)S(1)}, bf16[1024,768]{1,0:T(8,128)(2,1)S(1)}, u32[]{:S(2)}, u32[]{:S(2)}) collective-permute-start(bf16[1024,768]{1,0:T(8,128)(2,1)S(1)} %finish.1), channel_id=1, source_target_pairs={{16,3},{17,2},{2,17},{3,16},{20,7},{21,6},{6,21},{7,20},{24,11},{2... | collective-permute-start | bytes 4718600 | tf_op jit(solution)/shard_map/ppermute | solution.py:821
  472.8 26.9 %collective-permute-start.60 = (bf16[2,4,96,768]{3,2,1,0:T(8,128)(2,1)S(1)}, bf16[2,4,96,768]{3,2,1,0:T(8,128)(2,1)S(1)}, u32[]{:S(2)}, u32[]{:S(2)}) collective-permute-start(bf16[2,4,96,768]{3,2,1,0:T(8,128)(2,1)S(1)} %collective-permute-done.45.refs_4_), channel_id=1, source_target_pairs={{0,16},{1,17},{2,18},{3,19},{4,20},{5,21},{6,22},{7,23},{8,24},{9,... | collective-permute-start | bytes 3538952 | tf_op jit(solution)/shard_map/ppermute | solution.py:977
  476.7 24.4 %collective-permute-start.61 = (bf16[2,4,96,768]{3,2,1,0:T(8,128)(2,1)S(1)}, bf16[2,4,96,768]{3,2,1,0:T(8,128)(2,1)S(1)}, u32[]{:S(2)}, u32[]{:S(2)}) collective-permute-start(bf16[2,4,96,768]{3,2,1,0:T(8,128)(2,1)S(1)} %collective-permute-done.46.refs_5_), channel_id=1, source_target_pairs={{0,16},{1,17},{2,18},{3,19},{4,20},{5,21},{6,22},{7,23},{8,24},{9,... | collective-permute-start | bytes 3538952 | tf_op jit(solution)/shard_map/ppermute | solution.py:977
  (79 other events, 747.6 us)
Sparse Core Ops, SparseCore 0:
  9.6 24.5 all-gather.2
  35.7 23.0 all-gather.4
